TPU v7x, 512 devices: a whole 4x8x8 slice. The times are simulated.
512 devices in a mesh: row: 16 (over x, z_lo, core), col: 32 (over z_hi, y).
Axes of the slice: x: 4, y: 8, z: 8 (z_hi: 4, z_lo: 2; z = z_hi * 2 + z_lo), core: 2. Of those that a mesh axis runs over, the one named last changes fastest.
Arguments:
- val_orbitals: bfloat16 [48, 64, 4096], P(None, 'col'), may hold values from -6 to 6
- cond_orbitals: bfloat16 [64, 64, 4096], P(None, 'col'), may hold values from -6 to 6
- val_index: int32 [1024], replicated, may hold values from 0 to 47
- cond_index: int32 [1024], replicated, may hold values from 0 to 63
- val_energy: float32 [48], replicated, may hold values from -12 to -2
- cond_energy: float32 [64], replicated, may hold values from 0.5 to 15
- freqs: float32 [2], replicated, may hold values from 0.5 to 20
- gmap: int32 [12288], replicated, may hold values from 1 to 524255, as said below
Outputs:
- chi_zero: float32 [2, 12288, 12288], P(None, 'row', 'col')
Inputs may be any that keep to these rules, and one draw needn't show every extreme that they name: `gmap`: the entries are distinct. Each is ((part * 64 + a) * 64 + q) * 64 + k with part 0 or 1, a and q below 64 and 1 <= k < 32; (a, q, k) lies among the 12288 such wave vectors nearest to zero, length measured with a and q read as a - 64 and q - 64 when they are 32 or more (ties broken by the order of ((a * 64 + q) * 64 + k)); a wave vector present with part 0 is present with part 1 too.
All inputs are finite; a program needn't handle non-finite values.
Results may differ from a plain program's by a relative error of at most 0.0099.
Values may be sent and summed in bfloat16 or wider, within the bound.
No kernel may reach another device: no remote copies, remote signals or barrier semaphores. Data moves between devices by JAX's collectives and lax.ppermute only.
A program may use at most 64 MiB of HBM per device.

v0:
```python
import math

import jax
import jax.numpy as jnp
from jax import lax
from jax.sharding import PartitionSpec as P

GRID = 64
NG = 12288


def dft_tables(length, count):
    rows_iota = jnp.arange(length, dtype=jnp.int32)[:, None]
    cols_iota = jnp.arange(count, dtype=jnp.int32)[None, :]
    phase = (rows_iota * cols_iota % length).astype(jnp.float32) * (2.0 * math.pi / length)
    return (jnp.cos(phase).astype(jnp.bfloat16), jnp.sin(phase).astype(jnp.bfloat16))


def pair_weights(val_index, cond_index, val_energy, cond_energy, freqs):
    val_hit = val_index[:, None] == jnp.arange(val_energy.shape[0], dtype=jnp.int32)[None, :]
    cond_hit = cond_index[:, None] == jnp.arange(cond_energy.shape[0], dtype=jnp.int32)[None, :]
    gap = jnp.sum(jnp.where(cond_hit, cond_energy[None, :], 0.0), 1) - jnp.sum(
        jnp.where(val_hit, val_energy[None, :], 0.0), 1
    )
    return -4.0 * gap[None, :] / (gap[None, :] ** 2 + freqs[:, None] ** 2)


def shards(
    val_orbitals, cond_orbitals, val_index, cond_index, val_energy, cond_energy, freqs, gmap
):
    row_index = lax.axis_index("row")
    col_index = lax.axis_index("col")
    row_count = lax.axis_size("row")
    col_count = lax.axis_size("col")
    half_grid = GRID // 2
    pair_dev = val_index.shape[0] // row_count
    own_val = lax.dynamic_slice_in_dim(val_index, row_index * pair_dev, pair_dev)
    own_cond = lax.dynamic_slice_in_dim(cond_index, row_index * pair_dev, pair_dev)
    density = (
        jnp.take(val_orbitals, own_val, axis=0).astype(jnp.float32)
        * jnp.take(cond_orbitals, own_cond, axis=0).astype(jnp.float32)
    ).astype(jnp.bfloat16)
    slab = density.shape[1]
    density = density.reshape(pair_dev, slab, GRID, GRID)
    cos_full, sin_full = dft_tables(GRID, GRID)
    cos_half, sin_half = dft_tables(GRID, half_grid)
    z_table = jnp.concatenate([cos_half, -sin_half], 1)
    z_partial = jnp.einsum(
        "pxyz,zk->pxyk", density, z_table, preferred_element_type=jnp.float32
    ).astype(jnp.bfloat16)
    with_cos = jnp.einsum("pxyk,yq->pxqk", z_partial, cos_full, preferred_element_type=jnp.float32)
    with_sin = jnp.einsum("pxyk,yq->pxqk", z_partial, sin_full, preferred_element_type=jnp.float32)
    y_partial = jnp.concatenate(
        [
            with_cos[..., :half_grid] + with_sin[..., half_grid:],
            with_cos[..., half_grid:] - with_sin[..., :half_grid],
        ],
        -1,
    ).astype(jnp.bfloat16)
    block = lax.all_to_all(y_partial, "col", split_axis=2, concat_axis=1, tiled=True)
    x_cos = jnp.einsum("pxqk,xa->paqk", block, cos_full, preferred_element_type=jnp.float32)
    x_sin = jnp.einsum("pxqk,xa->paqk", block, sin_full, preferred_element_type=jnp.float32)
    spectrum = jnp.concatenate(
        [
            x_cos[..., :half_grid] + x_sin[..., half_grid:],
            x_cos[..., half_grid:] - x_sin[..., :half_grid],
        ],
        -1,
    )
    ky_slab = spectrum.shape[2]
    spec_flat = spectrum.reshape(spectrum.shape[0], -1)
    scale_grid = float(GRID) ** (-1.5)
    cube = GRID * GRID * GRID
    weights = pair_weights(val_index, cond_index, val_energy, cond_energy, freqs)
    freq_count = freqs.shape[0]
    col_width = NG // col_count
    contract = (((1,), (1,)), ((), ()))
    part_of = gmap // cube
    remain = gmap % cube
    wave_a = remain // (GRID * GRID)
    wave_q = remain // GRID % GRID
    wave_k = remain % GRID
    is_local = wave_q // ky_slab == col_index
    local_q = jnp.where(is_local, wave_q - col_index * ky_slab, 0)
    flat_index = (wave_a * ky_slab + local_q) * GRID + part_of * half_grid + wave_k
    values = jnp.take(spec_flat, flat_index, axis=1)
    packed = lax.psum(
        (jnp.where(is_local[None, :], values, 0.0) * scale_grid).T.astype(jnp.bfloat16), "col"
    )
    row_block = lax.all_to_all(packed, "row", split_axis=0, concat_axis=1, tiled=True)
    scaled = (weights[:, None, :] * row_block.astype(jnp.float32)[None]).astype(jnp.bfloat16)
    weighted = scaled.reshape(freq_count * row_block.shape[0], row_block.shape[1])
    own_block = lax.dynamic_slice_in_dim(packed, col_index * col_width, col_width, 0)
    product = lax.dot_general(
        weighted,
        lax.all_gather(own_block, "row", axis=1, tiled=True),
        contract,
        preferred_element_type=jnp.float32,
    )
    scale = 1.0 / math.sqrt(val_index.shape[0])
    return (product * scale).reshape(freq_count, -1, col_width)


def solution(mesh):
    placed = (P(None, "col", None), P(None, "col", None), P(), P(), P(), P(), P(), P())
    return jax.shard_map(
        shards, mesh=mesh, in_specs=placed, out_specs=P(None, "row", "col"), check_vma=False
    )
```

profile of v0, /device:TPU:1, one launch (start us, length us, event | category | flops | bytes accessed | tf_op | source)
XLA Modules:
  0.0 551.0 jit_solution(15660078154196803901)
XLA Ops:
  7.6 3.8 gather_fusion
  11.4 2.6 gather.17
  14.0 2.7 gather_fusion.1
  16.6 2.3 gather.19
  19.0 3.2 fusion.7
  25.9 4.1 copy.49
  30.0 5.8 %reshape.130 = bf16[32,2,8192]{2,1,0:T(2,128)(2,1)} reshape(bf16[64,64,2,64]{3,2,1,0:T(2,128)(2,1)} %bitcast.53) | data formatting | bytes 2097152
  35.8 16.5 %all-to-all-start = ((bf16[32,2,8192]{2,1,0:T(2,128)(2,1)}), bf16[32,2,8192]{2,1,0:T(2,128)(2,1)S(1)}, u32[]{:S(2)}, u32[]{:S(2)}) async-start(bf16[32,2,8192]{2,1,0:T(2,128)(2,1)} %reshape.130), calls=%async_computation | async-start | bytes 2097152 | tf_op jit(solution)/shard_map/all_to_all | solution.py:60
  52.6 26.2 %all-to-all-done = bf16[32,2,8192]{2,1,0:T(2,128)(2,1)S(1)} async-done(((bf16[32,2,8192]{2,1,0:T(2,128)(2,1)}), bf16[32,2,8192]{2,1,0:T(2,128)(2,1)S(1)}, u32[]{:S(2)}, u32[]{:S(2)}) %all-to-all-start) | async-done | bytes 1048608 | tf_op jit(solution)/shard_map/all_to_all | solution.py:60
  78.9 1.3 reshape.131
  80.8 1.5 copy.51
  82.3 3.7 copy.52
  88.6 2.4 pad_maximum_fusion
  91.0 6.1 %copy.65 = f32[64,64,2,64]{0,3,2,1:T(8,128)} copy(f32[64,64,2,64]{1,3,2,0:T(8,128)} %pad_maximum_fusion) | data formatting | bytes 4194304 | tf_op jit(solution)/shard_map/reshape | solution.py:71
  97.1 43.2 %gather_fusion.2 = f32[12288,64]{1,0:T(8,128)} fusion(f32[64,8192]{0,1:T(8,128)} %bitcast.47, s32[12288]{0:T(1024)S(1)} %broadcast_clamp_fusion), kind=kCustom, calls=%fused_computation.2 | custom fusion | bytes 6340608 | tf_op jit(solution)/shard_map/jit(_take)/gather | solution.py:86
  140.3 10.6 %multiply_convert_fusion = bf16[12288,64]{1,0:T(8,128)(2,1)} fusion(f32[12288,64]{1,0:T(8,128)} %gather_fusion.2, pred[12288]{0:T(1024)(128)(4,1)S(1)} %fusion.11, pred[12288]{0:T(1024)(128)(4,1)S(1)} %get-tuple-element.5), kind=kLoop, calls=%fused_computation.3 | loop fusion | flops 3145728 | bytes 4743168 | tf_op jit(solution)/shard_map/convert_element_type | solution.py:88
  151.0 312.3 %all-reduce.2.cloned.1.call-done = bf16[12288,64]{1,0:T(8,128)(2,1)} async-done(((bf16[12288,64]{1,0:T(8,128)(2,1)}), bf16[12288,64]{1,0:T(8,128)(2,1)}) %all-reduce.2.cloned.1.call-update) | async-done | bytes 1572880 | tf_op jit(solution)/shard_map/psum | solution.py:87
  463.3 4.3 copy.56
  467.6 27.4 %all-to-all-start.1 = ((bf16[16,768,64]{1,2,0:T(8,128)(2,1)}), bf16[16,768,64]{1,2,0:T(8,128)(2,1)S(1)}, u32[]{:S(2)}, u32[]{:S(2)}) async-start(bf16[16,768,64]{1,2,0:T(8,128)(2,1)} %copy.56), calls=%async_computation.1 | async-start | bytes 3145728 | tf_op jit(solution)/shard_map/all_to_all | solution.py:90
  496.4 36.4 %all_gather.3 = bf16[384,1024]{0,1:T(8,128)(2,1)S(1)} all-gather(bf16[384,64]{0,1:T(8,128)(2,1)S(1)} %copy.58), channel_id=1, replica_groups=mesh['row'=16,'col'=32] {'row'}, dimensions={1}, use_global_device_ids=true | all-gather | bytes 835584 | tf_op jit(solution)/shard_map/all_gather | solution.py:96
  532.8 2.0 convert_element_type.90
  534.8 3.6 copy.57
  538.3 2.6 multiply_convert_fusion.1
  540.9 3.2 convolution_multiply_fusion
  (42 shorter events, 9.6 us)
Async XLA Ops:
  6.5 7.4 %copy-start = (bf16[64,2,4096]{2,1,0:T(2,128)(2,1)S(1)}, bf16[64,2,4096]{2,1,0:T(2,128)(2,1)}, u32[]{:S(2)}) copy-start(bf16[64,2,4096]{2,1,0:T(2,128)(2,1)} %param.9) | copy-start | bytes 3145732
  30.0 22.3 %copy-start.2 = (s32[12288]{0:T(1024)S(1)}, s32[12288]{0:T(1024)}, u32[]{:S(2)}) copy-start(s32[12288]{0:T(1024)} %param.15) | copy-start | bytes 147460
  35.8 43.1 %all-to-all-start = ((bf16[32,2,8192]{2,1,0:T(2,128)(2,1)}), bf16[32,2,8192]{2,1,0:T(2,128)(2,1)S(1)}, u32[]{:S(2)}, u32[]{:S(2)}) async-start(bf16[32,2,8192]{2,1,0:T(2,128)(2,1)} %reshape.130), calls=%async_computation | async-start | bytes 2097152 | tf_op jit(solution)/shard_map/all_to_all | solution.py:60
  52.3 411.0 %all-reduce.2.cloned.1.call-start = ((), (), s32[]{:S(2)}) async-start(), calls=%async_computation.2 | async-start | bytes 6291456 | tf_op jit(solution)/shard_map/psum | solution.py:87
  467.6 27.4 %copy-start.7 = (f32[2]{0:T(128)S(1)}, f32[2]{0:T(128)}, u32[]{:S(2)}) copy-start(f32[2]{0:T(128)} %param.14) | copy-start | bytes 28
  467.6 27.4 %copy-start.3 = (s32[1024]{0:T(1024)S(1)}, s32[1024]{0:T(1024)}, u32[]{:S(2)}) copy-start(s32[1024]{0:T(1024)} %param.10) | copy-start | bytes 12292
  467.6 27.5 %copy-start.5 = (f32[48]{0:T(128)S(1)}, f32[48]{0:T(128)}, u32[]{:S(2)}) copy-start(f32[48]{0:T(128)} %param.12) | copy-start | bytes 580
  467.6 27.6 %copy-start.4 = (s32[1024]{0:T(1024)S(1)}, s32[1024]{0:T(1024)}, u32[]{:S(2)}) copy-start(s32[1024]{0:T(1024)} %param.11) | copy-start | bytes 12292
  467.6 27.6 %copy-start.6 = (f32[64]{0:T(128)S(1)}, f32[64]{0:T(128)}, u32[]{:S(2)}) copy-start(f32[64]{0:T(128)} %param.13) | copy-start | bytes 772
  467.6 65.2 %all-to-all-start.1 = ((bf16[16,768,64]{1,2,0:T(8,128)(2,1)}), bf16[16,768,64]{1,2,0:T(8,128)(2,1)S(1)}, u32[]{:S(2)}, u32[]{:S(2)}) async-start(bf16[16,768,64]{1,2,0:T(8,128)(2,1)} %copy.56), calls=%async_computation.1 | async-start | bytes 3145728 | tf_op jit(solution)/shard_map/all_to_all | solution.py:90
  540.9 3.3 copy-start.1
Sparse Core Ops, SparseCore 0:
  151.1 312.1 all-reduce.1
where the time goes:
time: 552 us; the launch traced here: 551 us
  waiting for transfers between devices  339 us (61%)
  local copies, waits for them, and re-layouts  86.5 us (16%)
  starting transfers between devices  43.9 us (8%)
  blocking collectives  36.4 us (7%)
  other arithmetic  21.9 us (4%)
  between operations  13.6 us (2%)
  matrix products  10.1 us (2%)
    psum x1, waiting for transfers between devices, shards(): lax.psum((jnp.where(is_local[None, :], values, 0.0) * scale_grid).T.astyp...  312 us
    gather x1, local copies, waits for them, and re-layouts, shards(): values = jnp.take(spec_flat, flat_index, axis=1)  43.2 us
    all_gather x1, blocking collectives, shards(): lax.all_gather(own_block, 'row', axis=1, tiled=True)  36.4 us
    all_to_all x1, starting transfers between devices, shards(): lax.all_to_all(packed, 'row', split_axis=0, concat_axis=1, tiled=True)  27.4 us
    all_to_all x1, waiting for transfers between devices, shards(): lax.all_to_all(y_partial, 'col', split_axis=2, concat_axis=1, tiled=True)  26.2 us
    all_to_all x1, starting transfers between devices, shards(): lax.all_to_all(y_partial, 'col', split_axis=2, concat_axis=1, tiled=True)  16.5 us
  transfers between devices with their start and end apart: 3, of which 2 were waited for; matrix products, arithmetic and copies ran while one was open for 0% of the time, Pallas kernels for 0%

commit v1 on v0

v1 whole, which is shorter than its diff:
```python
import functools
import math

import jax
import jax.numpy as jnp
import numpy as np
from jax import lax
from jax.experimental import pallas as pl
from jax.experimental.pallas import tpu as pltpu
from jax.sharding import Mesh, PartitionSpec as P

GRID = 64
NG = 12288
REACH = 18
SIDE = 2 * REACH + 1
RADIUS2 = 334
COLS = 512
PAIR_ROWS = 80
TILE = 128
BF16 = jnp.bfloat16
F32 = jnp.float32


def tables():
    idx = np.arange(GRID)
    phase = (idx[:, None] * idx[None, :] % GRID).astype(np.float32) * np.float32(2.0 * math.pi / GRID)
    phase = phase.astype(np.float64)
    return np.cos(phase), np.sin(phase)


def columns():
    found = []
    for k in range(1, REACH + 1):
        for q in range(-REACH, REACH + 1):
            if q * q + k * k <= RADIUS2:
                found.append((q % GRID, k))
    return found


def z_constant():
    cos, sin = tables()
    out = np.zeros((REACH, 4, 2, 4, GRID), np.float64)
    for k in range(1, REACH + 1):
        for y in range(4):
            out[k - 1, y, 0, y] = cos[:, k]
            out[k - 1, y, 1, y] = -sin[:, k]
    return out.reshape(REACH * 8, 4 * GRID)


def y_spans():
    cols = columns()
    spans = []
    for start in range(0, COLS, TILE):
        ks = [k for _, k in cols[start : start + TILE]]
        spans.append((min(ks) - 1, max(ks)))
    return spans


def y_constant():
    cos, sin = tables()
    cols = columns()
    blocks = []
    for tile, (first, last) in enumerate(y_spans()):
        block = np.zeros((last - first, GRID, 2, 2, TILE), np.float64)
        for lane, (q, k) in enumerate(cols[tile * TILE : (tile + 1) * TILE]):
            block[k - 1 - first, :, 0, 0, lane] = cos[:, q]
            block[k - 1 - first, :, 1, 0, lane] = sin[:, q]
            block[k - 1 - first, :, 0, 1, lane] = -sin[:, q]
            block[k - 1 - first, :, 1, 1, lane] = cos[:, q]
        blocks.append(block.reshape(-1, 2 * TILE))
    return np.concatenate(blocks, 0)


def x_constant():
    cos, sin = tables()
    out = np.zeros((2, PAIR_ROWS, GRID // 2, 2, 2, 2), np.float64)
    for pair in range(2):
        for a in range(-REACH, REACH + 1):
            c = cos[:, a % GRID].reshape(-1, 2)
            s = sin[:, a % GRID].reshape(-1, 2)
            out[pair, a + REACH, :, 0, pair] = c
            out[pair, a + REACH, :, 1, pair] = s
            out[pair, SIDE + a + REACH, :, 0, pair] = -s
            out[pair, SIDE + a + REACH, :, 1, pair] = c
    return out.reshape(2 * PAIR_ROWS, 4 * GRID)


def column_keys():
    keys = np.full((COLS, 1), -1, np.int32)
    for lane, (q, k) in enumerate(columns()):
        keys[lane, 0] = q * GRID + k
    return keys


def transform_kernel(vi_ref, ci_ref, val_ref, cond_ref, zt_ref, yt_ref, out_ref, dens_ref, part_ref):
    pairs = dens_ref.shape[0] // 2
    for p in range(pairs):
        dens_ref[2 * p : 2 * p + 2, :] = val_ref[vi_ref[p]] * cond_ref[ci_ref[p]]
    for j in range(GRID // 4):
        zt = lax.dot_general(
            zt_ref[...],
            dens_ref[:, j * 256 : (j + 1) * 256],
            (((1,), (1,)), ((), ())),
            preferred_element_type=F32,
        )
        part_ref[:, j * 8 : (j + 1) * 8, :] = zt.reshape(REACH, 8, 2 * pairs)
    low = lax.broadcasted_iota(jnp.int32, (2 * pairs, TILE), 0) % 8 < 4
    row = 0
    for tile, (first, last) in enumerate(y_spans()):
        depth = (last - first) * 2 * GRID
        left = part_ref[first:last].astype(BF16).reshape(depth, 2 * pairs)
        both = lax.dot_general(
            left, yt_ref[row : row + depth, :], (((0,), (0,)), ((), ())), preferred_element_type=F32
        )
        row += depth
        real, imag = both[:, :TILE], both[:, TILE:]
        even = jnp.where(low, real, pltpu.roll(imag, 4, 0))
        odd = jnp.where(low, pltpu.roll(real, 2 * pairs - 4, 0), imag)
        for m in range(2 * pairs // 8):
            out_ref[16 * m : 16 * m + 16, tile * TILE : (tile + 1) * TILE] = jnp.concatenate(
                [even[8 * m : 8 * m + 8], odd[8 * m : 8 * m + 8]], 0
            ).astype(BF16)


def transform(own_val, own_cond, val_orbitals, cond_orbitals):
    pairs = own_val.shape[0]
    smem = pl.BlockSpec(memory_space=pltpu.SMEM)
    vmem = pl.BlockSpec(memory_space=pltpu.VMEM)
    return pl.pallas_call(
        transform_kernel,
        out_shape=jax.ShapeDtypeStruct((4 * pairs, COLS), BF16),
        in_specs=[smem, smem, vmem, vmem, vmem, vmem],
        out_specs=vmem,
        scratch_shapes=[
            pltpu.VMEM((2 * pairs, GRID * GRID), BF16),
            pltpu.VMEM((REACH, 2 * GRID, 2 * pairs), F32),
        ],
        compiler_params=pltpu.CompilerParams(vmem_limit_bytes=40 * 2**20),
        name="transform",
    )(
        own_val,
        own_cond,
        val_orbitals,
        cond_orbitals,
        jnp.asarray(z_constant(), BF16),
        jnp.asarray(y_constant(), BF16),
    )


def select_kernel(y_ref, xt_ref, key_ref, gmap_ref, g_ref, h_ref, spec_ref):
    @pl.when(pl.program_id(0) == 0)
    def _():
        spec = jnp.dot(xt_ref[...], y_ref[...], preferred_element_type=F32)
        spec_ref[...] = (spec * float(GRID) ** (-1.5)).astype(BF16)

    entry = gmap_ref[0]
    width = entry.shape[1]
    key = entry & (GRID * GRID - 1)
    wave_a = (entry >> 12) & (GRID - 1)
    row = (entry >> 18) * SIDE + ((wave_a + REACH) & (GRID - 1))
    hit = jnp.where(key_ref[...] == key, 1.0, 0.0).astype(BF16)
    found = jnp.dot(spec_ref[...], hit, preferred_element_type=F32)
    rows = lax.broadcasted_iota(jnp.int32, (PAIR_ROWS, width), 0) == row
    picked = [
        jnp.sum(jnp.where(rows, found[i * PAIR_ROWS : (i + 1) * PAIR_ROWS], 0.0), 0, keepdims=True)
        for i in range(2)
    ]
    both = jnp.concatenate(picked, 0).astype(BF16)
    for copy in range(g_ref.shape[0]):
        g_ref[copy] = both
    half = width // 2
    h_ref[0] = both[:, :half]
    h_ref[1] = both[:, half:]


def select(block, gmap, copies, rows):
    width = NG // rows
    return pl.pallas_call(
        select_kernel,
        grid=(rows,),
        out_shape=(
            jax.ShapeDtypeStruct((rows * copies, 2, width), BF16),
            jax.ShapeDtypeStruct((rows * 2, 2, width // 2), BF16),
        ),
        in_specs=[
            pl.BlockSpec((4 * GRID, COLS), lambda i: (0, 0)),
            pl.BlockSpec((2 * PAIR_ROWS, 4 * GRID), lambda i: (0, 0)),
            pl.BlockSpec((COLS, 1), lambda i: (0, 0)),
            pl.BlockSpec((1, 1, width), lambda i: (i, 0, 0)),
        ],
        out_specs=(
            pl.BlockSpec((copies, 2, width), lambda i: (i, 0, 0)),
            pl.BlockSpec((2, 2, width // 2), lambda i: (i, 0, 0)),
        ),
        scratch_shapes=[pltpu.VMEM((2 * PAIR_ROWS, COLS), BF16)],
        compiler_params=pltpu.CompilerParams(
            dimension_semantics=("arbitrary",), vmem_limit_bytes=40 * 2**20
        ),
        name="select",
    )(block, jnp.asarray(x_constant(), BF16), jnp.asarray(column_keys()), gmap.reshape(rows, 1, width))


def pair_weights(val_index, cond_index, val_energy, cond_energy, freqs):
    val_hit = val_index[:, None] == jnp.arange(val_energy.shape[0], dtype=jnp.int32)[None, :]
    cond_hit = cond_index[:, None] == jnp.arange(cond_energy.shape[0], dtype=jnp.int32)[None, :]
    gap = jnp.sum(jnp.where(cond_hit, cond_energy[None, :], 0.0), 1) - jnp.sum(
        jnp.where(val_hit, val_energy[None, :], 0.0), 1
    )
    return -4.0 * gap[None, :] / (gap[None, :] ** 2 + freqs[:, None] ** 2)


ROW = ("x", "z_lo", "core")
COL = ("z_hi", "y")


def reorder(pair_values):
    return pair_values.reshape(16, 4, 8, 2).transpose(2, 0, 1, 3).reshape(-1)


def shards(
    val_orbitals, cond_orbitals, val_index, cond_index, val_energy, cond_energy, freqs, gmap
):
    row_count = lax.axis_size(ROW)
    col_count = lax.axis_size(COL)
    pair_dev = val_index.shape[0] // row_count
    row_index = lax.axis_index(ROW)
    own_val = lax.dynamic_slice_in_dim(val_index, row_index * pair_dev, pair_dev)
    own_cond = lax.dynamic_slice_in_dim(cond_index, row_index * pair_dev, pair_dev)
    partial = transform(own_val, own_cond, val_orbitals, cond_orbitals)
    block = lax.all_to_all(
        partial.reshape(col_count, 8, COLS), COL, split_axis=0, concat_axis=0, tiled=True
    ).reshape(4 * GRID, COLS)
    for_rows, for_cols = select(block, gmap, 4, row_count)
    mine = lax.all_to_all(for_rows, ROW + ("z_hi",), split_axis=0, concat_axis=0, tiled=True)
    mine, for_cols = lax.optimization_barrier((mine, for_cols))
    left = lax.all_gather(mine.reshape(-1, NG // row_count), "y", axis=0, tiled=True)
    width = NG // col_count
    column = lax.all_to_all(for_cols, COL, split_axis=0, concat_axis=0, tiled=True)
    column = column.reshape(4, 8, 2, width).transpose(1, 0, 2, 3).reshape(1, pair_dev, width)
    spread = lax.all_to_all(
        jnp.broadcast_to(column, (row_count, pair_dev, width)), ROW, split_axis=0, concat_axis=0, tiled=True
    )
    right = spread.reshape(row_count, 8, 8, width).transpose(1, 0, 2, 3).reshape(-1, width)
    weights = pair_weights(reorder(val_index), reorder(cond_index), val_energy, cond_energy, freqs)
    weighted = (weights[:, :, None] * left.astype(F32)[None]).astype(BF16)
    product = lax.dot_general(
        weighted, right, (((1,), (0,)), ((), ())), preferred_element_type=F32
    )
    return product * (1.0 / math.sqrt(val_index.shape[0]))


def solution(mesh):
    fine = Mesh(mesh.devices.reshape(4, 2, 2, 4, 8), ROW + COL)
    orbitals = P(None, COL, None)
    placed = (orbitals, orbitals, P(), P(), P(), P(), P(), P())
    return jax.shard_map(
        shards, mesh=fine, in_specs=placed, out_specs=P(None, ROW, COL), check_vma=False
    )
```

time: 552 us -> 122 us (0.22)
  waiting for transfers between devices: 339 us -> 11.6 us
  local copies, waits for them, and re-layouts: 86.5 us -> 11.6 us
  starting transfers between devices: 43.9 us -> 5.47 us
  blocking collectives: 36.4 us -> 65.2 us
  other arithmetic: 21.9 us -> 0.3 us
  Pallas kernels: 0 us -> 8.84 us
  matrix products: 10.1 us -> 4.34 us
    psum x1 -> x0, waiting for transfers between devices: 312 us -> none  [shards(): lax.psum((jnp.where(is_local[None, :], values, 0.0) * scale_grid).T.astyp...]
    all_to_all x0 -> x3, blocking collectives: none -> 65.2 us  [the longest x1 29.1 us: shards(): lax.all_to_all(partial.reshape(col_count, 8, COLS), COL, split_axis=0, co...]
    gather x5 -> x0, local copies, waits for them, and re-layouts: 54.5 us -> none  [the longest x1 43.2 us: shards(): values = jnp.take(spec_flat, flat_index, axis=1)]
    all_to_all x2 -> x1, starting transfers between devices: 43.9 us -> 5.47 us  [shards(): lax.all_to_all(jnp.broadcast_to(column, (row_count, pair_dev, width)), RO...]
    all_gather x1 -> x0, blocking collectives: 36.4 us -> none  [shards(): lax.all_gather(own_block, 'row', axis=1, tiled=True)]
    convert_element_type x4 -> x0, other arithmetic: 15.3 us -> none  [the longest x1 10.6 us: shards(): (jnp.where(is_local[None, :], values, 0.0) * scale_grid).T.astype(jnp.bfl...]
    all_to_all x2 -> x1, waiting for transfers between devices: 26.2 us -> 11.6 us  [shards(): lax.all_to_all(jnp.broadcast_to(column, (row_count, pair_dev, width)), RO...]
    all_to_all x4 -> x0, local copies, waits for them, and re-layouts: 10.1 us -> none  [the longest x3 5.77 us: shards(): lax.all_to_all(y_partial, 'col', split_axis=2, concat_axis=1, tiled=True)]
  transfers between devices with their start and end apart: 3 -> 2, of which waited for: 2 -> 1; matrix products, arithmetic and copies ran while one was open for 0% -> 3% of each run, Pallas kernels for 0% -> 0%
where the time goes in v1:
time: 122 us; the launch traced here: 121 us
  blocking collectives  65.2 us (53%)
  between operations  13.6 us (11%)
  local copies, waits for them, and re-layouts  11.6 us (10%)
  waiting for transfers between devices  11.6 us (10%)
  Pallas kernels  8.84 us (7%)
  starting transfers between devices  5.47 us (4%)
  matrix products  4.34 us (4%)
    all_to_all x1, blocking collectives, shards(): lax.all_to_all(partial.reshape(col_count, 8, COLS), COL, split_axis=0, co...  29.1 us
    all_to_all x1, blocking collectives, shards(): lax.all_to_all(for_rows, ROW + ('z_hi',), split_axis=0, concat_axis=0, ti...  21.4 us
    all_to_all x1, blocking collectives, shards(): lax.all_to_all(for_cols, COL, split_axis=0, concat_axis=0, tiled=True)  14.8 us
    all_to_all x1, waiting for transfers between devices, shards(): lax.all_to_all(jnp.broadcast_to(column, (row_count, pair_dev, width)), RO...  11.6 us
    pallas_call x1, Pallas kernels, select(): pl.pallas_call(select_kernel, grid=(rows,), out_shape=(jax.ShapeDtypeStru...  6.99 us
    all_to_all x1, starting transfers between devices, shards(): lax.all_to_all(jnp.broadcast_to(column, (row_count, pair_dev, width)), RO...  5.47 us
    unnamed x24, local copies, waits for them, and re-layouts  4.62 us
    dot_general x1, matrix products, shards(): lax.dot_general(weighted, right, (((1,), (0,)), ((), ())), preferred_elem...  4.34 us
  transfers between devices with their start and end apart: 2, of which 1 were waited for; matrix products, arithmetic and copies ran while one was open for 3% of the time, Pallas kernels for 0%

profile of v1, /device:TPU:1, one launch (start us, length us, event | category | flops | bytes accessed | tf_op | source)
XLA Modules:
  0.0 120.9 jit_solution(10993496463658787117)
XLA Ops:
  6.5 0.8 dynamic_slice.6.vi_ref
  7.3 0.8 dynamic_slice.7.ci_ref
  8.1 1.3 %copy-done = bf16[2688,256]{1,0:T(8,128)(2,1)S(1)} copy-done((bf16[2688,256]{1,0:T(8,128)(2,1)S(1)}, bf16[2688,256]{1,0:T(8,128)(2,1)}, u32[]{:S(2)}) %copy-start) | copy-done | bytes 1376280
  9.4 1.2 %copy-done.1 = bf16[64,2,4096]{2,1,0:T(2,128)(2,1)S(1)} copy-done((bf16[64,2,4096]{2,1,0:T(2,128)(2,1)S(1)}, bf16[64,2,4096]{2,1,0:T(2,128)(2,1)}, u32[]{:S(2)}) %copy-start.1) | copy-done | bytes 1048600
  10.6 1.1 copy-done.2
  11.8 0.9 copy-done.5
  12.6 1.9 %transform.1 = bf16[256,512]{1,0:T(8,128)(2,1)S(1)} custom-call(s32[64]{0:T(128)S(1)} %dynamic_slice.6.vi_ref, s32[64]{0:T(128)S(1)} %dynamic_slice.7.ci_ref, bf16[48,2,4096]{2,1,0:T(2,128)(2,1)S(1)} %copy-done.2, bf16[64,2,4096]{2,1,0:T(2,128)(2,1)S(1)} %copy-done.1, bf16[144,256]{1,0:T(8,128)(2,1)S(1)} %copy-done.5, bf16[2688,256]{1,0:T(8,128)(2,1)S(1)} %copy-done), custom_call_target="tpu_custom_call" | custom-call | tf_op jit(solution)/shard_map/transform/pallas_call | solution.py:129
  14.5 29.1 %all_to_all.20 = bf16[32,8,512]{2,1,0:T(8,128)(2,1)S(1)} all-to-all(bf16[32,8,512]{2,1,0:T(8,128)(2,1)S(1)} %bitcast.17), channel_id=1, replica_groups=mesh['x'=4,'z_lo'=2,'core'=2,'z_hi'=4,'y'=8] {'z_hi','y'}, dimensions={0} | all-to-all | bytes 524288 | tf_op jit(solution)/shard_map/all_to_all | solution.py:230
  43.7 7.0 %select.1 = (bf16[64,2,768]{2,1,0:T(2,128)(2,1)S(1)}, bf16[32,2,384]{2,1,0:T(2,128)(2,1)S(1)}) custom-call(bf16[256,512]{1,0:T(8,128)(2,1)S(1)} %bitcast.16, bf16[160,256]{1,0:T(8,128)(2,1)S(1)} %copy-done.4, s32[512,1]{1,0:T(8,128)S(1)} %copy-done.3, s32[16,1,768]{2,1,0:T(1,128)S(1)} %bitcast.18), custom_call_target="tpu_custom_call" | custom-call | tf_op jit(solution)/shard_map/select/pallas_call | solution.py:178
  50.7 21.4 %all_to_all.21 = bf16[64,2,768]{2,1,0:T(2,128)(2,1)S(1)} all-to-all(bf16[64,2,768]{2,1,0:T(2,128)(2,1)S(1)} %get-tuple-element.9), channel_id=1, replica_groups=mesh['x'=4,'z_lo'=2,'core'=2,'z_hi'=4,'y'=8] {'x','z_lo','core','z_hi'}, dimensions={0} | all-to-all | bytes 393216 | tf_op jit(solution)/shard_map/all_to_all | solution.py:234
  72.0 0.7 reshape.94
  72.8 14.8 %all_to_all.22 = bf16[32,2,384]{2,1,0:T(2,128)(2,1)S(1)} all-to-all(bf16[32,2,384]{2,1,0:T(2,128)(2,1)S(1)} %get-tuple-element.12), channel_id=1, replica_groups=mesh['x'=4,'z_lo'=2,'core'=2,'z_hi'=4,'y'=8] {'z_hi','y'}, dimensions={0} | all-to-all | bytes 98304 | tf_op jit(solution)/shard_map/all_to_all | solution.py:238
  87.6 1.0 broadcast_in_dim.45
  88.6 5.5 %all-to-all-start.3 = ((bf16[16,64,384]{2,1,0:T(8,128)(2,1)}), bf16[16,64,384]{2,1,0:T(8,128)(2,1)S(1)}, u32[]{:S(2)}, u32[]{:S(2)}) async-start(bf16[16,64,384]{2,1,0:T(8,128)(2,1)} %broadcast_in_dim.45), calls=%async_computation.3 | async-start | bytes 1572864 | tf_op jit(solution)/shard_map/all_to_all | solution.py:240
  94.1 0.2 reshape.90
  94.3 0.2 reshape.89
  94.6 0.2 eq.34
  94.9 0.2 eq.30
  95.2 0.1 select_reduce_fusion.1
  95.3 0.1 select_reduce_fusion
  95.5 11.6 %all-to-all-done.3 = bf16[16,64,384]{2,1,0:T(8,128)(2,1)S(1)} async-done(((bf16[16,64,384]{2,1,0:T(8,128)(2,1)}), bf16[16,64,384]{2,1,0:T(8,128)(2,1)S(1)}, u32[]{:S(2)}, u32[]{:S(2)}) %all-to-all-start.3) | async-done | bytes 786464 | tf_op jit(solution)/shard_map/all_to_all | solution.py:240
  107.1 1.0 copy.23
  108.0 1.7 %copy.21 = f32[1024,768]{0,1:T(8,128)S(1)} copy(bf16[1024,768]{1,0:T(8,128)(2,1)} %all-gather.2.cloned.1.call-done) | data formatting | bytes 4718592 | tf_op jit(solution)/shard_map/convert_element_type | solution.py:245
  109.8 4.3 %fusion.3 = f32[2,768,384]{2,1,0:T(8,128)} fusion(bf16[1024,384,1]{1,0,2:T(8,128)(2,1)} %bitcast.22, f32[1024,768]{0,1:T(8,128)S(1)} %copy.21, f32[2,1024]{1,0:T(2,128)S(1)} %add_divide_fusion), kind=kOutput, calls=%fused_computation.4 | convolution fusion | flops 1211695104 | bytes 6299648 | tf_op jit(solution)/shard_map/dot_general | solution.py:246
  (30 shorter events, 0.4 us)
Async XLA Ops:
  6.5 101.5 %all-gather.2.cloned.1.call-start = ((), (), s32[]{:S(2)}) async-start(), calls=%async_computation.4 | async-start | bytes 1769472 | tf_op jit(solution)/shard_map/all_gather | solution.py:236
  8.1 1.3 %copy-start = (bf16[2688,256]{1,0:T(8,128)(2,1)S(1)}, bf16[2688,256]{1,0:T(8,128)(2,1)}, u32[]{:S(2)}) copy-start(bf16[2688,256]{1,0:T(8,128)(2,1)} %constant.41.clone.yt_ref) | copy-start | bytes 4128772
  9.4 1.2 %copy-start.1 = (bf16[64,2,4096]{2,1,0:T(2,128)(2,1)S(1)}, bf16[64,2,4096]{2,1,0:T(2,128)(2,1)}, u32[]{:S(2)}) copy-start(bf16[64,2,4096]{2,1,0:T(2,128)(2,1)} %cond_ref.1) | copy-start | bytes 3145732
  10.6 1.1 copy-start.2
  11.8 0.9 copy-start.5
  12.6 31.0 %copy-start.3 = (s32[512,1]{1,0:T(8,128)S(1)}, s32[512,1]{1,0:T(8,128)}, u32[]{:S(2)}) copy-start(s32[512,1]{1,0:T(8,128)} %constant.43.clone.key_ref) | copy-start | bytes 6148
  12.6 31.0 %copy-start.4 = (bf16[160,256]{1,0:T(8,128)(2,1)S(1)}, bf16[160,256]{1,0:T(8,128)(2,1)}, u32[]{:S(2)}) copy-start(bf16[160,256]{1,0:T(8,128)(2,1)} %constant.42.clone.xt_ref) | copy-start | bytes 245764
  12.6 31.0 %copy-start.6 = (s32[12288]{0:T(1024)S(1)}, s32[12288]{0:T(1024)}, u32[]{:S(2)}) copy-start(s32[12288]{0:T(1024)} %param.19) | copy-start | bytes 147460
  14.5 79.6 %copy-start.7 = (s32[1024]{0:T(1024)S(1)}, s32[1024]{0:T(1024)}, u32[]{:S(2)}) copy-start(s32[1024]{0:T(1024)} %param.14) | copy-start | bytes 12292
  14.5 79.8 %copy-start.8 = (s32[1024]{0:T(1024)S(1)}, s32[1024]{0:T(1024)}, u32[]{:S(2)}) copy-start(s32[1024]{0:T(1024)} %param.15) | copy-start | bytes 12292
  14.5 80.0 %copy-start.11 = (f32[2]{0:T(128)S(1)}, f32[2]{0:T(128)}, u32[]{:S(2)}) copy-start(f32[2]{0:T(128)} %param.18) | copy-start | bytes 28
  43.6 51.5 %copy-start.9 = (f32[48]{0:T(128)S(1)}, f32[48]{0:T(128)}, u32[]{:S(2)}) copy-start(f32[48]{0:T(128)} %param.16) | copy-start | bytes 580
  43.6 51.6 %copy-start.10 = (f32[64]{0:T(128)S(1)}, f32[64]{0:T(128)}, u32[]{:S(2)}) copy-start(f32[64]{0:T(128)} %param.17) | copy-start | bytes 772
  88.6 18.5 %all-to-all-start.3 = ((bf16[16,64,384]{2,1,0:T(8,128)(2,1)}), bf16[16,64,384]{2,1,0:T(8,128)(2,1)S(1)}, u32[]{:S(2)}, u32[]{:S(2)}) async-start(bf16[16,64,384]{2,1,0:T(8,128)(2,1)} %broadcast_in_dim.45), calls=%async_computation.3 | async-start | bytes 1572864 | tf_op jit(solution)/shard_map/all_to_all | solution.py:240
Sparse Core Ops, SparseCore 0:
  72.9 30.0 all-gather.1

commit v2 on v1

--- a/solution.py
+++ b/solution.py
@@ -17,8 +17,10 @@
 COLS = 512
 PAIR_ROWS = 80
 TILE = 128
+CUTS = 1
 BF16 = jnp.bfloat16
 F32 = jnp.float32
+VMEM_LIMIT = 60 * 2**20
 
 
 def tables():
@@ -92,10 +94,29 @@
     return keys
 
 
-def transform_kernel(vi_ref, ci_ref, val_ref, cond_ref, zt_ref, yt_ref, out_ref, dens_ref, part_ref):
+def transform_kernel(
+    row_ref, vi_ref, ci_ref, val_hbm, cond_hbm, zt_hbm, yt_hbm, out_ref,
+    val_ref, cond_ref, zt_ref, yt_ref, dens_ref, part_ref, sems,
+):
     pairs = dens_ref.shape[0] // 2
+    moves = []
+    for src, dst, parts in (
+        (val_hbm, val_ref, CUTS),
+        (cond_hbm, cond_ref, CUTS),
+        (zt_hbm, zt_ref, 1),
+        (yt_hbm, yt_ref, CUTS),
+    ):
+        size = src.shape[0] // parts
+        for part in range(parts):
+            cut = pl.ds(part * size, size)
+            moves.append(pltpu.make_async_copy(src.at[cut], dst.at[cut], sems.at[len(moves)]))
+            moves[-1].start()
+    first_pair = row_ref[0] * pairs
+    for move in moves[: 2 * CUTS]:
+        move.wait()
     for p in range(pairs):
-        dens_ref[2 * p : 2 * p + 2, :] = val_ref[vi_ref[p]] * cond_ref[ci_ref[p]]
+        dens_ref[2 * p : 2 * p + 2, :] = val_ref[vi_ref[first_pair + p]] * cond_ref[ci_ref[first_pair + p]]
+    moves[2 * CUTS].wait()
     for j in range(GRID // 4):
         zt = lax.dot_general(
             zt_ref[...],
@@ -105,6 +126,8 @@
         )
         part_ref[:, j * 8 : (j + 1) * 8, :] = zt.reshape(REACH, 8, 2 * pairs)
     low = lax.broadcasted_iota(jnp.int32, (2 * pairs, TILE), 0) % 8 < 4
+    for move in moves[2 * CUTS + 1 :]:
+        move.wait()
     row = 0
     for tile, (first, last) in enumerate(y_spans()):
         depth = (last - first) * 2 * GRID
@@ -122,82 +145,99 @@
             ).astype(BF16)
 
 
-def transform(own_val, own_cond, val_orbitals, cond_orbitals):
-    pairs = own_val.shape[0]
+def transform(row_index, pairs, val_index, cond_index, val_orbitals, cond_orbitals):
     smem = pl.BlockSpec(memory_space=pltpu.SMEM)
-    vmem = pl.BlockSpec(memory_space=pltpu.VMEM)
+    hbm = pl.BlockSpec(memory_space=pltpu.HBM)
+    z_table, y_table = z_constant(), y_constant()
     return pl.pallas_call(
         transform_kernel,
         out_shape=jax.ShapeDtypeStruct((4 * pairs, COLS), BF16),
-        in_specs=[smem, smem, vmem, vmem, vmem, vmem],
-        out_specs=vmem,
+        in_specs=[smem, smem, smem, hbm, hbm, hbm, hbm],
+        out_specs=pl.BlockSpec(memory_space=pltpu.VMEM),
         scratch_shapes=[
+            pltpu.VMEM(val_orbitals.shape, BF16),
+            pltpu.VMEM(cond_orbitals.shape, BF16),
+            pltpu.VMEM(z_table.shape, BF16),
+            pltpu.VMEM(y_table.shape, BF16),
             pltpu.VMEM((2 * pairs, GRID * GRID), BF16),
             pltpu.VMEM((REACH, 2 * GRID, 2 * pairs), F32),
+            pltpu.SemaphoreType.DMA((3 * CUTS + 1,)),
         ],
-        compiler_params=pltpu.CompilerParams(vmem_limit_bytes=40 * 2**20),
+        compiler_params=pltpu.CompilerParams(vmem_limit_bytes=VMEM_LIMIT),
         name="transform",
     )(
-        own_val,
-        own_cond,
+        row_index.reshape(1),
+        val_index,
+        cond_index,
         val_orbitals,
         cond_orbitals,
-        jnp.asarray(z_constant(), BF16),
-        jnp.asarray(y_constant(), BF16),
+        jnp.asarray(z_table, BF16),
+        jnp.asarray(y_table, BF16),
     )
 
 
-def select_kernel(y_ref, xt_ref, key_ref, gmap_ref, g_ref, h_ref, spec_ref):
-    @pl.when(pl.program_id(0) == 0)
-    def _():
-        spec = jnp.dot(xt_ref[...], y_ref[...], preferred_element_type=F32)
-        spec_ref[...] = (spec * float(GRID) ** (-1.5)).astype(BF16)
-
-    entry = gmap_ref[0]
-    width = entry.shape[1]
-    key = entry & (GRID * GRID - 1)
-    wave_a = (entry >> 12) & (GRID - 1)
-    row = (entry >> 18) * SIDE + ((wave_a + REACH) & (GRID - 1))
-    hit = jnp.where(key_ref[...] == key, 1.0, 0.0).astype(BF16)
-    found = jnp.dot(spec_ref[...], hit, preferred_element_type=F32)
-    rows = lax.broadcasted_iota(jnp.int32, (PAIR_ROWS, width), 0) == row
-    picked = [
-        jnp.sum(jnp.where(rows, found[i * PAIR_ROWS : (i + 1) * PAIR_ROWS], 0.0), 0, keepdims=True)
-        for i in range(2)
-    ]
-    both = jnp.concatenate(picked, 0).astype(BF16)
-    for copy in range(g_ref.shape[0]):
-        g_ref[copy] = both
-    half = width // 2
-    h_ref[0] = both[:, :half]
-    h_ref[1] = both[:, half:]
+def select_kernel(y_ref, xt_ref, key_ref, gmap_ref, out_ref):
+    spec = jnp.dot(xt_ref[...], y_ref[...], preferred_element_type=F32)
+    spec = (spec * float(GRID) ** (-1.5)).astype(BF16)
+    rows, _, width = gmap_ref.shape
+    copies = out_ref.shape[0] // rows
+    side = lax.broadcasted_iota(jnp.int32, (PAIR_ROWS, width), 0)
+    for r in range(rows):
+        entry = gmap_ref[r]
+        key = entry & (GRID * GRID - 1)
+        wave_a = (entry >> 12) & (GRID - 1)
+        row = (entry >> 18) * SIDE + ((wave_a + REACH) & (GRID - 1))
+        hit = jnp.where(key_ref[...] == key, 1.0, 0.0).astype(BF16)
+        found = jnp.dot(spec, hit, preferred_element_type=F32)
+        here = side == row
+        picked = [
+            jnp.sum(jnp.where(here, found[i * PAIR_ROWS : (i + 1) * PAIR_ROWS], 0.0), 0, keepdims=True)
+            for i in range(2)
+        ]
+        both = jnp.concatenate(picked, 0).astype(BF16)
+        for copy in range(copies):
+            out_ref[r * copies + copy] = both
 
 
 def select(block, gmap, copies, rows):
     width = NG // rows
+    vmem = pl.BlockSpec(memory_space=pltpu.VMEM)
     return pl.pallas_call(
         select_kernel,
-        grid=(rows,),
-        out_shape=(
-            jax.ShapeDtypeStruct((rows * copies, 2, width), BF16),
-            jax.ShapeDtypeStruct((rows * 2, 2, width // 2), BF16),
-        ),
-        in_specs=[
-            pl.BlockSpec((4 * GRID, COLS), lambda i: (0, 0)),
-            pl.BlockSpec((2 * PAIR_ROWS, 4 * GRID), lambda i: (0, 0)),
-            pl.BlockSpec((COLS, 1), lambda i: (0, 0)),
-            pl.BlockSpec((1, 1, width), lambda i: (i, 0, 0)),
-        ],
-        out_specs=(
-            pl.BlockSpec((copies, 2, width), lambda i: (i, 0, 0)),
-            pl.BlockSpec((2, 2, width // 2), lambda i: (i, 0, 0)),
-        ),
-        scratch_shapes=[pltpu.VMEM((2 * PAIR_ROWS, COLS), BF16)],
-        compiler_params=pltpu.CompilerParams(
-            dimension_semantics=("arbitrary",), vmem_limit_bytes=40 * 2**20
-        ),
+        out_shape=jax.ShapeDtypeStruct((rows * copies, 2, width), BF16),
+        in_specs=[vmem] * 4,
+        out_specs=vmem,
+        compiler_params=pltpu.CompilerParams(vmem_limit_bytes=40 * 2**20),
         name="select",
     )(block, jnp.asarray(x_constant(), BF16), jnp.asarray(column_keys()), gmap.reshape(rows, 1, width))
+
+
+def product_kernel(left_ref, right_ref, weight_ref, out_ref):
+    turned = left_ref[...].T.astype(F32)
+    for f in range(out_ref.shape[0]):
+        weighted = (turned * weight_ref[f : f + 1, :]).astype(BF16)
+        part = jnp.dot(weighted, right_ref[...], preferred_element_type=F32)
+        out_ref[f] = part * (1.0 / math.sqrt(left_ref.shape[0]))
+
+
+def product(left, right, weights, step=384):
+    pairs, rows = left.shape
+    width = right.shape[1]
+    return pl.pallas_call(
+        product_kernel,
+        grid=(rows // step,),
+        out_shape=jax.ShapeDtypeStruct((weights.shape[0], rows, width), F32),
+        in_specs=[
+            pl.BlockSpec((pairs, step), lambda i: (0, i)),
+            pl.BlockSpec((pairs, width), lambda i: (0, 0)),
+            pl.BlockSpec(weights.shape, lambda i: (0, 0)),
+        ],
+        out_specs=pl.BlockSpec((weights.shape[0], step, width), lambda i: (0, i, 0)),
+        compiler_params=pltpu.CompilerParams(
+            dimension_semantics=("arbitrary",), vmem_limit_bytes=VMEM_LIMIT
+        ),
+        name="product",
+    )(left, right, weights)
 
 
 def pair_weights(val_index, cond_index, val_energy, cond_energy, freqs):
@@ -223,30 +263,34 @@
     row_count = lax.axis_size(ROW)
     col_count = lax.axis_size(COL)
     pair_dev = val_index.shape[0] // row_count
-    row_index = lax.axis_index(ROW)
-    own_val = lax.dynamic_slice_in_dim(val_index, row_index * pair_dev, pair_dev)
-    own_cond = lax.dynamic_slice_in_dim(cond_index, row_index * pair_dev, pair_dev)
-    partial = transform(own_val, own_cond, val_orbitals, cond_orbitals)
+    partial = transform(
+        lax.axis_index(ROW), pair_dev, val_index, cond_index, val_orbitals, cond_orbitals
+    )
     block = lax.all_to_all(
         partial.reshape(col_count, 8, COLS), COL, split_axis=0, concat_axis=0, tiled=True
     ).reshape(4 * GRID, COLS)
-    for_rows, for_cols = select(block, gmap, 4, row_count)
+    for_rows = select(block, gmap, 4, row_count)
     mine = lax.all_to_all(for_rows, ROW + ("z_hi",), split_axis=0, concat_axis=0, tiled=True)
-    mine, for_cols = lax.optimization_barrier((mine, for_cols))
-    left = lax.all_gather(mine.reshape(-1, NG // row_count), "y", axis=0, tiled=True)
+    mine = mine.reshape(-1, NG // row_count)
+    left = lax.all_gather(mine, "y", axis=0, tiled=True)
     width = NG // col_count
-    column = lax.all_to_all(for_cols, COL, split_axis=0, concat_axis=0, tiled=True)
-    column = column.reshape(4, 8, 2, width).transpose(1, 0, 2, 3).reshape(1, pair_dev, width)
-    spread = lax.all_to_all(
+    z_hi = lax.axis_index("z_hi")
+    piece = lax.dynamic_slice(mine, (z_hi // 2 * pair_dev, z_hi % 2 * width), (pair_dev, width))
+    column = lax.ppermute(piece, ROW + COL, column_moves())
+    right = lax.all_to_all(
         jnp.broadcast_to(column, (row_count, pair_dev, width)), ROW, split_axis=0, concat_axis=0, tiled=True
-    )
-    right = spread.reshape(row_count, 8, 8, width).transpose(1, 0, 2, 3).reshape(-1, width)
+    ).reshape(-1, width)
     weights = pair_weights(reorder(val_index), reorder(cond_index), val_energy, cond_energy, freqs)
-    weighted = (weights[:, :, None] * left.astype(F32)[None]).astype(BF16)
-    product = lax.dot_general(
-        weighted, right, (((1,), (0,)), ((), ())), preferred_element_type=F32
-    )
-    return product * (1.0 / math.sqrt(val_index.shape[0]))
+    return product(left, right, weights)
+
+
+def column_moves():
+    moves = []
+    for row in range(16):
+        for z_hi in range(4):
+            for y in range(8):
+                moves.append((row * 32 + z_hi * 8 + y, (2 * y + z_hi // 2) * 32 + 2 * row + z_hi % 2))
+    return moves
 
 
 def solution(mesh):

time: 122 us -> 112 us (0.918)
  blocking collectives: 65.2 us -> 50.5 us
  starting transfers between devices: 5.47 us -> 13.2 us
  local copies, waits for them, and re-layouts: 11.6 us -> 4.47 us
  waiting for transfers between devices: 11.6 us -> 16.5 us
  matrix products: 4.34 us -> 0 us
  Pallas kernels: 8.84 us -> 12 us
    all_to_all x1 -> x0, blocking collectives: 14.8 us -> none  [shards(): lax.all_to_all(for_cols, COL, split_axis=0, concat_axis=0, tiled=True)]
    ppermute x0 -> x1, waiting for transfers between devices: none -> 5.47 us  [shards(): column = lax.ppermute(piece, ROW + COL, column_moves())]
    dot_general x1 -> x0, matrix products: 4.34 us -> none  [shards(): lax.dot_general(weighted, right, (((1,), (0,)), ((), ())), preferred_elem...]
    all_to_all x1, starting transfers between devices: 5.47 us -> 9.38 us  [shards(): lax.all_to_all(jnp.broadcast_to(column, (row_count, pair_dev, width)), RO...]
    ppermute x0 -> x1, starting transfers between devices: none -> 3.83 us  [shards(): column = lax.ppermute(piece, ROW + COL, column_moves())]
    unnamed x24 -> x18, local copies, waits for them, and re-layouts: 4.62 us -> 0.9 us
    pallas_call x1, Pallas kernels: 1.85 us -> 4.56 us  [transform(): pl.pallas_call(transform_kernel, out_shape=jax.ShapeDtypeStruct((4 * pair...]
    convert_element_type x1 -> x0, local copies, waits for them, and re-layouts: 1.71 us -> none  [shards(): weighted = (weights[:, :, None] * left.astype(F32)[None]).astype(BF16)]
  transfers between devices with their start and end apart: 2 -> 3, of which waited for: 1 -> 2; matrix products, arithmetic and copies ran while one was open for 3% -> 3% of each run, Pallas kernels for 0% -> 0%
where the time goes in v2:
time: 112 us; the launch traced here: 111 us
  blocking collectives  50.5 us (45%)
  waiting for transfers between devices  16.5 us (15%)
  between operations  13.5 us (12%)
  starting transfers between devices  13.2 us (12%)
  Pallas kernels  12 us (11%)
  local copies, waits for them, and re-layouts  4.47 us (4%)
    all_to_all x1, blocking collectives, shards(): lax.all_to_all(partial.reshape(col_count, 8, COLS), COL, split_axis=0, co...  29.2 us
    all_to_all x1, blocking collectives, shards(): lax.all_to_all(for_rows, ROW + ('z_hi',), split_axis=0, concat_axis=0, ti...  21.4 us
    all_to_all x1, waiting for transfers between devices, shards(): lax.all_to_all(jnp.broadcast_to(column, (row_count, pair_dev, width)), RO...  11 us
    all_to_all x1, starting transfers between devices, shards(): lax.all_to_all(jnp.broadcast_to(column, (row_count, pair_dev, width)), RO...  9.38 us
    ppermute x1, waiting for transfers between devices, shards(): column = lax.ppermute(piece, ROW + COL, column_moves())  5.47 us
    pallas_call x1, Pallas kernels, transform(): pl.pallas_call(transform_kernel, out_shape=jax.ShapeDtypeStruct((4 * pair...  4.56 us
    pallas_call x1, Pallas kernels, product(): pl.pallas_call(product_kernel, grid=(rows // step,), out_shape=jax.ShapeD...  4.45 us
    ppermute x1, starting transfers between devices, shards(): column = lax.ppermute(piece, ROW + COL, column_moves())  3.83 us
  transfers between devices with their start and end apart: 3, of which 2 were waited for; matrix products, arithmetic and copies ran while one was open for 3% of the time, Pallas kernels for 0%

profile of v2, /device:TPU:1, one launch (start us, length us, event | category | flops | bytes accessed | tf_op | source)
XLA Modules:
  0.0 111.1 jit_solution(9684436384401149790)
XLA Ops:
  6.5 4.6 %transform.1 = bf16[256,512]{1,0:T(8,128)(2,1)} custom-call(s32[1]{0:T(128)} %bitcast.row_ref, s32[1024]{0:T(1024)} %vi_ref.1, s32[1024]{0:T(1024)} %ci_ref.1, bf16[48,2,4096]{2,1,0:T(2,128)(2,1)} %val_hbm.1, bf16[64,2,4096]{2,1,0:T(2,128)(2,1)} %cond_hbm.1, bf16[144,256]{1,0:T(8,128)(2,1)} %constant.66.clone.zt_hbm, bf16[2688,256]{1,0:T(8,128)(2,1)} %constant.67.clone.yt_hbm), custom_call_target="tpu_custom_call" | custom-call | tf_op jit(solution)/shard_map/transform/pallas_call | solution.py:152
  11.1 29.2 %all_to_all.15 = bf16[32,8,512]{2,1,0:T(8,128)(2,1)S(1)} all-to-all(bf16[32,8,512]{2,1,0:T(8,128)(2,1)} %bitcast.12), channel_id=1, replica_groups=mesh['x'=4,'z_lo'=2,'core'=2,'z_hi'=4,'y'=8] {'z_hi','y'}, dimensions={0} | all-to-all | bytes 524288 | tf_op jit(solution)/shard_map/all_to_all | solution.py:269
  40.3 3.0 %select.7 = bf16[64,2,768]{2,1,0:T(2,128)(2,1)S(1)} custom-call(bf16[256,512]{1,0:T(8,128)(2,1)S(1)} %bitcast.7, bf16[160,256]{1,0:T(8,128)(2,1)S(1)} %copy-done.1, s32[512,1]{1,0:T(8,128)S(1)} %copy-done, s32[16,1,768]{2,1,0:T(1,128)S(1)} %bitcast.8), custom_call_target="tpu_custom_call" | custom-call | tf_op jit(solution)/shard_map/select/pallas_call | solution.py:205
  43.3 21.4 %all_to_all.16 = bf16[64,2,768]{2,1,0:T(2,128)(2,1)S(1)} all-to-all(bf16[64,2,768]{2,1,0:T(2,128)(2,1)S(1)} %select.7), channel_id=1, replica_groups=mesh['x'=4,'z_lo'=2,'core'=2,'z_hi'=4,'y'=8] {'x','z_lo','core','z_hi'}, dimensions={0} | all-to-all | bytes 393216 | tf_op jit(solution)/shard_map/all_to_all | solution.py:273
  64.6 0.8 reshape.47
  65.4 0.0 all-gather.2.cloned.1.call-update
  65.4 0.0 copy-start.8
  65.5 0.8 dynamic_slice.3
  66.3 3.8 %collective-permute-start = (bf16[64,384]{1,0:T(8,128)(2,1)S(1)}, bf16[64,384]{1,0:T(8,128)(2,1)S(1)}, u32[]{:S(2)}, u32[]{:S(2)}) collective-permute-start(bf16[64,384]{1,0:T(8,128)(2,1)S(1)} %dynamic_slice.3), channel_id=1, source_target_pairs={{0,0},{1,64},{2,128},{3,192},{4,256},{5,320},{6,384},{7,448},{8,1}... | collective-permute-start | bytes 147464 | tf_op jit(solution)/shard_map/ppermute | solution.py:279
  70.1 5.5 %collective-permute-done = bf16[64,384]{1,0:T(8,128)(2,1)S(1)} collective-permute-done((bf16[64,384]{1,0:T(8,128)(2,1)S(1)}, bf16[64,384]{1,0:T(8,128)(2,1)S(1)}, u32[]{:S(2)}, u32[]{:S(2)}) %collective-permute-start) | collective-permute-done | bytes 49184 | tf_op jit(solution)/shard_map/ppermute | solution.py:279
  75.6 1.0 broadcast_in_dim.34
  76.6 9.4 %all-to-all-start.2 = ((bf16[16,64,384]{2,1,0:T(8,128)(2,1)}), bf16[16,64,384]{2,1,0:T(8,128)(2,1)S(1)}, u32[]{:S(2)}, u32[]{:S(2)}) async-start(bf16[16,64,384]{2,1,0:T(8,128)(2,1)} %broadcast_in_dim.34), calls=%async_computation.2 | async-start | bytes 1572864 | tf_op jit(solution)/shard_map/all_to_all | solution.py:280
  86.0 0.2 reshape.50
  86.2 0.2 reshape.49
  86.4 0.1 copy.16
  86.5 0.2 eq.36
  86.7 0.1 copy.15
  86.8 0.2 eq.32
  87.0 0.1 select_reduce_fusion.1
  87.2 0.1 select_reduce_fusion
  87.3 0.7 add_divide_fusion.weight_ref
  88.0 11.0 %all-to-all-done.2 = bf16[16,64,384]{2,1,0:T(8,128)(2,1)S(1)} async-done(((bf16[16,64,384]{2,1,0:T(8,128)(2,1)}), bf16[16,64,384]{2,1,0:T(8,128)(2,1)S(1)}, u32[]{:S(2)}, u32[]{:S(2)}) %all-to-all-start.2) | async-done | bytes 786464 | tf_op jit(solution)/shard_map/all_to_all | solution.py:280
  98.9 0.9 copy-done.3
  99.8 4.4 %product.1 = f32[2,768,384]{2,1,0:T(8,128)} custom-call(bf16[1024,768]{1,0:T(8,128)(2,1)} %all-gather.2.cloned.1.call-done.left_ref, bf16[1024,384]{1,0:T(8,128)(2,1)} %bitcast.9, f32[2,1024]{1,0:T(2,128)} %add_divide_fusion.weight_ref), custom_call_target="tpu_custom_call" | custom-call | tf_op jit(solution)/shard_map/product/pallas_call | solution.py:226
  (20 shorter events, 0.0 us)
Async XLA Ops:
  6.5 92.4 %all-gather.2.cloned.1.call-start = ((), (), s32[]{:S(2)}) async-start(), calls=%async_computation.3 | async-start | bytes 1769472 | tf_op jit(solution)/shard_map/all_gather | solution.py:275
  6.5 33.7 %copy-start = (s32[512,1]{1,0:T(8,128)S(1)}, s32[512,1]{1,0:T(8,128)}, u32[]{:S(2)}) copy-start(s32[512,1]{1,0:T(8,128)} %constant.69.clone.key_ref) | copy-start | bytes 6148
  6.5 33.7 %copy-start.1 = (bf16[160,256]{1,0:T(8,128)(2,1)S(1)}, bf16[160,256]{1,0:T(8,128)(2,1)}, u32[]{:S(2)}) copy-start(bf16[160,256]{1,0:T(8,128)(2,1)} %constant.68.clone.xt_ref) | copy-start | bytes 245764
  6.5 33.7 %copy-start.2 = (s32[12288]{0:T(1024)S(1)}, s32[12288]{0:T(1024)}, u32[]{:S(2)}) copy-start(s32[12288]{0:T(1024)} %param.19) | copy-start | bytes 147460
  64.6 21.3 %copy-start.4 = (s32[1024]{0:T(1024)S(1)}, s32[1024]{0:T(1024)}, u32[]{:S(2)}) copy-start(s32[1024]{0:T(1024)} %vi_ref.1) | copy-start | bytes 12292
  65.4 20.8 %copy-start.5 = (s32[1024]{0:T(1024)S(1)}, s32[1024]{0:T(1024)}, u32[]{:S(2)}) copy-start(s32[1024]{0:T(1024)} %ci_ref.1) | copy-start | bytes 12292
  65.4 21.0 %copy-start.8 = (f32[2]{0:T(128)S(1)}, f32[2]{0:T(128)}, u32[]{:S(2)}) copy-start(f32[2]{0:T(128)} %param.18) | copy-start | bytes 28
  66.3 9.3 %collective-permute-start = (bf16[64,384]{1,0:T(8,128)(2,1)S(1)}, bf16[64,384]{1,0:T(8,128)(2,1)S(1)}, u32[]{:S(2)}, u32[]{:S(2)}) collective-permute-start(bf16[64,384]{1,0:T(8,128)(2,1)S(1)} %dynamic_slice.3), channel_id=1, source_target_pairs={{0,0},{1,64},{2,128},{3,192},{4,256},{5,320},{6,384},{7,448},{8,1}... | collective-permute-start | bytes 147464 | tf_op jit(solution)/shard_map/ppermute | solution.py:279
  76.6 10.5 %copy-start.6 = (f32[48]{0:T(128)S(1)}, f32[48]{0:T(128)}, u32[]{:S(2)}) copy-start(f32[48]{0:T(128)} %param.16) | copy-start | bytes 580
  76.6 10.6 %copy-start.7 = (f32[64]{0:T(128)S(1)}, f32[64]{0:T(128)}, u32[]{:S(2)}) copy-start(f32[64]{0:T(128)} %param.17) | copy-start | bytes 772
  76.6 22.4 %all-to-all-start.2 = ((bf16[16,64,384]{2,1,0:T(8,128)(2,1)}), bf16[16,64,384]{2,1,0:T(8,128)(2,1)S(1)}, u32[]{:S(2)}, u32[]{:S(2)}) async-start(bf16[16,64,384]{2,1,0:T(8,128)(2,1)} %broadcast_in_dim.34), calls=%async_computation.2 | async-start | bytes 1572864 | tf_op jit(solution)/shard_map/all_to_all | solution.py:280
  98.9 0.9 copy-start.3
Sparse Core Ops, SparseCore 0:
  65.5 31.5 all-gather.1

commit v3 on v2

--- a/solution.py
+++ b/solution.py
@@ -234,7 +234,7 @@
         ],
         out_specs=pl.BlockSpec((weights.shape[0], step, width), lambda i: (0, i, 0)),
         compiler_params=pltpu.CompilerParams(
-            dimension_semantics=("arbitrary",), vmem_limit_bytes=VMEM_LIMIT
+            dimension_semantics=("arbitrary",), vmem_limit_bytes=32 * 2**20
         ),
         name="product",
     )(left, right, weights)
@@ -271,15 +271,17 @@
     ).reshape(4 * GRID, COLS)
     for_rows = select(block, gmap, 4, row_count)
     mine = lax.all_to_all(for_rows, ROW + ("z_hi",), split_axis=0, concat_axis=0, tiled=True)
-    mine = mine.reshape(-1, NG // row_count)
-    left = lax.all_gather(mine, "y", axis=0, tiled=True)
+    wide = NG // row_count
     width = NG // col_count
     z_hi = lax.axis_index("z_hi")
-    piece = lax.dynamic_slice(mine, (z_hi // 2 * pair_dev, z_hi % 2 * width), (pair_dev, width))
+    piece = lax.dynamic_slice(
+        mine, (z_hi // 2 * (pair_dev // 2), 0, z_hi % 2 * width), (pair_dev // 2, 2, width)
+    )
     column = lax.ppermute(piece, ROW + COL, column_moves())
-    right = lax.all_to_all(
-        jnp.broadcast_to(column, (row_count, pair_dev, width)), ROW, split_axis=0, concat_axis=0, tiled=True
-    ).reshape(-1, width)
+    copies = jnp.broadcast_to(mine.reshape(1, -1, wide), (lax.axis_size("y"), 2 * mine.shape[0], wide))
+    copies, column = lax.optimization_barrier((copies, column))
+    left = lax.all_to_all(copies, "y", split_axis=0, concat_axis=0, tiled=True).reshape(-1, wide)
+    right = lax.all_gather(column.reshape(pair_dev, width), ROW, axis=0, tiled=True)
     weights = pair_weights(reorder(val_index), reorder(cond_index), val_energy, cond_energy, freqs)
     return product(left, right, weights)
 

time: 112 us -> 121 us (1.080)
  waiting for transfers between devices: 16.5 us -> 34 us
  between operations: 13.5 us -> 0.19 us
  starting transfers between devices: 13.2 us -> 20 us
  local copies, waits for them, and re-layouts: 4.47 us -> 2.44 us
  blocking collectives: 50.5 us -> 51.9 us
    all_gather x0 -> x1, blocking collectives: none -> 22.7 us  [shards(): lax.all_gather(column.reshape(pair_dev, width), ROW, axis=0, tiled=True)]
    all_to_all x1 -> x0, blocking collectives: 21.4 us -> none  [shards(): lax.all_to_all(for_rows, ROW + ('z_hi',), split_axis=0, concat_axis=0, ti...]
    all_to_all x1 -> x2, waiting for transfers between devices: 11 us -> 28.6 us  [the longest x1 16.3 us: shards(): lax.all_to_all(copies, 'y', split_axis=0, concat_axis=0, tiled=True)]
    all_to_all x1 -> x2, starting transfers between devices: 9.38 us -> 16.1 us  [the longest x1 9.18 us: shards(): lax.all_to_all(for_rows, ROW + ('z_hi',), split_axis=0, concat_axis=0, ti...]
  transfers between devices with their start and end apart: 3 -> 3, of which waited for: 2 -> 3; matrix products, arithmetic and copies ran while one was open for 3% -> 1% of each run, Pallas kernels for 0% -> 0%
where the time goes in v3:
time: 121 us; the launch traced here: 120 us
  blocking collectives  51.9 us (43%)
  waiting for transfers between devices  34 us (28%)
  starting transfers between devices  20 us (17%)
  Pallas kernels  11.4 us (9%)
  local copies, waits for them, and re-layouts  2.44 us (2%)
    all_to_all x1, blocking collectives, shards(): lax.all_to_all(partial.reshape(col_count, 8, COLS), COL, split_axis=0, co...  29.1 us
    all_gather x1, blocking collectives, shards(): lax.all_gather(column.reshape(pair_dev, width), ROW, axis=0, tiled=True)  22.7 us
    all_to_all x1, waiting for transfers between devices, shards(): lax.all_to_all(copies, 'y', split_axis=0, concat_axis=0, tiled=True)  16.3 us
    all_to_all x1, waiting for transfers between devices, shards(): lax.all_to_all(for_rows, ROW + ('z_hi',), split_axis=0, concat_axis=0, ti...  12.4 us
    all_to_all x1, starting transfers between devices, shards(): lax.all_to_all(for_rows, ROW + ('z_hi',), split_axis=0, concat_axis=0, ti...  9.18 us
    all_to_all x1, starting transfers between devices, shards(): lax.all_to_all(copies, 'y', split_axis=0, concat_axis=0, tiled=True)  6.94 us
    ppermute x1, waiting for transfers between devices, shards(): column = lax.ppermute(piece, ROW + COL, column_moves())  5.38 us
    pallas_call x1, Pallas kernels, transform(): pl.pallas_call(transform_kernel, out_shape=jax.ShapeDtypeStruct((4 * pair...  4.57 us
  transfers between devices with their start and end apart: 3, of which 3 were waited for; matrix products, arithmetic and copies ran while one was open for 1% of the time, Pallas kernels for 0%

profile of v3, /device:TPU:1, one launch (start us, length us, event | category | flops | bytes accessed | tf_op | source)
XLA Modules:
  0.0 120.2 jit_solution(17175910034507685842)
XLA Ops:
  0.0 4.6 %transform.1 = bf16[256,512]{1,0:T(8,128)(2,1)} custom-call(s32[1]{0:T(128)} %bitcast.row_ref, s32[1024]{0:T(1024)} %vi_ref.1, s32[1024]{0:T(1024)} %ci_ref.1, bf16[48,2,4096]{2,1,0:T(2,128)(2,1)} %val_hbm.1, bf16[64,2,4096]{2,1,0:T(2,128)(2,1)} %cond_hbm.1, bf16[144,256]{1,0:T(8,128)(2,1)} %constant.66.clone.zt_hbm, bf16[2688,256]{1,0:T(8,128)(2,1)} %constant.67.clone.yt_hbm), custom_call_target="tpu_custom_call" | custom-call | tf_op jit(solution)/shard_map/transform/pallas_call | solution.py:152
  4.6 29.1 %all_to_all.15 = bf16[32,8,512]{2,1,0:T(8,128)(2,1)S(1)} all-to-all(bf16[32,8,512]{2,1,0:T(8,128)(2,1)} %bitcast.12), channel_id=1, replica_groups=mesh['x'=4,'z_lo'=2,'core'=2,'z_hi'=4,'y'=8] {'z_hi','y'}, dimensions={0} | all-to-all | bytes 524288 | tf_op jit(solution)/shard_map/all_to_all | solution.py:269
  33.7 3.6 %select.7 = bf16[64,2,768]{2,1,0:T(2,128)(2,1)} custom-call(bf16[256,512]{1,0:T(8,128)(2,1)S(1)} %bitcast.8, bf16[160,256]{1,0:T(8,128)(2,1)S(1)} %copy-done.1, s32[512,1]{1,0:T(8,128)S(1)} %copy-done, s32[16,1,768]{2,1,0:T(1,128)S(1)} %bitcast.9), custom_call_target="tpu_custom_call" | custom-call | tf_op jit(solution)/shard_map/select/pallas_call | solution.py:205
  37.4 9.2 %all-to-all-start.1 = ((bf16[64,2,768]{2,1,0:T(2,128)(2,1)}), bf16[64,2,768]{2,1,0:T(2,128)(2,1)S(1)}, u32[]{:S(2)}, u32[]{:S(2)}) async-start(bf16[64,2,768]{2,1,0:T(2,128)(2,1)} %select.7), calls=%async_computation.1 | async-start | bytes 393216 | tf_op jit(solution)/shard_map/all_to_all | solution.py:273
  46.6 12.4 %all-to-all-done.1 = bf16[64,2,768]{2,1,0:T(2,128)(2,1)S(1)} async-done(((bf16[64,2,768]{2,1,0:T(2,128)(2,1)}), bf16[64,2,768]{2,1,0:T(2,128)(2,1)S(1)}, u32[]{:S(2)}, u32[]{:S(2)}) %all-to-all-start.1) | async-done | bytes 196640 | tf_op jit(solution)/shard_map/all_to_all | solution.py:273
  59.0 3.8 %collective-permute-start = (bf16[32,2,384]{2,1,0:T(2,128)(2,1)S(1)}, bf16[32,2,384]{2,1,0:T(2,128)(2,1)S(1)}, u32[]{:S(2)}, u32[]{:S(2)}) collective-permute-start(bf16[32,2,384]{2,1,0:T(2,128)(2,1)S(1)} %constant_dynamic-slice_fusion), channel_id=1, source_target_pairs={{0,0},{1,64},{2,128},{3,192},{4,256},{5,320},{6,384},{7,448},{8,1}... | collective-permute-start | bytes 147464 | tf_op jit(solution)/shard_map/ppermute | solution.py:280
  62.8 0.1 broadcast_in_dim.38
  62.9 5.4 %collective-permute-done = bf16[32,2,384]{2,1,0:T(2,128)(2,1)S(1)} collective-permute-done((bf16[32,2,384]{2,1,0:T(2,128)(2,1)S(1)}, bf16[32,2,384]{2,1,0:T(2,128)(2,1)S(1)}, u32[]{:S(2)}, u32[]{:S(2)}) %collective-permute-start) | collective-permute-done | bytes 49184 | tf_op jit(solution)/shard_map/ppermute | solution.py:280
  68.3 1.2 %broadcast_in_dim.39 = bf16[8,128,768]{2,1,0:T(8,128)(2,1)} broadcast(bf16[128,768]{1,0:T(8,128)(2,1)S(1)} %broadcast_in_dim.38), dimensions={1,2} | broadcast | bytes 1769472 | tf_op jit(solution)/shard_map/broadcast_in_dim | solution.py:281
  69.5 6.9 %all-to-all-start.2 = ((bf16[8,128,768]{2,1,0:T(8,128)(2,1)}), bf16[8,128,768]{2,1,0:T(8,128)(2,1)S(1)}, u32[]{:S(2)}, u32[]{:S(2)}) async-start(bf16[8,128,768]{2,1,0:T(8,128)(2,1)} %broadcast_in_dim.39), calls=%async_computation.2 | async-start | bytes 3145728 | tf_op jit(solution)/shard_map/all_to_all | solution.py:283
  76.5 0.0 copy-start.5
  76.5 0.0 copy-start.6
  76.5 0.2 reshape.52
  76.7 0.2 reshape.51
  77.0 0.1 copy.16
  77.0 0.2 eq.36
  77.3 0.1 copy.15
  77.4 0.2 eq.32
  77.6 0.1 select_reduce_fusion.1
  77.7 0.1 select_reduce_fusion
  77.8 0.1 add_divide_fusion.weight_ref
  78.0 22.7 %all_gather.3.right_ref = bf16[1024,384]{1,0:T(8,128)(2,1)S(1)} all-gather(bf16[64,384]{1,0:T(8,128)(2,1)S(1)} %reshape.50), channel_id=1, replica_groups=mesh['x'=4,'z_lo'=2,'core'=2,'z_hi'=4,'y'=8] {'x','z_lo','core'}, dimensions={0}, use_global_device_ids=true | all-gather | bytes 835584 | tf_op jit(solution)/shard_map/all_gather | solution.py:284
  100.7 16.3 %all-to-all-done.2 = bf16[8,128,768]{2,1,0:T(8,128)(2,1)S(1)} async-done(((bf16[8,128,768]{2,1,0:T(8,128)(2,1)}), bf16[8,128,768]{2,1,0:T(8,128)(2,1)S(1)}, u32[]{:S(2)}, u32[]{:S(2)}) %all-to-all-start.2) | async-done | bytes 1572896 | tf_op jit(solution)/shard_map/all_to_all | solution.py:283
  116.9 3.2 %product.1 = f32[2,768,384]{2,1,0:T(8,128)} custom-call(bf16[1024,768]{1,0:T(8,128)(2,1)S(1)} %bitcast.7, bf16[1024,384]{1,0:T(8,128)(2,1)S(1)} %all_gather.3.right_ref, f32[2,1024]{1,0:T(2,128)S(1)} %add_divide_fusion.weight_ref), custom_call_target="tpu_custom_call" | custom-call | tf_op jit(solution)/shard_map/product/pallas_call | solution.py:226
  (18 shorter events, 0.1 us)
Async XLA Ops:
  0.0 33.7 %copy-start = (s32[512,1]{1,0:T(8,128)S(1)}, s32[512,1]{1,0:T(8,128)}, u32[]{:S(2)}) copy-start(s32[512,1]{1,0:T(8,128)} %constant.69.clone.key_ref) | copy-start | bytes 6148
  0.0 33.7 %copy-start.1 = (bf16[160,256]{1,0:T(8,128)(2,1)S(1)}, bf16[160,256]{1,0:T(8,128)(2,1)}, u32[]{:S(2)}) copy-start(bf16[160,256]{1,0:T(8,128)(2,1)} %constant.68.clone.xt_ref) | copy-start | bytes 245764
  0.0 33.7 %copy-start.2 = (s32[12288]{0:T(1024)S(1)}, s32[12288]{0:T(1024)}, u32[]{:S(2)}) copy-start(s32[12288]{0:T(1024)} %param.19) | copy-start | bytes 147460
  37.4 21.6 %all-to-all-start.1 = ((bf16[64,2,768]{2,1,0:T(2,128)(2,1)}), bf16[64,2,768]{2,1,0:T(2,128)(2,1)S(1)}, u32[]{:S(2)}, u32[]{:S(2)}) async-start(bf16[64,2,768]{2,1,0:T(2,128)(2,1)} %select.7), calls=%async_computation.1 | async-start | bytes 393216 | tf_op jit(solution)/shard_map/all_to_all | solution.py:273
  59.0 9.3 %collective-permute-start = (bf16[32,2,384]{2,1,0:T(2,128)(2,1)S(1)}, bf16[32,2,384]{2,1,0:T(2,128)(2,1)S(1)}, u32[]{:S(2)}, u32[]{:S(2)}) collective-permute-start(bf16[32,2,384]{2,1,0:T(2,128)(2,1)S(1)} %constant_dynamic-slice_fusion), channel_id=1, source_target_pairs={{0,0},{1,64},{2,128},{3,192},{4,256},{5,320},{6,384},{7,448},{8,1}... | collective-permute-start | bytes 147464 | tf_op jit(solution)/shard_map/ppermute | solution.py:280
  69.5 7.0 %copy-start.3 = (s32[1024]{0:T(1024)S(1)}, s32[1024]{0:T(1024)}, u32[]{:S(2)}) copy-start(s32[1024]{0:T(1024)} %vi_ref.1) | copy-start | bytes 12292
  69.5 7.2 %copy-start.4 = (s32[1024]{0:T(1024)S(1)}, s32[1024]{0:T(1024)}, u32[]{:S(2)}) copy-start(s32[1024]{0:T(1024)} %ci_ref.1) | copy-start | bytes 12292
  69.5 7.4 %copy-start.7 = (f32[2]{0:T(128)S(1)}, f32[2]{0:T(128)}, u32[]{:S(2)}) copy-start(f32[2]{0:T(128)} %param.18) | copy-start | bytes 28
  69.5 47.4 %all-to-all-start.2 = ((bf16[8,128,768]{2,1,0:T(8,128)(2,1)}), bf16[8,128,768]{2,1,0:T(8,128)(2,1)S(1)}, u32[]{:S(2)}, u32[]{:S(2)}) async-start(bf16[8,128,768]{2,1,0:T(8,128)(2,1)} %broadcast_in_dim.39), calls=%async_computation.2 | async-start | bytes 3145728 | tf_op jit(solution)/shard_map/all_to_all | solution.py:283
  76.5 1.1 copy-start.5
  76.5 1.2 %copy-start.6 = (f32[64]{0:T(128)S(1)}, f32[64]{0:T(128)}, u32[]{:S(2)}) copy-start(f32[64]{0:T(128)} %param.17) | copy-start | bytes 772

commit v4 on v3

--- a/solution.py
+++ b/solution.py
@@ -212,32 +212,40 @@
     )(block, jnp.asarray(x_constant(), BF16), jnp.asarray(column_keys()), gmap.reshape(rows, 1, width))
 
 
-def product_kernel(left_ref, right_ref, weight_ref, out_ref):
-    turned = left_ref[...].T.astype(F32)
+def product_kernel(turn_ref, *refs):
+    pieces, (right_ref, weight_ref, out_ref, turned_ref) = refs[:-4], refs[-4:]
+    pairs = right_ref.shape[0]
+    part = pairs // len(pieces)
+    for shift, piece in enumerate(pieces):
+        place = lax.rem(turn_ref[0] + shift, len(pieces))
+        turned_ref[:, pl.ds(pl.multiple_of(place * part, part), part)] = piece[...].T
+    turned = turned_ref[...].astype(F32)
     for f in range(out_ref.shape[0]):
         weighted = (turned * weight_ref[f : f + 1, :]).astype(BF16)
-        part = jnp.dot(weighted, right_ref[...], preferred_element_type=F32)
-        out_ref[f] = part * (1.0 / math.sqrt(left_ref.shape[0]))
-
-
-def product(left, right, weights, step=384):
-    pairs, rows = left.shape
-    width = right.shape[1]
+        total = jnp.dot(weighted, right_ref[...], preferred_element_type=F32)
+        out_ref[f] = total * (1.0 / math.sqrt(pairs))
+
+
+def product(turn, pieces, right, weights, step=384):
+    part, rows = pieces[0].shape
+    pairs, width = right.shape
     return pl.pallas_call(
         product_kernel,
         grid=(rows // step,),
         out_shape=jax.ShapeDtypeStruct((weights.shape[0], rows, width), F32),
-        in_specs=[
-            pl.BlockSpec((pairs, step), lambda i: (0, i)),
+        in_specs=[pl.BlockSpec(memory_space=pltpu.SMEM)]
+        + [pl.BlockSpec((part, step), lambda i: (0, i)) for _ in pieces]
+        + [
             pl.BlockSpec((pairs, width), lambda i: (0, 0)),
             pl.BlockSpec(weights.shape, lambda i: (0, 0)),
         ],
         out_specs=pl.BlockSpec((weights.shape[0], step, width), lambda i: (0, i, 0)),
+        scratch_shapes=[pltpu.VMEM((step, pairs), BF16)],
         compiler_params=pltpu.CompilerParams(
             dimension_semantics=("arbitrary",), vmem_limit_bytes=32 * 2**20
         ),
         name="product",
-    )(left, right, weights)
+    )(turn.reshape(1), *pieces, right, weights)
 
 
 def pair_weights(val_index, cond_index, val_energy, cond_energy, freqs):
@@ -278,12 +286,26 @@
         mine, (z_hi // 2 * (pair_dev // 2), 0, z_hi % 2 * width), (pair_dev // 2, 2, width)
     )
     column = lax.ppermute(piece, ROW + COL, column_moves())
-    copies = jnp.broadcast_to(mine.reshape(1, -1, wide), (lax.axis_size("y"), 2 * mine.shape[0], wide))
-    copies, column = lax.optimization_barrier((copies, column))
-    left = lax.all_to_all(copies, "y", split_axis=0, concat_axis=0, tiled=True).reshape(-1, wide)
-    right = lax.all_gather(column.reshape(pair_dev, width), ROW, axis=0, tiled=True)
+    pieces = gather_y(mine.reshape(-1, wide))
+    right = lax.all_to_all(
+        jnp.broadcast_to(column.reshape(pair_dev, width), (row_count, pair_dev, width)),
+        ROW, split_axis=0, concat_axis=0, tiled=True,
+    ).reshape(-1, width)
     weights = pair_weights(reorder(val_index), reorder(cond_index), val_energy, cond_energy, freqs)
-    return product(left, right, weights)
+    return product(lax.axis_index("y"), pieces, right, weights)
+
+
+def gather_y(block):
+    count = lax.axis_size("y")
+
+    def fetch(value, ahead):
+        return lax.ppermute(value, "y", [((i + ahead) % count, i) for i in range(count)])
+
+    one, last = fetch(block, 1), fetch(block, -1)
+    two, back_two = fetch(block, 2), fetch(block, -2)
+    three, back_three = fetch(two, 1), fetch(back_two, -1)
+    four = fetch(two, 2)
+    return [block, one, two, three, four, back_three, back_two, last]
 
 
 def column_moves():

time: 121 us -> 120 us (level)
  starting transfers between devices: 20 us -> 46 us
  blocking collectives: 51.9 us -> 29.3 us
  waiting for transfers between devices: 34 us -> 29.9 us
    ppermute x0 -> x7, starting transfers between devices: none -> 23.8 us  [fetch(): lax.ppermute(value, 'y', [((i + ahead) % count, i) for i in range(count)])]
    all_gather x1 -> x0, blocking collectives: 22.7 us -> none  [shards(): lax.all_gather(column.reshape(pair_dev, width), ROW, axis=0, tiled=True)]
    all_to_all x1, waiting for transfers between devices: 16.3 us -> 0.01 us  [shards(): lax.all_to_all(jnp.broadcast_to(column.reshape(pair_dev, width), (row_cou...]
    ppermute x0 -> x7, waiting for transfers between devices: none -> 12.1 us  [fetch(): lax.ppermute(value, 'y', [((i + ahead) % count, i) for i in range(count)])]
    all_to_all x1, starting transfers between devices: 6.94 us -> 9.15 us  [shards(): lax.all_to_all(jnp.broadcast_to(column.reshape(pair_dev, width), (row_cou...]
  transfers between devices with their start and end apart: 3 -> 10, of which waited for: 3 -> 5; matrix products, arithmetic and copies ran while one was open for 1% -> 1% of each run, Pallas kernels for 0% -> 0%
where the time goes in v4:
time: 120 us
  starting transfers between devices  46 us (38%)
  waiting for transfers between devices  29.9 us (25%)
  blocking collectives  29.3 us (24%)
  Pallas kernels  11.9 us (10%)
  local copies, waits for them, and re-layouts  2.18 us (2%)
    all_to_all x1, blocking collectives, shards(): lax.all_to_all(partial.reshape(col_count, 8, COLS), COL, split_axis=0, co...  29.3 us
    ppermute x7, starting transfers between devices, fetch(): lax.ppermute(value, 'y', [((i + ahead) % count, i) for i in range(count)])  23.8 us
    all_to_all x1, waiting for transfers between devices, shards(): lax.all_to_all(for_rows, ROW + ('z_hi',), split_axis=0, concat_axis=0, ti...  12.3 us
    ppermute x7, waiting for transfers between devices, fetch(): lax.ppermute(value, 'y', [((i + ahead) % count, i) for i in range(count)])  12.1 us
    all_to_all x1, starting transfers between devices, shards(): lax.all_to_all(for_rows, ROW + ('z_hi',), split_axis=0, concat_axis=0, ti...  9.17 us
    all_to_all x1, starting transfers between devices, shards(): lax.all_to_all(jnp.broadcast_to(column.reshape(pair_dev, width), (row_cou...  9.15 us
    ppermute x1, waiting for transfers between devices, shards(): column = lax.ppermute(piece, ROW + COL, column_moves())  5.47 us
    pallas_call x1, Pallas kernels, transform(): pl.pallas_call(transform_kernel, out_shape=jax.ShapeDtypeStruct((4 * pair...  4.57 us
  transfers between devices with their start and end apart: 10, of which 5 were waited for; matrix products, arithmetic and copies ran while one was open for 1% of the time, Pallas kernels for 0%

profile of v4, /device:TPU:1, one launch (start us, length us, event | category | flops | bytes accessed | tf_op | source)
XLA Modules:
  0.0 119.9 jit_solution(6994982581014168656)
XLA Ops:
  0.0 4.6 %transform.1 = bf16[256,512]{1,0:T(8,128)(2,1)} custom-call(s32[1]{0:T(128)} %bitcast.1.row_ref, s32[1024]{0:T(1024)} %vi_ref.1, s32[1024]{0:T(1024)} %ci_ref.1, bf16[48,2,4096]{2,1,0:T(2,128)(2,1)} %val_hbm.1, bf16[64,2,4096]{2,1,0:T(2,128)(2,1)} %cond_hbm.1, bf16[144,256]{1,0:T(8,128)(2,1)} %constant.68.clone.zt_hbm, bf16[2688,256]{1,0:T(8,128)(2,1)} %constant.69.clone.yt_hbm), custom_call_target="tpu_custom_call" | custom-call | tf_op jit(solution)/shard_map/transform/pallas_call | solution.py:152
  4.6 29.3 %all_to_all.15 = bf16[32,8,512]{2,1,0:T(8,128)(2,1)S(1)} all-to-all(bf16[32,8,512]{2,1,0:T(8,128)(2,1)} %bitcast.13), channel_id=1, replica_groups=mesh['x'=4,'z_lo'=2,'core'=2,'z_hi'=4,'y'=8] {'z_hi','y'}, dimensions={0} | all-to-all | bytes 524288 | tf_op jit(solution)/shard_map/all_to_all | solution.py:277
  33.9 3.6 %select.7 = bf16[64,2,768]{2,1,0:T(2,128)(2,1)} custom-call(bf16[256,512]{1,0:T(8,128)(2,1)S(1)} %bitcast.9, bf16[160,256]{1,0:T(8,128)(2,1)S(1)} %copy-done.1, s32[512,1]{1,0:T(8,128)S(1)} %copy-done, s32[16,1,768]{2,1,0:T(1,128)S(1)} %bitcast.10), custom_call_target="tpu_custom_call" | custom-call | tf_op jit(solution)/shard_map/select/pallas_call | solution.py:205
  37.5 9.2 %all-to-all-start.1 = ((bf16[64,2,768]{2,1,0:T(2,128)(2,1)}), bf16[64,2,768]{2,1,0:T(2,128)(2,1)S(1)}, u32[]{:S(2)}, u32[]{:S(2)}) async-start(bf16[64,2,768]{2,1,0:T(2,128)(2,1)} %select.7), calls=%async_computation.1 | async-start | bytes 393216 | tf_op jit(solution)/shard_map/all_to_all | solution.py:281
  46.8 12.3 %all-to-all-done.1 = bf16[64,2,768]{2,1,0:T(2,128)(2,1)S(1)} async-done(((bf16[64,2,768]{2,1,0:T(2,128)(2,1)}), bf16[64,2,768]{2,1,0:T(2,128)(2,1)S(1)}, u32[]{:S(2)}, u32[]{:S(2)}) %all-to-all-start.1) | async-done | bytes 196640 | tf_op jit(solution)/shard_map/all_to_all | solution.py:281
  59.2 3.8 %collective-permute-start.7 = (bf16[32,2,384]{2,1,0:T(2,128)(2,1)S(1)}, bf16[32,2,384]{2,1,0:T(2,128)(2,1)S(1)}, u32[]{:S(2)}, u32[]{:S(2)}) collective-permute-start(bf16[32,2,384]{2,1,0:T(2,128)(2,1)S(1)} %constant_dynamic-slice_fusion), channel_id=1, source_target_pairs={{0,0},{1,64},{2,128},{3,192},{4,256},{5,320},{6,384},{7,448},{8,1}... | collective-permute-start | bytes 147464 | tf_op jit(solution)/shard_map/ppermute | solution.py:288
  63.0 5.5 %collective-permute-done.7 = bf16[32,2,384]{2,1,0:T(2,128)(2,1)S(1)} collective-permute-done((bf16[32,2,384]{2,1,0:T(2,128)(2,1)S(1)}, bf16[32,2,384]{2,1,0:T(2,128)(2,1)S(1)}, u32[]{:S(2)}, u32[]{:S(2)}) %collective-permute-start.7) | collective-permute-done | bytes 49184 | tf_op jit(solution)/shard_map/ppermute | solution.py:288
  68.5 1.0 broadcast_in_dim.34
  69.5 9.2 %all-to-all-start.2 = ((bf16[16,64,384]{2,1,0:T(8,128)(2,1)}), bf16[16,64,384]{2,1,0:T(8,128)(2,1)S(1)}, u32[]{:S(2)}, u32[]{:S(2)}) async-start(bf16[16,64,384]{2,1,0:T(8,128)(2,1)} %broadcast_in_dim.34), calls=%async_computation.2 | async-start | bytes 1572864 | tf_op jit(solution)/shard_map/all_to_all | solution.py:290
  78.6 0.2 reshape.58
  78.9 0.2 reshape.57
  79.2 0.2 eq.36
  79.5 0.2 eq.32
  80.0 3.2 %collective-permute-start.4 = (bf16[128,768]{1,0:T(8,128)(2,1)S(1)}, bf16[128,768]{1,0:T(8,128)(2,1)S(1)}, u32[]{:S(2)}, u32[]{:S(2)}) collective-permute-start(bf16[128,768]{1,0:T(8,128)(2,1)S(1)} %reshape.54.refs_0_), channel_id=1, source_target_pairs={{6,0},{7,1},{0,2},{1,3},{2,4},{3,5},{4,6},{5,7},{14,8},{15,9},{8,1... | collective-permute-start | bytes 589832 | tf_op jit(solution)/shard_map/ppermute | solution.py:302
  83.2 4.2 %collective-permute-start.1 = (bf16[128,768]{1,0:T(8,128)(2,1)S(1)}, bf16[128,768]{1,0:T(8,128)(2,1)S(1)}, u32[]{:S(2)}, u32[]{:S(2)}) collective-permute-start(bf16[128,768]{1,0:T(8,128)(2,1)S(1)} %reshape.54.refs_0_), channel_id=1, source_target_pairs={{2,0},{3,1},{4,2},{5,3},{6,4},{7,5},{0,6},{1,7},{10,8},{11,9},{12,... | collective-permute-start | bytes 589832 | tf_op jit(solution)/shard_map/ppermute | solution.py:302
  87.5 3.2 %collective-permute-start.6 = (bf16[128,768]{1,0:T(8,128)(2,1)S(1)}, bf16[128,768]{1,0:T(8,128)(2,1)S(1)}, u32[]{:S(2)}, u32[]{:S(2)}) collective-permute-start(bf16[128,768]{1,0:T(8,128)(2,1)S(1)} %reshape.54.refs_0_), channel_id=1, source_target_pairs={{7,0},{0,1},{1,2},{2,3},{3,4},{4,5},{5,6},{6,7},{15,8},{8,9},{9,10... | collective-permute-start | bytes 589832 | tf_op jit(solution)/shard_map/ppermute | solution.py:302
  90.7 3.3 %collective-permute-start = (bf16[128,768]{1,0:T(8,128)(2,1)S(1)}, bf16[128,768]{1,0:T(8,128)(2,1)S(1)}, u32[]{:S(2)}, u32[]{:S(2)}) collective-permute-start(bf16[128,768]{1,0:T(8,128)(2,1)S(1)} %reshape.54.refs_0_), channel_id=1, source_target_pairs={{1,0},{2,1},{3,2},{4,3},{5,4},{6,5},{7,6},{0,7},{9,8},{10,9},{11,1... | collective-permute-start | bytes 589832 | tf_op jit(solution)/shard_map/ppermute | solution.py:302
  94.0 2.9 %collective-permute-done.1.refs_2_ = bf16[128,768]{1,0:T(8,128)(2,1)S(1)} collective-permute-done((bf16[128,768]{1,0:T(8,128)(2,1)S(1)}, bf16[128,768]{1,0:T(8,128)(2,1)S(1)}, u32[]{:S(2)}, u32[]{:S(2)}) %collective-permute-start.1) | collective-permute-done | bytes 196640 | tf_op jit(solution)/shard_map/ppermute | solution.py:302
  96.9 3.6 %collective-permute-start.3 = (bf16[128,768]{1,0:T(8,128)(2,1)S(1)}, bf16[128,768]{1,0:T(8,128)(2,1)S(1)}, u32[]{:S(2)}, u32[]{:S(2)}) collective-permute-start(bf16[128,768]{1,0:T(8,128)(2,1)S(1)} %collective-permute-done.1.refs_2_), channel_id=1, source_target_pairs={{2,0},{3,1},{4,2},{5,3},{6,4},{7,5},{0,6},{1,7},{10,8},{11,9},{12,... | collective-permute-start | bytes 589832 | tf_op jit(solution)/shard_map/ppermute | solution.py:302
  100.5 3.2 %collective-permute-start.2 = (bf16[128,768]{1,0:T(8,128)(2,1)S(1)}, bf16[128,768]{1,0:T(8,128)(2,1)S(1)}, u32[]{:S(2)}, u32[]{:S(2)}) collective-permute-start(bf16[128,768]{1,0:T(8,128)(2,1)S(1)} %collective-permute-done.1.refs_2_), channel_id=1, source_target_pairs={{1,0},{2,1},{3,2},{4,3},{5,4},{6,5},{7,6},{0,7},{9,8},{10,9},{11,1... | collective-permute-start | bytes 589832 | tf_op jit(solution)/shard_map/ppermute | solution.py:302
  103.7 3.1 %collective-permute-start.5 = (bf16[128,768]{1,0:T(8,128)(2,1)S(1)}, bf16[128,768]{1,0:T(8,128)(2,1)S(1)}, u32[]{:S(2)}, u32[]{:S(2)}) collective-permute-start(bf16[128,768]{1,0:T(8,128)(2,1)S(1)} %collective-permute-done.4.refs_6_), channel_id=1, source_target_pairs={{7,0},{0,1},{1,2},{2,3},{3,4},{4,5},{5,6},{6,7},{15,8},{8,9},{9,10... | collective-permute-start | bytes 589832 | tf_op jit(solution)/shard_map/ppermute | solution.py:302
  106.9 4.4 %collective-permute-done.5.refs_5_ = bf16[128,768]{1,0:T(8,128)(2,1)S(1)} collective-permute-done((bf16[128,768]{1,0:T(8,128)(2,1)S(1)}, bf16[128,768]{1,0:T(8,128)(2,1)S(1)}, u32[]{:S(2)}, u32[]{:S(2)}) %collective-permute-start.5) | collective-permute-done | bytes 196640 | tf_op jit(solution)/shard_map/ppermute | solution.py:302
  111.4 4.8 %collective-permute-done.2.refs_3_ = bf16[128,768]{1,0:T(8,128)(2,1)S(1)} collective-permute-done((bf16[128,768]{1,0:T(8,128)(2,1)S(1)}, bf16[128,768]{1,0:T(8,128)(2,1)S(1)}, u32[]{:S(2)}, u32[]{:S(2)}) %collective-permute-start.2) | collective-permute-done | bytes 196640 | tf_op jit(solution)/shard_map/ppermute | solution.py:302
  116.1 3.8 %product.1 = f32[2,768,384]{2,1,0:T(8,128)} custom-call(s32[1]{0:T(128)} %bitcast.turn_ref, bf16[128,768]{1,0:T(8,128)(2,1)S(1)} %reshape.54.refs_0_, bf16[128,768]{1,0:T(8,128)(2,1)S(1)} %collective-permute-done.refs_1_, bf16[128,768]{1,0:T(8,128)(2,1)S(1)} %collective-permute-done.1.refs_2_, bf16[128,768]{1,0:T(8,128)(2,1)S(1)} %collective-permute-done.2.refs_3_, ...), custom_call_target="tpu_custom_call" | custom-call | tf_op jit(solution)/shard_map/product/pallas_call | solution.py:232
  (31 shorter events, 0.6 us)
Async XLA Ops:
  0.0 33.9 %copy-start = (s32[512,1]{1,0:T(8,128)S(1)}, s32[512,1]{1,0:T(8,128)}, u32[]{:S(2)}) copy-start(s32[512,1]{1,0:T(8,128)} %constant.71.clone.key_ref) | copy-start | bytes 6148
  0.0 33.9 %copy-start.1 = (bf16[160,256]{1,0:T(8,128)(2,1)S(1)}, bf16[160,256]{1,0:T(8,128)(2,1)}, u32[]{:S(2)}) copy-start(bf16[160,256]{1,0:T(8,128)(2,1)} %constant.70.clone.xt_ref) | copy-start | bytes 245764
  0.0 33.9 %copy-start.2 = (s32[12288]{0:T(1024)S(1)}, s32[12288]{0:T(1024)}, u32[]{:S(2)}) copy-start(s32[12288]{0:T(1024)} %param.19) | copy-start | bytes 147460
  4.6 74.0 %copy-start.3 = (s32[1024]{0:T(1024)S(1)}, s32[1024]{0:T(1024)}, u32[]{:S(2)}) copy-start(s32[1024]{0:T(1024)} %vi_ref.1) | copy-start | bytes 12292
  4.6 74.2 %copy-start.4 = (s32[1024]{0:T(1024)S(1)}, s32[1024]{0:T(1024)}, u32[]{:S(2)}) copy-start(s32[1024]{0:T(1024)} %ci_ref.1) | copy-start | bytes 12292
  4.6 74.4 %copy-start.7 = (f32[2]{0:T(128)S(1)}, f32[2]{0:T(128)}, u32[]{:S(2)}) copy-start(f32[2]{0:T(128)} %param.18) | copy-start | bytes 28
  37.5 21.6 %all-to-all-start.1 = ((bf16[64,2,768]{2,1,0:T(2,128)(2,1)}), bf16[64,2,768]{2,1,0:T(2,128)(2,1)S(1)}, u32[]{:S(2)}, u32[]{:S(2)}) async-start(bf16[64,2,768]{2,1,0:T(2,128)(2,1)} %select.7), calls=%async_computation.1 | async-start | bytes 393216 | tf_op jit(solution)/shard_map/all_to_all | solution.py:281
  46.8 33.0 %copy-start.5 = (f32[48]{0:T(128)S(1)}, f32[48]{0:T(128)}, u32[]{:S(2)}) copy-start(f32[48]{0:T(128)} %param.16) | copy-start | bytes 580
  46.8 33.1 %copy-start.6 = (f32[64]{0:T(128)S(1)}, f32[64]{0:T(128)}, u32[]{:S(2)}) copy-start(f32[64]{0:T(128)} %param.17) | copy-start | bytes 772
  59.2 9.3 %collective-permute-start.7 = (bf16[32,2,384]{2,1,0:T(2,128)(2,1)S(1)}, bf16[32,2,384]{2,1,0:T(2,128)(2,1)S(1)}, u32[]{:S(2)}, u32[]{:S(2)}) collective-permute-start(bf16[32,2,384]{2,1,0:T(2,128)(2,1)S(1)} %constant_dynamic-slice_fusion), channel_id=1, source_target_pairs={{0,0},{1,64},{2,128},{3,192},{4,256},{5,320},{6,384},{7,448},{8,1}... | collective-permute-start | bytes 147464 | tf_op jit(solution)/shard_map/ppermute | solution.py:288
  69.5 46.7 %all-to-all-start.2 = ((bf16[16,64,384]{2,1,0:T(8,128)(2,1)}), bf16[16,64,384]{2,1,0:T(8,128)(2,1)S(1)}, u32[]{:S(2)}, u32[]{:S(2)}) async-start(bf16[16,64,384]{2,1,0:T(8,128)(2,1)} %broadcast_in_dim.34), calls=%async_computation.2 | async-start | bytes 1572864 | tf_op jit(solution)/shard_map/all_to_all | solution.py:290
  80.0 23.7 %collective-permute-start.4 = (bf16[128,768]{1,0:T(8,128)(2,1)S(1)}, bf16[128,768]{1,0:T(8,128)(2,1)S(1)}, u32[]{:S(2)}, u32[]{:S(2)}) collective-permute-start(bf16[128,768]{1,0:T(8,128)(2,1)S(1)} %reshape.54.refs_0_), channel_id=1, source_target_pairs={{6,0},{7,1},{0,2},{1,3},{2,4},{3,5},{4,6},{5,7},{14,8},{15,9},{8,1... | collective-permute-start | bytes 589832 | tf_op jit(solution)/shard_map/ppermute | solution.py:302
  83.2 13.6 %collective-permute-start.1 = (bf16[128,768]{1,0:T(8,128)(2,1)S(1)}, bf16[128,768]{1,0:T(8,128)(2,1)S(1)}, u32[]{:S(2)}, u32[]{:S(2)}) collective-permute-start(bf16[128,768]{1,0:T(8,128)(2,1)S(1)} %reshape.54.refs_0_), channel_id=1, source_target_pairs={{2,0},{3,1},{4,2},{5,3},{6,4},{7,5},{0,6},{1,7},{10,8},{11,9},{12,... | collective-permute-start | bytes 589832 | tf_op jit(solution)/shard_map/ppermute | solution.py:302
  87.5 19.4 %collective-permute-start.6 = (bf16[128,768]{1,0:T(8,128)(2,1)S(1)}, bf16[128,768]{1,0:T(8,128)(2,1)S(1)}, u32[]{:S(2)}, u32[]{:S(2)}) collective-permute-start(bf16[128,768]{1,0:T(8,128)(2,1)S(1)} %reshape.54.refs_0_), channel_id=1, source_target_pairs={{7,0},{0,1},{1,2},{2,3},{3,4},{4,5},{5,6},{6,7},{15,8},{8,9},{9,10... | collective-permute-start | bytes 589832 | tf_op jit(solution)/shard_map/ppermute | solution.py:302
  90.7 16.3 %collective-permute-start = (bf16[128,768]{1,0:T(8,128)(2,1)S(1)}, bf16[128,768]{1,0:T(8,128)(2,1)S(1)}, u32[]{:S(2)}, u32[]{:S(2)}) collective-permute-start(bf16[128,768]{1,0:T(8,128)(2,1)S(1)} %reshape.54.refs_0_), channel_id=1, source_target_pairs={{1,0},{2,1},{3,2},{4,3},{5,4},{6,5},{7,6},{0,7},{9,8},{10,9},{11,1... | collective-permute-start | bytes 589832 | tf_op jit(solution)/shard_map/ppermute | solution.py:302
  96.9 14.5 %collective-permute-start.3 = (bf16[128,768]{1,0:T(8,128)(2,1)S(1)}, bf16[128,768]{1,0:T(8,128)(2,1)S(1)}, u32[]{:S(2)}, u32[]{:S(2)}) collective-permute-start(bf16[128,768]{1,0:T(8,128)(2,1)S(1)} %collective-permute-done.1.refs_2_), channel_id=1, source_target_pairs={{2,0},{3,1},{4,2},{5,3},{6,4},{7,5},{0,6},{1,7},{10,8},{11,9},{12,... | collective-permute-start | bytes 589832 | tf_op jit(solution)/shard_map/ppermute | solution.py:302
  100.5 15.6 %collective-permute-start.2 = (bf16[128,768]{1,0:T(8,128)(2,1)S(1)}, bf16[128,768]{1,0:T(8,128)(2,1)S(1)}, u32[]{:S(2)}, u32[]{:S(2)}) collective-permute-start(bf16[128,768]{1,0:T(8,128)(2,1)S(1)} %collective-permute-done.1.refs_2_), channel_id=1, source_target_pairs={{1,0},{2,1},{3,2},{4,3},{5,4},{6,5},{7,6},{0,7},{9,8},{10,9},{11,1... | collective-permute-start | bytes 589832 | tf_op jit(solution)/shard_map/ppermute | solution.py:302
  103.7 7.6 %collective-permute-start.5 = (bf16[128,768]{1,0:T(8,128)(2,1)S(1)}, bf16[128,768]{1,0:T(8,128)(2,1)S(1)}, u32[]{:S(2)}, u32[]{:S(2)}) collective-permute-start(bf16[128,768]{1,0:T(8,128)(2,1)S(1)} %collective-permute-done.4.refs_6_), channel_id=1, source_target_pairs={{7,0},{0,1},{1,2},{2,3},{3,4},{4,5},{5,6},{6,7},{15,8},{8,9},{9,10... | collective-permute-start | bytes 589832 | tf_op jit(solution)/shard_map/ppermute | solution.py:302

commit v5 on v2

--- a/solution.py
+++ b/solution.py
@@ -17,7 +17,6 @@
 COLS = 512
 PAIR_ROWS = 80
 TILE = 128
-CUTS = 1
 BF16 = jnp.bfloat16
 F32 = jnp.float32
 VMEM_LIMIT = 60 * 2**20
@@ -60,17 +59,25 @@
 
 def y_constant():
     cos, sin = tables()
+    out = np.zeros((2, GRID, 2, TILE), np.float64)
+    for q in range(-REACH, REACH + 1):
+        out[0, :, 0, q + REACH] = cos[:, q % GRID]
+        out[0, :, 1, q + REACH] = sin[:, q % GRID]
+        out[1, :, 0, q + REACH] = -sin[:, q % GRID]
+        out[1, :, 1, q + REACH] = cos[:, q % GRID]
+    return out.reshape(2, 2 * GRID, TILE)
+
+
+def y_runs():
     cols = columns()
-    blocks = []
+    runs = []
     for tile, (first, last) in enumerate(y_spans()):
-        block = np.zeros((last - first, GRID, 2, 2, TILE), np.float64)
-        for lane, (q, k) in enumerate(cols[tile * TILE : (tile + 1) * TILE]):
-            block[k - 1 - first, :, 0, 0, lane] = cos[:, q]
-            block[k - 1 - first, :, 1, 0, lane] = sin[:, q]
-            block[k - 1 - first, :, 0, 1, lane] = -sin[:, q]
-            block[k - 1 - first, :, 1, 1, lane] = cos[:, q]
-        blocks.append(block.reshape(-1, 2 * TILE))
-    return np.concatenate(blocks, 0)
+        own = cols[tile * TILE : (tile + 1) * TILE]
+        for k in range(first + 1, last + 1):
+            lanes = [lane for lane, col in enumerate(own) if col[1] == k]
+            q = own[lanes[0]][0]
+            runs.append((lanes[0], lanes[-1] + 1, (q + REACH) % GRID))
+    return runs
 
 
 def x_constant():
@@ -95,28 +102,43 @@
 
 
 def transform_kernel(
-    row_ref, vi_ref, ci_ref, val_hbm, cond_hbm, zt_hbm, yt_hbm, out_ref,
-    val_ref, cond_ref, zt_ref, yt_ref, dens_ref, part_ref, sems,
+    val_hbm, cond_hbm, vi_hbm, ci_hbm, yq_hbm, zt_hbm, out_ref,
+    val_ref, cond_ref, vi_ref, ci_ref, yq_ref, zt_ref, yt_ref, dens_ref, part_ref, sems,
 ):
     pairs = dens_ref.shape[0] // 2
-    moves = []
-    for src, dst, parts in (
-        (val_hbm, val_ref, CUTS),
-        (cond_hbm, cond_ref, CUTS),
-        (zt_hbm, zt_ref, 1),
-        (yt_hbm, yt_ref, CUTS),
-    ):
-        size = src.shape[0] // parts
-        for part in range(parts):
-            cut = pl.ds(part * size, size)
-            moves.append(pltpu.make_async_copy(src.at[cut], dst.at[cut], sems.at[len(moves)]))
-            moves[-1].start()
-    first_pair = row_ref[0] * pairs
-    for move in moves[: 2 * CUTS]:
+    moves = [
+        pltpu.make_async_copy(src, dst, sems.at[i])
+        for i, (src, dst) in enumerate(
+            (
+                (yq_hbm, yq_ref),
+                (val_hbm, val_ref),
+                (cond_hbm, cond_ref),
+                (vi_hbm, vi_ref),
+                (ci_hbm, ci_ref),
+                (zt_hbm, zt_ref),
+            )
+        )
+    ]
+    for move in moves:
+        move.start()
+    moves[0].wait()
+    lane = lax.broadcasted_iota(jnp.int32, (2 * GRID, TILE), 1)
+    for i, (first, last, place) in enumerate(y_runs()):
+        inside = (lane >= first) & (lane < last)
+        for out in range(2):
+            moved = pltpu.roll(yq_ref[out], (first - place) % TILE, 1)
+            yt_ref[2 * GRID * i : 2 * GRID * (i + 1), out * TILE : (out + 1) * TILE] = jnp.where(
+                inside, moved, 0.0
+            ).astype(BF16)
+    first_pair = (
+        (lax.axis_index("x") * 2 + lax.axis_index("z_lo")) * 2 + lax.axis_index("core")
+    ) * pairs
+    for move in moves[1:]:
         move.wait()
     for p in range(pairs):
-        dens_ref[2 * p : 2 * p + 2, :] = val_ref[vi_ref[first_pair + p]] * cond_ref[ci_ref[first_pair + p]]
-    moves[2 * CUTS].wait()
+        val = val_ref[vi_ref[first_pair + p]]
+        cond = cond_ref[ci_ref[first_pair + p]]
+        dens_ref[2 * p : 2 * p + 2, :] = val * cond
     for j in range(GRID // 4):
         zt = lax.dot_general(
             zt_ref[...],
@@ -126,8 +148,6 @@
         )
         part_ref[:, j * 8 : (j + 1) * 8, :] = zt.reshape(REACH, 8, 2 * pairs)
     low = lax.broadcasted_iota(jnp.int32, (2 * pairs, TILE), 0) % 8 < 4
-    for move in moves[2 * CUTS + 1 :]:
-        move.wait()
     row = 0
     for tile, (first, last) in enumerate(y_spans()):
         depth = (last - first) * 2 * GRID
@@ -145,35 +165,30 @@
             ).astype(BF16)
 
 
-def transform(row_index, pairs, val_index, cond_index, val_orbitals, cond_orbitals):
-    smem = pl.BlockSpec(memory_space=pltpu.SMEM)
+def transform(pairs, val_index, cond_index, val_orbitals, cond_orbitals):
     hbm = pl.BlockSpec(memory_space=pltpu.HBM)
-    z_table, y_table = z_constant(), y_constant()
+    y_table = jnp.asarray(jnp.asarray(y_constant(), BF16), F32)
+    z_table = jnp.asarray(z_constant(), BF16)
     return pl.pallas_call(
         transform_kernel,
         out_shape=jax.ShapeDtypeStruct((4 * pairs, COLS), BF16),
-        in_specs=[smem, smem, smem, hbm, hbm, hbm, hbm],
+        in_specs=[hbm] * 6,
         out_specs=pl.BlockSpec(memory_space=pltpu.VMEM),
         scratch_shapes=[
             pltpu.VMEM(val_orbitals.shape, BF16),
             pltpu.VMEM(cond_orbitals.shape, BF16),
+            pltpu.SMEM(val_index.shape, jnp.int32),
+            pltpu.SMEM(cond_index.shape, jnp.int32),
+            pltpu.VMEM(y_table.shape, F32),
             pltpu.VMEM(z_table.shape, BF16),
-            pltpu.VMEM(y_table.shape, BF16),
+            pltpu.VMEM((len(y_runs()) * 2 * GRID, 2 * TILE), BF16),
             pltpu.VMEM((2 * pairs, GRID * GRID), BF16),
             pltpu.VMEM((REACH, 2 * GRID, 2 * pairs), F32),
-            pltpu.SemaphoreType.DMA((3 * CUTS + 1,)),
+            pltpu.SemaphoreType.DMA((6,)),
         ],
         compiler_params=pltpu.CompilerParams(vmem_limit_bytes=VMEM_LIMIT),
         name="transform",
-    )(
-        row_index.reshape(1),
-        val_index,
-        cond_index,
-        val_orbitals,
-        cond_orbitals,
-        jnp.asarray(z_table, BF16),
-        jnp.asarray(y_table, BF16),
-    )
+    )(val_orbitals, cond_orbitals, val_index, cond_index, y_table, z_table)
 
 
 def select_kernel(y_ref, xt_ref, key_ref, gmap_ref, out_ref):
@@ -263,9 +278,7 @@
     row_count = lax.axis_size(ROW)
     col_count = lax.axis_size(COL)
     pair_dev = val_index.shape[0] // row_count
-    partial = transform(
-        lax.axis_index(ROW), pair_dev, val_index, cond_index, val_orbitals, cond_orbitals
-    )
+    partial = transform(pair_dev, val_index, cond_index, val_orbitals, cond_orbitals)
     block = lax.all_to_all(
         partial.reshape(col_count, 8, COLS), COL, split_axis=0, concat_axis=0, tiled=True
     ).reshape(4 * GRID, COLS)

time: 112 us -> 111 us (level)
  no operation moved by 1% of the time
where the time goes in v5:
time: 111 us; the launch traced here: 110 us
  blocking collectives  50.5 us (45%)
  waiting for transfers between devices  16.4 us (15%)
  between operations  13.6 us (12%)
  starting transfers between devices  13.1 us (12%)
  Pallas kernels  11 us (10%)
  local copies, waits for them, and re-layouts  4.48 us (4%)
    all_to_all x1, blocking collectives, shards(): lax.all_to_all(partial.reshape(col_count, 8, COLS), COL, split_axis=0, co...  29.2 us
    all_to_all x1, blocking collectives, shards(): lax.all_to_all(for_rows, ROW + ('z_hi',), split_axis=0, concat_axis=0, ti...  21.4 us
    all_to_all x1, waiting for transfers between devices, shards(): lax.all_to_all(jnp.broadcast_to(column, (row_count, pair_dev, width)), RO...  11 us
    all_to_all x1, starting transfers between devices, shards(): lax.all_to_all(jnp.broadcast_to(column, (row_count, pair_dev, width)), RO...  9.25 us
    ppermute x1, waiting for transfers between devices, shards(): column = lax.ppermute(piece, ROW + COL, column_moves())  5.45 us
    pallas_call x1, Pallas kernels, product(): pl.pallas_call(product_kernel, grid=(rows // step,), out_shape=jax.ShapeD...  4.45 us
    ppermute x1, starting transfers between devices, shards(): column = lax.ppermute(piece, ROW + COL, column_moves())  3.85 us
    pallas_call x1, Pallas kernels, transform(): pl.pallas_call(transform_kernel, out_shape=jax.ShapeDtypeStruct((4 * pair...  3.61 us
  transfers between devices with their start and end apart: 3, of which 2 were waited for; matrix products, arithmetic and copies ran while one was open for 3% of the time, Pallas kernels for 0%

profile of v5, /device:TPU:1, one launch (start us, length us, event | category | flops | bytes accessed | tf_op | source)
XLA Modules:
  0.0 110.0 jit_solution(7073717506703608780)
XLA Ops:
  6.5 3.6 %transform.1 = bf16[256,512]{1,0:T(8,128)(2,1)} custom-call(bf16[48,2,4096]{2,1,0:T(2,128)(2,1)} %val_hbm.1, bf16[64,2,4096]{2,1,0:T(2,128)(2,1)} %cond_hbm.1, s32[1024]{0:T(1024)} %vi_hbm.1, s32[1024]{0:T(1024)} %ci_hbm.1, f32[2,128,128]{2,1,0:T(8,128)} %constant.56.yq_hbm, bf16[144,256]{1,0:T(8,128)(2,1)} %constant.51.clone.zt_hbm), custom_call_target="tpu_custom_call" | custom-call | tf_op jit(solution)/shard_map/transform/pallas_call | solution.py:172
  10.2 0.0 copy-start.4
  10.2 29.2 %all_to_all.15 = bf16[32,8,512]{2,1,0:T(8,128)(2,1)S(1)} all-to-all(bf16[32,8,512]{2,1,0:T(8,128)(2,1)} %bitcast.9), channel_id=1, replica_groups=mesh['x'=4,'z_lo'=2,'core'=2,'z_hi'=4,'y'=8] {'z_hi','y'}, dimensions={0} | all-to-all | bytes 524288 | tf_op jit(solution)/shard_map/all_to_all | solution.py:282
  39.4 3.0 %select.7 = bf16[64,2,768]{2,1,0:T(2,128)(2,1)S(1)} custom-call(bf16[256,512]{1,0:T(8,128)(2,1)S(1)} %bitcast.6, bf16[160,256]{1,0:T(8,128)(2,1)S(1)} %copy-done.1, s32[512,1]{1,0:T(8,128)S(1)} %copy-done, s32[16,1,768]{2,1,0:T(1,128)S(1)} %bitcast.7), custom_call_target="tpu_custom_call" | custom-call | tf_op jit(solution)/shard_map/select/pallas_call | solution.py:220
  42.3 21.4 %all_to_all.16 = bf16[64,2,768]{2,1,0:T(2,128)(2,1)S(1)} all-to-all(bf16[64,2,768]{2,1,0:T(2,128)(2,1)S(1)} %select.7), channel_id=1, replica_groups=mesh['x'=4,'z_lo'=2,'core'=2,'z_hi'=4,'y'=8] {'x','z_lo','core','z_hi'}, dimensions={0} | all-to-all | bytes 393216 | tf_op jit(solution)/shard_map/all_to_all | solution.py:286
  63.7 0.8 reshape.43
  64.5 0.0 all-gather.2.cloned.1.call-update
  64.5 0.8 dynamic_slice.3
  65.3 3.8 %collective-permute-start = (bf16[64,384]{1,0:T(8,128)(2,1)S(1)}, bf16[64,384]{1,0:T(8,128)(2,1)S(1)}, u32[]{:S(2)}, u32[]{:S(2)}) collective-permute-start(bf16[64,384]{1,0:T(8,128)(2,1)S(1)} %dynamic_slice.3), channel_id=1, source_target_pairs={{0,0},{1,64},{2,128},{3,192},{4,256},{5,320},{6,384},{7,448},{8,1}... | collective-permute-start | bytes 147464 | tf_op jit(solution)/shard_map/ppermute | solution.py:292
  69.2 5.5 %collective-permute-done = bf16[64,384]{1,0:T(8,128)(2,1)S(1)} collective-permute-done((bf16[64,384]{1,0:T(8,128)(2,1)S(1)}, bf16[64,384]{1,0:T(8,128)(2,1)S(1)}, u32[]{:S(2)}, u32[]{:S(2)}) %collective-permute-start) | collective-permute-done | bytes 49184 | tf_op jit(solution)/shard_map/ppermute | solution.py:292
  74.7 1.0 broadcast_in_dim.34
  75.6 9.2 %all-to-all-start.2 = ((bf16[16,64,384]{2,1,0:T(8,128)(2,1)}), bf16[16,64,384]{2,1,0:T(8,128)(2,1)S(1)}, u32[]{:S(2)}, u32[]{:S(2)}) async-start(bf16[16,64,384]{2,1,0:T(8,128)(2,1)} %broadcast_in_dim.34), calls=%async_computation.2 | async-start | bytes 1572864 | tf_op jit(solution)/shard_map/all_to_all | solution.py:293
  84.9 0.2 reshape.46
  85.1 0.2 reshape.45
  85.3 0.1 copy.16
  85.4 0.2 eq.36
  85.6 0.1 copy.15
  85.7 0.2 eq.32
  86.0 0.1 select_reduce_fusion.1
  86.1 0.1 select_reduce_fusion
  86.2 0.7 add_divide_fusion.weight_ref
  86.9 11.0 %all-to-all-done.2 = bf16[16,64,384]{2,1,0:T(8,128)(2,1)S(1)} async-done(((bf16[16,64,384]{2,1,0:T(8,128)(2,1)}), bf16[16,64,384]{2,1,0:T(8,128)(2,1)S(1)}, u32[]{:S(2)}, u32[]{:S(2)}) %all-to-all-start.2) | async-done | bytes 786464 | tf_op jit(solution)/shard_map/all_to_all | solution.py:293
  97.9 0.9 copy-done.3
  98.7 4.4 %product.1 = f32[2,768,384]{2,1,0:T(8,128)} custom-call(bf16[1024,768]{1,0:T(8,128)(2,1)} %all-gather.2.cloned.1.call-done.left_ref, bf16[1024,384]{1,0:T(8,128)(2,1)} %bitcast.8, f32[2,1024]{1,0:T(2,128)} %add_divide_fusion.weight_ref), custom_call_target="tpu_custom_call" | custom-call | tf_op jit(solution)/shard_map/product/pallas_call | solution.py:241
  (20 shorter events, 0.1 us)
Async XLA Ops:
  6.5 32.8 %copy-start = (s32[512,1]{1,0:T(8,128)S(1)}, s32[512,1]{1,0:T(8,128)}, u32[]{:S(2)}) copy-start(s32[512,1]{1,0:T(8,128)} %constant.53.clone.key_ref) | copy-start | bytes 6148
  6.5 32.8 %copy-start.1 = (bf16[160,256]{1,0:T(8,128)(2,1)S(1)}, bf16[160,256]{1,0:T(8,128)(2,1)}, u32[]{:S(2)}) copy-start(bf16[160,256]{1,0:T(8,128)(2,1)} %constant.52.clone.xt_ref) | copy-start | bytes 245764
  6.5 32.8 %copy-start.2 = (s32[12288]{0:T(1024)S(1)}, s32[12288]{0:T(1024)}, u32[]{:S(2)}) copy-start(s32[12288]{0:T(1024)} %param.19) | copy-start | bytes 147460
  6.5 91.3 %all-gather.2.cloned.1.call-start = ((), (), s32[]{:S(2)}) async-start(), calls=%async_computation.3 | async-start | bytes 1769472 | tf_op jit(solution)/shard_map/all_gather | solution.py:288
  10.2 74.7 %copy-start.4 = (s32[1024]{0:T(1024)S(1)}, s32[1024]{0:T(1024)}, u32[]{:S(2)}) copy-start(s32[1024]{0:T(1024)} %vi_hbm.1) | copy-start | bytes 12292
  39.3 45.8 %copy-start.5 = (s32[1024]{0:T(1024)S(1)}, s32[1024]{0:T(1024)}, u32[]{:S(2)}) copy-start(s32[1024]{0:T(1024)} %ci_hbm.1) | copy-start | bytes 12292
  39.3 46.0 %copy-start.8 = (f32[2]{0:T(128)S(1)}, f32[2]{0:T(128)}, u32[]{:S(2)}) copy-start(f32[2]{0:T(128)} %param.18) | copy-start | bytes 28
  64.5 21.5 %copy-start.6 = (f32[48]{0:T(128)S(1)}, f32[48]{0:T(128)}, u32[]{:S(2)}) copy-start(f32[48]{0:T(128)} %param.16) | copy-start | bytes 580
  64.5 21.6 %copy-start.7 = (f32[64]{0:T(128)S(1)}, f32[64]{0:T(128)}, u32[]{:S(2)}) copy-start(f32[64]{0:T(128)} %param.17) | copy-start | bytes 772
  65.3 9.3 %collective-permute-start = (bf16[64,384]{1,0:T(8,128)(2,1)S(1)}, bf16[64,384]{1,0:T(8,128)(2,1)S(1)}, u32[]{:S(2)}, u32[]{:S(2)}) collective-permute-start(bf16[64,384]{1,0:T(8,128)(2,1)S(1)} %dynamic_slice.3), channel_id=1, source_target_pairs={{0,0},{1,64},{2,128},{3,192},{4,256},{5,320},{6,384},{7,448},{8,1}... | collective-permute-start | bytes 147464 | tf_op jit(solution)/shard_map/ppermute | solution.py:292
  75.6 22.2 %all-to-all-start.2 = ((bf16[16,64,384]{2,1,0:T(8,128)(2,1)}), bf16[16,64,384]{2,1,0:T(8,128)(2,1)S(1)}, u32[]{:S(2)}, u32[]{:S(2)}) async-start(bf16[16,64,384]{2,1,0:T(8,128)(2,1)} %broadcast_in_dim.34), calls=%async_computation.2 | async-start | bytes 1572864 | tf_op jit(solution)/shard_map/all_to_all | solution.py:293
  97.9 0.9 copy-start.3
Sparse Core Ops, SparseCore 0:
  64.6 31.5 all-gather.1

commit v6 on v5

--- a/solution.py
+++ b/solution.py
@@ -11,6 +11,7 @@
 
 GRID = 64
 NG = 12288
+PAIRS = 1024
 REACH = 18
 SIDE = 2 * REACH + 1
 RADIUS2 = 334
@@ -195,7 +196,7 @@
     spec = jnp.dot(xt_ref[...], y_ref[...], preferred_element_type=F32)
     spec = (spec * float(GRID) ** (-1.5)).astype(BF16)
     rows, _, width = gmap_ref.shape
-    copies = out_ref.shape[0] // rows
+    half = width // 2
     side = lax.broadcasted_iota(jnp.int32, (PAIR_ROWS, width), 0)
     for r in range(rows):
         entry = gmap_ref[r]
@@ -210,49 +211,98 @@
             for i in range(2)
         ]
         both = jnp.concatenate(picked, 0).astype(BF16)
-        for copy in range(copies):
-            out_ref[r * copies + copy] = both
-
-
-def select(block, gmap, copies, rows):
+        halves = both[:, :half], both[:, half:]
+        for col in range(2 * rows):
+            out_ref[r * 2 * rows + col, :, :half] = halves[col % 2]
+        for which in range(2):
+            col = 2 * r + which
+            for other in range(rows):
+                start = other % 2 * TILE
+                out_ref[other * 2 * rows + col, :, half:] = halves[which][:, start : start + 2 * TILE]
+
+
+def select(block, gmap, rows):
     width = NG // rows
     vmem = pl.BlockSpec(memory_space=pltpu.VMEM)
     return pl.pallas_call(
         select_kernel,
-        out_shape=jax.ShapeDtypeStruct((rows * copies, 2, width), BF16),
+        out_shape=jax.ShapeDtypeStruct((2 * rows * rows, 2, width // 2 + 2 * TILE), BF16),
         in_specs=[vmem] * 4,
         out_specs=vmem,
-        compiler_params=pltpu.CompilerParams(vmem_limit_bytes=40 * 2**20),
+        compiler_params=pltpu.CompilerParams(vmem_limit_bytes=32 * 2**20),
         name="select",
     )(block, jnp.asarray(x_constant(), BF16), jnp.asarray(column_keys()), gmap.reshape(rows, 1, width))
 
 
-def product_kernel(left_ref, right_ref, weight_ref, out_ref):
-    turned = left_ref[...].T.astype(F32)
-    for f in range(out_ref.shape[0]):
+def half_product(left, right, weight_ref, out_ref, res_ref, sems, half):
+    pairs, rows = left.shape
+    turned = left.T.astype(F32)
+    place = pl.ds(pl.multiple_of(half * rows, rows), rows)
+    moves = []
+    for f in range(weight_ref.shape[0]):
         weighted = (turned * weight_ref[f : f + 1, :]).astype(BF16)
-        part = jnp.dot(weighted, right_ref[...], preferred_element_type=F32)
-        out_ref[f] = part * (1.0 / math.sqrt(left_ref.shape[0]))
-
-
-def product(left, right, weights, step=384):
-    pairs, rows = left.shape
-    width = right.shape[1]
+        total = jnp.dot(weighted, right, preferred_element_type=F32)
+        res_ref[f] = total * (1.0 / math.sqrt(pairs))
+        moves.append(pltpu.make_async_copy(res_ref.at[f], out_ref.at[f, place], sems.at[f]))
+        moves[-1].start()
+    for move in moves:
+        move.wait()
+
+
+def own_kernel(mine_ref, third_ref, weight_ref, out_ref, right_ref, res_ref, sems):
+    pairs = right_ref.shape[0]
+    half = mine_ref.shape[2] - 2 * TILE
+    core = lax.axis_index("core")
+    here = pl.ds(pl.multiple_of(core * TILE, TILE), 2 * TILE)
+    there = pl.ds(pl.multiple_of((1 - core) * 2 * TILE, TILE), TILE)
+    right_ref[:, here] = mine_ref[:, :, half:].reshape(pairs, 2 * TILE)
+    right_ref[:, there] = third_ref[...].reshape(pairs, TILE)
+    left = mine_ref[:, :, :half].reshape(pairs, half)
+    half_product(left, right_ref[...], weight_ref, out_ref, res_ref, sems, lax.axis_index("y") % 2)
+
+
+def rest_kernel(low_ref, high_ref, right_ref, weight_ref, begun_ref, out_ref, res_ref, sems):
+    part, _, half = low_ref.shape
+    left = jnp.concatenate(
+        [low_ref[...].reshape(2 * part, half), high_ref[...].reshape(2 * part, half)], 0
+    )
+    half_product(left, right_ref[...], weight_ref, out_ref, res_ref, sems, 1 - lax.axis_index("y") % 2)
+
+
+def half_call(kernel, name, in_specs, out_shape, out_specs, half, width, aliases):
+    work = 2 * 2 * PAIRS * half * width
     return pl.pallas_call(
-        product_kernel,
-        grid=(rows // step,),
-        out_shape=jax.ShapeDtypeStruct((weights.shape[0], rows, width), F32),
-        in_specs=[
-            pl.BlockSpec((pairs, step), lambda i: (0, i)),
-            pl.BlockSpec((pairs, width), lambda i: (0, 0)),
-            pl.BlockSpec(weights.shape, lambda i: (0, 0)),
-        ],
-        out_specs=pl.BlockSpec((weights.shape[0], step, width), lambda i: (0, i, 0)),
-        compiler_params=pltpu.CompilerParams(
-            dimension_semantics=("arbitrary",), vmem_limit_bytes=VMEM_LIMIT
-        ),
-        name="product",
-    )(left, right, weights)
+        kernel,
+        out_shape=out_shape,
+        in_specs=in_specs,
+        out_specs=out_specs,
+        scratch_shapes=[pltpu.VMEM((2, half, width), F32), pltpu.SemaphoreType.DMA((2,))],
+        input_output_aliases=aliases,
+        cost_estimate=pl.CostEstimate(flops=work, bytes_accessed=5 * 2**20, transcendentals=0),
+        compiler_params=pltpu.CompilerParams(vmem_limit_bytes=32 * 2**20),
+        name=name,
+    )
+
+
+def own_product(mine, third, weights, rows, width):
+    vmem = pl.BlockSpec(memory_space=pltpu.VMEM)
+    hbm = pl.BlockSpec(memory_space=pltpu.HBM)
+    shapes = (
+        jax.ShapeDtypeStruct((weights.shape[0], rows, width), F32),
+        jax.ShapeDtypeStruct((PAIRS, width), BF16),
+    )
+    call = half_call(own_kernel, "own_half", [vmem] * 3, shapes, (hbm, vmem), rows // 2, width, {})
+    return call(mine, third, weights)
+
+
+def rest_product(low, high, right, weights, begun):
+    vmem = pl.BlockSpec(memory_space=pltpu.VMEM)
+    hbm = pl.BlockSpec(memory_space=pltpu.HBM)
+    _, rows, width = begun.shape
+    shape = jax.ShapeDtypeStruct(begun.shape, F32)
+    specs = [vmem] * 4 + [hbm]
+    call = half_call(rest_kernel, "other_half", specs, shape, hbm, rows // 2, width, {4: 0})
+    return call(low, high, right, weights, begun)
 
 
 def pair_weights(val_index, cond_index, val_energy, cond_energy, freqs):
@@ -266,10 +316,6 @@
 
 ROW = ("x", "z_lo", "core")
 COL = ("z_hi", "y")
-
-
-def reorder(pair_values):
-    return pair_values.reshape(16, 4, 8, 2).transpose(2, 0, 1, 3).reshape(-1)
 
 
 def shards(
@@ -282,28 +328,22 @@
     block = lax.all_to_all(
         partial.reshape(col_count, 8, COLS), COL, split_axis=0, concat_axis=0, tiled=True
     ).reshape(4 * GRID, COLS)
-    for_rows = select(block, gmap, 4, row_count)
-    mine = lax.all_to_all(for_rows, ROW + ("z_hi",), split_axis=0, concat_axis=0, tiled=True)
-    mine = mine.reshape(-1, NG // row_count)
-    left = lax.all_gather(mine, "y", axis=0, tiled=True)
-    width = NG // col_count
-    z_hi = lax.axis_index("z_hi")
-    piece = lax.dynamic_slice(mine, (z_hi // 2 * pair_dev, z_hi % 2 * width), (pair_dev, width))
-    column = lax.ppermute(piece, ROW + COL, column_moves())
-    right = lax.all_to_all(
-        jnp.broadcast_to(column, (row_count, pair_dev, width)), ROW, split_axis=0, concat_axis=0, tiled=True
-    ).reshape(-1, width)
-    weights = pair_weights(reorder(val_index), reorder(cond_index), val_energy, cond_energy, freqs)
-    return product(left, right, weights)
-
-
-def column_moves():
-    moves = []
-    for row in range(16):
-        for z_hi in range(4):
-            for y in range(8):
-                moves.append((row * 32 + z_hi * 8 + y, (2 * y + z_hi // 2) * 32 + 2 * row + z_hi % 2))
-    return moves
+    mine = lax.all_to_all(
+        select(block, gmap, row_count), ROW + COL, split_axis=0, concat_axis=0, tiled=True
+    )
+    sources = mine.shape[0] // 2
+    rows, width = NG // row_count, NG // col_count
+    half = rows // 2
+    third = lax.dynamic_slice(
+        mine, (0, 0, half + lax.axis_index("core") * TILE), (2 * sources, 2, TILE)
+    )
+    third = lax.ppermute(third, "core", [(0, 1), (1, 0)])
+    count = lax.axis_size("y")
+    low = lax.ppermute(mine[:sources, :, :half], "y", [((i + 1) % count, i) for i in range(count)])
+    high = lax.ppermute(mine[sources:, :, :half], "y", [(i, (i + 1) % count) for i in range(count)])
+    weights = pair_weights(val_index, cond_index, val_energy, cond_energy, freqs)
+    begun, right = own_product(mine, third, weights, rows, width)
+    return rest_product(low, high, right, weights, begun)
 
 
 def solution(mesh):

time: 111 us -> 108 us (0.973)
  waiting for transfers between devices: 16.4 us -> 42.9 us
  blocking collectives: 50.5 us -> 29.2 us
  between operations: 13.6 us -> 0.16 us
  starting transfers between devices: 13.1 us -> 21.9 us
  local copies, waits for them, and re-layouts: 4.48 us -> 0.76 us
    all_to_all x1, waiting for transfers between devices: 11 us -> 37 us  [shards(): lax.all_to_all(select(block, gmap, row_count), ROW + COL, split_axis=0, c...]
    all_to_all x1 -> x0, blocking collectives: 21.4 us -> none  [shards(): lax.all_to_all(for_rows, ROW + ('z_hi',), split_axis=0, concat_axis=0, ti...]
    ppermute x1 -> x3, starting transfers between devices: 3.85 us -> 9.42 us  [the longest x1 3.61 us: shards(): lax.ppermute(mine[:sources, :, :half], 'y', [((i + 1) % count, i) for i i...]
    all_to_all x1, starting transfers between devices: 9.25 us -> 12.5 us  [shards(): lax.all_to_all(select(block, gmap, row_count), ROW + COL, split_axis=0, c...]
    reshape x3 -> x0, local copies, waits for them, and re-layouts: 1.16 us -> none  [the longest x1 0.76 us: shards(): mine = mine.reshape(-1, NG // row_count)]
    pallas_call x2 -> x3, Pallas kernels: 7.42 us -> 8.49 us  [the longest x1 4.32 us: select(): pl.pallas_call(select_kernel, out_shape=jax.ShapeDtypeStruct((2 * rows *...]
    ppermute x1 -> x3, waiting for transfers between devices: 5.45 us -> 5.88 us  [the longest x1 4.94 us: shards(): lax.ppermute(mine[sources:, :, :half], 'y', [(i, (i + 1) % count) for i i...]
  transfers between devices with their start and end apart: 3 -> 4, of which waited for: 2 -> 3; matrix products, arithmetic and copies ran while one was open for 3% -> 1% of each run, Pallas kernels for 0% -> 2%
where the time goes in v6:
time: 108 us; the launch traced here: 107 us
  waiting for transfers between devices  42.9 us (40%)
  blocking collectives  29.2 us (27%)
  starting transfers between devices  21.9 us (20%)
  Pallas kernels  12.1 us (11%)
    all_to_all x1, waiting for transfers between devices, shards(): lax.all_to_all(select(block, gmap, row_count), ROW + COL, split_axis=0, c...  37 us
    all_to_all x1, blocking collectives, shards(): lax.all_to_all(partial.reshape(col_count, 8, COLS), COL, split_axis=0, co...  29.2 us
    all_to_all x1, starting transfers between devices, shards(): lax.all_to_all(select(block, gmap, row_count), ROW + COL, split_axis=0, c...  12.5 us
    ppermute x1, waiting for transfers between devices, shards(): lax.ppermute(mine[sources:, :, :half], 'y', [(i, (i + 1) % count) for i i...  4.94 us
    pallas_call x1, Pallas kernels, select(): pl.pallas_call(select_kernel, out_shape=jax.ShapeDtypeStruct((2 * rows *...  4.32 us
    pallas_call x1, Pallas kernels, transform(): pl.pallas_call(transform_kernel, out_shape=jax.ShapeDtypeStruct((4 * pair...  3.62 us
    ppermute x1, starting transfers between devices, shards(): lax.ppermute(mine[:sources, :, :half], 'y', [((i + 1) % count, i) for i i...  3.61 us
    ppermute x1, starting transfers between devices, shards(): third = lax.ppermute(third, 'core', [(0, 1), (1, 0)])  2.93 us
  transfers between devices with their start and end apart: 4, of which 3 were waited for; matrix products, arithmetic and copies ran while one was open for 1% of the time, Pallas kernels for 2%

profile of v6, /device:TPU:1, one launch (start us, length us, event | category | flops | bytes accessed | tf_op | source)
XLA Modules:
  0.0 107.3 jit_solution(13140206793905386287)
XLA Ops:
  0.0 3.6 %transform.1 = bf16[256,512]{1,0:T(8,128)(2,1)} custom-call(bf16[48,2,4096]{2,1,0:T(2,128)(2,1)} %val_hbm.1, bf16[64,2,4096]{2,1,0:T(2,128)(2,1)} %cond_hbm.1, s32[1024]{0:T(1024)} %vi_hbm.1, s32[1024]{0:T(1024)} %ci_hbm.1, f32[2,128,128]{2,1,0:T(8,128)} %constant.33.yq_hbm, bf16[144,256]{1,0:T(8,128)(2,1)} %constant.28.clone.zt_hbm), custom_call_target="tpu_custom_call" | custom-call | tf_op jit(solution)/shard_map/transform/pallas_call | solution.py:173
  3.6 29.2 %all_to_all.10 = bf16[32,8,512]{2,1,0:T(8,128)(2,1)S(1)} all-to-all(bf16[32,8,512]{2,1,0:T(8,128)(2,1)} %bitcast.5), channel_id=1, replica_groups=mesh['x'=4,'z_lo'=2,'core'=2,'z_hi'=4,'y'=8] {'z_hi','y'}, dimensions={0} | all-to-all | bytes 524288 | tf_op jit(solution)/shard_map/all_to_all | solution.py:328
  32.8 0.0 copy-done
  32.8 0.0 copy-done.1
  32.8 0.0 copy-done.2
  32.8 4.3 %select.1 = bf16[512,2,640]{2,1,0:T(2,128)(2,1)} custom-call(bf16[256,512]{1,0:T(8,128)(2,1)S(1)} %bitcast.3, bf16[160,256]{1,0:T(8,128)(2,1)S(1)} %copy-done.1, s32[512,1]{1,0:T(8,128)S(1)} %copy-done, s32[16,1,768]{2,1,0:T(1,128)S(1)} %bitcast.4), custom_call_target="tpu_custom_call" | custom-call | tf_op jit(solution)/shard_map/select/pallas_call | solution.py:227
  37.1 12.5 %all-to-all-start.1 = ((bf16[512,2,640]{2,1,0:T(2,128)(2,1)}), bf16[512,2,640]{2,1,0:T(2,128)(2,1)S(1)}, u32[]{:S(2)}, u32[]{:S(2)}) async-start(bf16[512,2,640]{2,1,0:T(2,128)(2,1)} %select.1), calls=%async_computation.1 | async-start | bytes 2621440 | tf_op jit(solution)/shard_map/all_to_all | solution.py:331
  49.6 0.0 copy-start.7
  49.7 0.0 copy-done.3
  49.7 0.1 select_reduce_fusion.1
  49.8 0.1 select_reduce_fusion
  49.9 37.0 %all-to-all-done.1.mine_ref = bf16[512,2,640]{2,1,0:T(2,128)(2,1)S(1)} async-done(((bf16[512,2,640]{2,1,0:T(2,128)(2,1)}), bf16[512,2,640]{2,1,0:T(2,128)(2,1)S(1)}, u32[]{:S(2)}, u32[]{:S(2)}) %all-to-all-start.1) | async-done | bytes 1310752 | tf_op jit(solution)/shard_map/all_to_all | solution.py:331
  86.9 0.2 constant_dynamic-slice_fusion
  87.1 2.9 %collective-permute-start.2 = (bf16[512,2,128]{2,1,0:T(2,128)(2,1)S(1)}, bf16[512,2,128]{2,1,0:T(2,128)(2,1)S(1)}, u32[]{:S(2)}, u32[]{:S(2)}) collective-permute-start(bf16[512,2,128]{2,1,0:T(2,128)(2,1)S(1)} %constant_dynamic-slice_fusion), channel_id=1, source_target_pairs={{0,32},{32,0},{1,33},{33,1},{2,34},{34,2},{3,35},{35,3},{4,36},{36... | collective-permute-start | bytes 786440 | tf_op jit(solution)/shard_map/ppermute | solution.py:340
  90.0 0.5 fusion
  90.6 2.9 %collective-permute-start.1 = (bf16[256,2,384]{2,1,0:T(2,128)(2,1)S(1)}, bf16[256,2,384]{2,1,0:T(2,128)(2,1)S(1)}, u32[]{:S(2)}, u32[]{:S(2)}) collective-permute-start(bf16[256,2,384]{2,1,0:T(2,128)(2,1)S(1)} %get-tuple-element.9), channel_id=1, source_target_pairs={{0,1},{1,2},{2,3},{3,4},{4,5},{5,6},{6,7},{7,0},{8,9},{9,10},{10,1... | collective-permute-start | bytes 1179656 | tf_op jit(solution)/shard_map/ppermute | solution.py:343
  93.5 3.6 %collective-permute-start = (bf16[256,2,384]{2,1,0:T(2,128)(2,1)S(1)}, bf16[256,2,384]{2,1,0:T(2,128)(2,1)S(1)}, u32[]{:S(2)}, u32[]{:S(2)}) collective-permute-start(bf16[256,2,384]{2,1,0:T(2,128)(2,1)S(1)} %get-tuple-element.10), channel_id=1, source_target_pairs={{1,0},{2,1},{3,2},{4,3},{5,4},{6,5},{7,6},{0,7},{9,8},{10,9},{11,1... | collective-permute-start | bytes 1179656 | tf_op jit(solution)/shard_map/ppermute | solution.py:342
  97.1 0.0 copy-done.7
  97.1 0.1 add_divide_fusion.weight_ref
  97.2 0.0 collective-permute-done.2.third_ref
  97.2 2.3 %own_half.1 = (f32[2,768,384]{2,1,0:T(8,128)}, bf16[1024,384]{1,0:T(8,128)(2,1)S(1)}) custom-call(bf16[512,2,640]{2,1,0:T(2,128)(2,1)S(1)} %all-to-all-done.1.mine_ref, bf16[512,2,128]{2,1,0:T(2,128)(2,1)S(1)} %collective-permute-done.2.third_ref, f32[2,1024]{1,0:T(2,128)S(1)} %add_divide_fusion.weight_ref), custom_call_target="tpu_custom_call" | custom-call | flops 603979776 | bytes 5242880 | tf_op jit(solution)/shard_map/own_half/pallas_call | solution.py:295
  99.5 4.9 %collective-permute-done.1.high_ref = bf16[256,2,384]{2,1,0:T(2,128)(2,1)S(1)} collective-permute-done((bf16[256,2,384]{2,1,0:T(2,128)(2,1)S(1)}, bf16[256,2,384]{2,1,0:T(2,128)(2,1)S(1)}, u32[]{:S(2)}, u32[]{:S(2)}) %collective-permute-start.1) | collective-permute-done | bytes 393248 | tf_op jit(solution)/shard_map/ppermute | solution.py:343
  104.4 0.9 collective-permute-done.low_ref
  105.4 1.9 %other_half.1 = f32[2,768,384]{2,1,0:T(8,128)} custom-call(bf16[256,2,384]{2,1,0:T(2,128)(2,1)S(1)} %collective-permute-done.low_ref, bf16[256,2,384]{2,1,0:T(2,128)(2,1)S(1)} %collective-permute-done.1.high_ref, bf16[1024,384]{1,0:T(8,128)(2,1)S(1)} %get-tuple-element.7.right_ref, ...), custom_call_target="tpu_custom_call", output_to_operand_aliasing={{}: (4, {})} | custom-call | flops 603979776 | bytes 5242880 | tf_op jit(solution)/shard_map/other_half/pallas_call | solution.py:305
  (12 shorter events, 0.0 us)
Async XLA Ops:
  0.0 32.8 %copy-start = (s32[512,1]{1,0:T(8,128)S(1)}, s32[512,1]{1,0:T(8,128)}, u32[]{:S(2)}) copy-start(s32[512,1]{1,0:T(8,128)} %constant.30.clone.key_ref) | copy-start | bytes 6148
  0.0 32.8 %copy-start.1 = (bf16[160,256]{1,0:T(8,128)(2,1)S(1)}, bf16[160,256]{1,0:T(8,128)(2,1)}, u32[]{:S(2)}) copy-start(bf16[160,256]{1,0:T(8,128)(2,1)} %constant.29.clone.xt_ref) | copy-start | bytes 245764
  0.0 32.8 %copy-start.2 = (s32[12288]{0:T(1024)S(1)}, s32[12288]{0:T(1024)}, u32[]{:S(2)}) copy-start(s32[12288]{0:T(1024)} %param.19) | copy-start | bytes 147460
  37.1 12.5 %copy-start.3 = (s32[1024]{0:T(1024)S(1)}, s32[1024]{0:T(1024)}, u32[]{:S(2)}) copy-start(s32[1024]{0:T(1024)} %vi_hbm.1) | copy-start | bytes 12292
  37.1 12.6 %copy-start.5 = (f32[48]{0:T(128)S(1)}, f32[48]{0:T(128)}, u32[]{:S(2)}) copy-start(f32[48]{0:T(128)} %param.16) | copy-start | bytes 580
  37.1 12.7 %copy-start.4 = (s32[1024]{0:T(1024)S(1)}, s32[1024]{0:T(1024)}, u32[]{:S(2)}) copy-start(s32[1024]{0:T(1024)} %ci_hbm.1) | copy-start | bytes 12292
  37.1 12.7 %copy-start.6 = (f32[64]{0:T(128)S(1)}, f32[64]{0:T(128)}, u32[]{:S(2)}) copy-start(f32[64]{0:T(128)} %param.17) | copy-start | bytes 772
  37.1 49.8 %all-to-all-start.1 = ((bf16[512,2,640]{2,1,0:T(2,128)(2,1)}), bf16[512,2,640]{2,1,0:T(2,128)(2,1)S(1)}, u32[]{:S(2)}, u32[]{:S(2)}) async-start(bf16[512,2,640]{2,1,0:T(2,128)(2,1)} %select.1), calls=%async_computation.1 | async-start | bytes 2621440 | tf_op jit(solution)/shard_map/all_to_all | solution.py:331
  49.6 47.5 %copy-start.7 = (f32[2]{0:T(128)S(1)}, f32[2]{0:T(128)}, u32[]{:S(2)}) copy-start(f32[2]{0:T(128)} %param.18) | copy-start | bytes 28
  87.1 10.1 %collective-permute-start.2 = (bf16[512,2,128]{2,1,0:T(2,128)(2,1)S(1)}, bf16[512,2,128]{2,1,0:T(2,128)(2,1)S(1)}, u32[]{:S(2)}, u32[]{:S(2)}) collective-permute-start(bf16[512,2,128]{2,1,0:T(2,128)(2,1)S(1)} %constant_dynamic-slice_fusion), channel_id=1, source_target_pairs={{0,32},{32,0},{1,33},{33,1},{2,34},{34,2},{3,35},{35,3},{4,36},{36... | collective-permute-start | bytes 786440 | tf_op jit(solution)/shard_map/ppermute | solution.py:340
  90.6 13.8 %collective-permute-start.1 = (bf16[256,2,384]{2,1,0:T(2,128)(2,1)S(1)}, bf16[256,2,384]{2,1,0:T(2,128)(2,1)S(1)}, u32[]{:S(2)}, u32[]{:S(2)}) collective-permute-start(bf16[256,2,384]{2,1,0:T(2,128)(2,1)S(1)} %get-tuple-element.9), channel_id=1, source_target_pairs={{0,1},{1,2},{2,3},{3,4},{4,5},{5,6},{6,7},{7,0},{8,9},{9,10},{10,1... | collective-permute-start | bytes 1179656 | tf_op jit(solution)/shard_map/ppermute | solution.py:343
  93.5 11.9 %collective-permute-start = (bf16[256,2,384]{2,1,0:T(2,128)(2,1)S(1)}, bf16[256,2,384]{2,1,0:T(2,128)(2,1)S(1)}, u32[]{:S(2)}, u32[]{:S(2)}) collective-permute-start(bf16[256,2,384]{2,1,0:T(2,128)(2,1)S(1)} %get-tuple-element.10), channel_id=1, source_target_pairs={{1,0},{2,1},{3,2},{4,3},{5,4},{6,5},{7,6},{0,7},{9,8},{10,9},{11,1... | collective-permute-start | bytes 1179656 | tf_op jit(solution)/shard_map/ppermute | solution.py:342

commit v7 on v6

--- a/solution.py
+++ b/solution.py
@@ -203,7 +203,8 @@
         key = entry & (GRID * GRID - 1)
         wave_a = (entry >> 12) & (GRID - 1)
         row = (entry >> 18) * SIDE + ((wave_a + REACH) & (GRID - 1))
-        hit = jnp.where(key_ref[...] == key, 1.0, 0.0).astype(BF16)
+        same = key_ref[...].astype(jnp.int16) == key.astype(jnp.int16)
+        hit = jnp.where(same, jnp.asarray(1, BF16), jnp.asarray(0, BF16))
         found = jnp.dot(spec, hit, preferred_element_type=F32)
         here = side == row
         picked = [
@@ -249,14 +250,14 @@
         move.wait()
 
 
-def own_kernel(mine_ref, third_ref, weight_ref, out_ref, right_ref, res_ref, sems):
+def own_kernel(mine_ref, thirds_ref, weight_ref, out_ref, right_ref, res_ref, sems):
     pairs = right_ref.shape[0]
     half = mine_ref.shape[2] - 2 * TILE
     core = lax.axis_index("core")
     here = pl.ds(pl.multiple_of(core * TILE, TILE), 2 * TILE)
     there = pl.ds(pl.multiple_of((1 - core) * 2 * TILE, TILE), TILE)
     right_ref[:, here] = mine_ref[:, :, half:].reshape(pairs, 2 * TILE)
-    right_ref[:, there] = third_ref[...].reshape(pairs, TILE)
+    right_ref[:, there] = thirds_ref[1 - core].reshape(pairs, TILE)
     left = mine_ref[:, :, :half].reshape(pairs, half)
     half_product(left, right_ref[...], weight_ref, out_ref, res_ref, sems, lax.axis_index("y") % 2)
 
@@ -284,7 +285,7 @@
     )
 
 
-def own_product(mine, third, weights, rows, width):
+def own_product(mine, thirds, weights, rows, width):
     vmem = pl.BlockSpec(memory_space=pltpu.VMEM)
     hbm = pl.BlockSpec(memory_space=pltpu.HBM)
     shapes = (
@@ -292,7 +293,7 @@
         jax.ShapeDtypeStruct((PAIRS, width), BF16),
     )
     call = half_call(own_kernel, "own_half", [vmem] * 3, shapes, (hbm, vmem), rows // 2, width, {})
-    return call(mine, third, weights)
+    return call(mine, thirds, weights)
 
 
 def rest_product(low, high, right, weights, begun):
@@ -334,15 +335,15 @@
     sources = mine.shape[0] // 2
     rows, width = NG // row_count, NG // col_count
     half = rows // 2
-    third = lax.dynamic_slice(
-        mine, (0, 0, half + lax.axis_index("core") * TILE), (2 * sources, 2, TILE)
-    )
-    third = lax.ppermute(third, "core", [(0, 1), (1, 0)])
     count = lax.axis_size("y")
     low = lax.ppermute(mine[:sources, :, :half], "y", [((i + 1) % count, i) for i in range(count)])
     high = lax.ppermute(mine[sources:, :, :half], "y", [(i, (i + 1) % count) for i in range(count)])
+    third = lax.dynamic_slice(
+        mine, (0, 0, half + lax.axis_index("core") * TILE), (2 * sources, 2, TILE)
+    )
+    thirds = lax.all_gather(third, "core")
     weights = pair_weights(val_index, cond_index, val_energy, cond_energy, freqs)
-    begun, right = own_product(mine, third, weights, rows, width)
+    begun, right = own_product(mine, thirds, weights, rows, width)
     return rest_product(low, high, right, weights, begun)
 
 

time: 108 us -> 106 us (0.981)
  blocking collectives: 29.2 us -> 32.5 us
  starting transfers between devices: 21.9 us -> 19 us
  waiting for transfers between devices: 42.9 us -> 41 us
    ppermute x1, waiting for transfers between devices: 4.94 us -> 0.24 us  [shards(): lax.ppermute(mine[sources:, :, :half], 'y', [(i, (i + 1) % count) for i i...]
    all_gather x0 -> x1, blocking collectives: none -> 3.39 us  [shards(): thirds = lax.all_gather(third, 'core')]
    ppermute x1 -> x0, starting transfers between devices: 2.93 us -> none  [shards(): third = lax.ppermute(third, 'core', [(0, 1), (1, 0)])]
    ppermute x1, waiting for transfers between devices: 0.94 us -> 3.76 us  [shards(): lax.ppermute(mine[:sources, :, :half], 'y', [((i + 1) % count, i) for i i...]
  transfers between devices with their start and end apart: 4 -> 3, of which waited for: 3 -> 3; matrix products, arithmetic and copies ran while one was open for 1% -> 0% of each run, Pallas kernels for 2% -> 2%
where the time goes in v7:
time: 106 us; the launch traced here: 105 us
  waiting for transfers between devices  41 us (39%)
  blocking collectives  32.5 us (31%)
  starting transfers between devices  19 us (18%)
  Pallas kernels  11.8 us (11%)
    all_to_all x1, waiting for transfers between devices, shards(): lax.all_to_all(select(block, gmap, row_count), ROW + COL, split_axis=0, c...  37 us
    all_to_all x1, blocking collectives, shards(): lax.all_to_all(partial.reshape(col_count, 8, COLS), COL, split_axis=0, co...  29.2 us
    all_to_all x1, starting transfers between devices, shards(): lax.all_to_all(select(block, gmap, row_count), ROW + COL, split_axis=0, c...  12.5 us
    pallas_call x1, Pallas kernels, select(): pl.pallas_call(select_kernel, out_shape=jax.ShapeDtypeStruct((2 * rows *...  3.95 us
    ppermute x1, starting transfers between devices, shards(): lax.ppermute(mine[sources:, :, :half], 'y', [(i, (i + 1) % count) for i i...  3.89 us
    ppermute x1, waiting for transfers between devices, shards(): lax.ppermute(mine[:sources, :, :half], 'y', [((i + 1) % count, i) for i i...  3.76 us
    pallas_call x1, Pallas kernels, transform(): pl.pallas_call(transform_kernel, out_shape=jax.ShapeDtypeStruct((4 * pair...  3.62 us
    all_gather x1, blocking collectives, shards(): thirds = lax.all_gather(third, 'core')  3.39 us
  transfers between devices with their start and end apart: 3, of which 3 were waited for; matrix products, arithmetic and copies ran while one was open for 0% of the time, Pallas kernels for 2%

profile of v7, /device:TPU:1, one launch (start us, length us, event | category | flops | bytes accessed | tf_op | source)
XLA Modules:
  0.0 105.5 jit_solution(1803229082967121389)
XLA Ops:
  0.0 3.6 %transform.1 = bf16[256,512]{1,0:T(8,128)(2,1)} custom-call(bf16[48,2,4096]{2,1,0:T(2,128)(2,1)} %val_hbm.1, bf16[64,2,4096]{2,1,0:T(2,128)(2,1)} %cond_hbm.1, s32[1024]{0:T(1024)} %vi_hbm.1, s32[1024]{0:T(1024)} %ci_hbm.1, f32[2,128,128]{2,1,0:T(8,128)} %constant.33.yq_hbm, bf16[144,256]{1,0:T(8,128)(2,1)} %constant.28.clone.zt_hbm), custom_call_target="tpu_custom_call" | custom-call | tf_op jit(solution)/shard_map/transform/pallas_call | solution.py:173
  3.6 29.2 %all_to_all.10 = bf16[32,8,512]{2,1,0:T(8,128)(2,1)S(1)} all-to-all(bf16[32,8,512]{2,1,0:T(8,128)(2,1)} %bitcast.7), channel_id=1, replica_groups=mesh['x'=4,'z_lo'=2,'core'=2,'z_hi'=4,'y'=8] {'z_hi','y'}, dimensions={0} | all-to-all | bytes 524288 | tf_op jit(solution)/shard_map/all_to_all | solution.py:329
  32.8 0.0 copy-done
  32.8 0.0 copy-done.1
  32.8 0.0 copy-done.2
  32.8 4.0 %select.1 = bf16[512,2,640]{2,1,0:T(2,128)(2,1)} custom-call(bf16[256,512]{1,0:T(8,128)(2,1)S(1)} %bitcast.4, bf16[160,256]{1,0:T(8,128)(2,1)S(1)} %copy-done.1, s32[512,1]{1,0:T(8,128)S(1)} %copy-done, s32[16,1,768]{2,1,0:T(1,128)S(1)} %bitcast.6), custom_call_target="tpu_custom_call" | custom-call | tf_op jit(solution)/shard_map/select/pallas_call | solution.py:228
  36.8 0.0 copy-start.6
  36.8 12.5 %all-to-all-start.1 = ((bf16[512,2,640]{2,1,0:T(2,128)(2,1)}), bf16[512,2,640]{2,1,0:T(2,128)(2,1)S(1)}, u32[]{:S(2)}, u32[]{:S(2)}) async-start(bf16[512,2,640]{2,1,0:T(2,128)(2,1)} %select.1), calls=%async_computation.1 | async-start | bytes 2621440 | tf_op jit(solution)/shard_map/all_to_all | solution.py:332
  49.3 0.0 copy-done.7
  49.3 0.0 copy-done.3
  49.3 0.0 copy-done.5
  49.3 0.1 select_reduce_fusion.1
  49.5 0.1 select_reduce_fusion
  49.6 37.0 %all-to-all-done.1.mine_ref = bf16[512,2,640]{2,1,0:T(2,128)(2,1)S(1)} async-done(((bf16[512,2,640]{2,1,0:T(2,128)(2,1)}), bf16[512,2,640]{2,1,0:T(2,128)(2,1)S(1)}, u32[]{:S(2)}, u32[]{:S(2)}) %all-to-all-start.1) | async-done | bytes 1310752 | tf_op jit(solution)/shard_map/all_to_all | solution.py:332
  86.6 0.5 fusion
  87.1 3.9 %collective-permute-start.1 = (bf16[256,2,384]{2,1,0:T(2,128)(2,1)S(1)}, bf16[256,2,384]{2,1,0:T(2,128)(2,1)S(1)}, u32[]{:S(2)}, u32[]{:S(2)}) collective-permute-start(bf16[256,2,384]{2,1,0:T(2,128)(2,1)S(1)} %get-tuple-element.9), channel_id=1, source_target_pairs={{0,1},{1,2},{2,3},{3,4},{4,5},{5,6},{6,7},{7,0},{8,9},{9,10},{10,1... | collective-permute-start | bytes 1179656 | tf_op jit(solution)/shard_map/ppermute | solution.py:340
  91.0 2.6 %collective-permute-start = (bf16[256,2,384]{2,1,0:T(2,128)(2,1)S(1)}, bf16[256,2,384]{2,1,0:T(2,128)(2,1)S(1)}, u32[]{:S(2)}, u32[]{:S(2)}) collective-permute-start(bf16[256,2,384]{2,1,0:T(2,128)(2,1)S(1)} %get-tuple-element.10), channel_id=1, source_target_pairs={{1,0},{2,1},{3,2},{4,3},{5,4},{6,5},{7,6},{0,7},{9,8},{10,9},{11,1... | collective-permute-start | bytes 1179656 | tf_op jit(solution)/shard_map/ppermute | solution.py:339
  93.6 0.1 add_divide_fusion.weight_ref
  93.7 0.2 constant_dynamic-slice_fusion
  93.9 3.4 %all-gather = bf16[1024,2,128]{2,1,0:T(2,128)(2,1)S(1)} all-gather(bf16[512,2,128]{2,1,0:T(2,128)(2,1)S(1)} %constant_dynamic-slice_fusion), channel_id=2, replica_groups=mesh['x'=4,'z_lo'=2,'core'=2,'z_hi'=4,'y'=8] {'core'}, dimensions={0}, use_global_device_ids=true | all-gather | bytes 786432 | tf_op jit(solution)/shard_map/all_gather | solution.py:344
  97.3 2.3 %own_half.1 = (f32[2,768,384]{2,1,0:T(8,128)}, bf16[1024,384]{1,0:T(8,128)(2,1)S(1)}) custom-call(bf16[512,2,640]{2,1,0:T(2,128)(2,1)S(1)} %all-to-all-done.1.mine_ref, bf16[2,512,2,128]{3,2,1,0:T(2,128)(2,1)S(1)} %bitcast.5, f32[2,1024]{1,0:T(2,128)S(1)} %add_divide_fusion.weight_ref), custom_call_target="tpu_custom_call" | custom-call | flops 603979776 | bytes 5242880 | tf_op jit(solution)/shard_map/own_half/pallas_call | solution.py:296
  99.6 0.2 collective-permute-done.1.high_ref
  99.8 3.8 %collective-permute-done.low_ref = bf16[256,2,384]{2,1,0:T(2,128)(2,1)S(1)} collective-permute-done((bf16[256,2,384]{2,1,0:T(2,128)(2,1)S(1)}, bf16[256,2,384]{2,1,0:T(2,128)(2,1)S(1)}, u32[]{:S(2)}, u32[]{:S(2)}) %collective-permute-start) | collective-permute-done | bytes 393248 | tf_op jit(solution)/shard_map/ppermute | solution.py:339
  103.6 1.9 %other_half.1 = f32[2,768,384]{2,1,0:T(8,128)} custom-call(bf16[256,2,384]{2,1,0:T(2,128)(2,1)S(1)} %collective-permute-done.low_ref, bf16[256,2,384]{2,1,0:T(2,128)(2,1)S(1)} %collective-permute-done.1.high_ref, bf16[1024,384]{1,0:T(8,128)(2,1)S(1)} %get-tuple-element.7.right_ref, ...), custom_call_target="tpu_custom_call", output_to_operand_aliasing={{}: (4, {})} | custom-call | flops 603979776 | bytes 5242880 | tf_op jit(solution)/shard_map/other_half/pallas_call | solution.py:306
  (11 shorter events, 0.0 us)
Async XLA Ops:
  0.0 32.8 %copy-start = (s32[512,1]{1,0:T(8,128)S(1)}, s32[512,1]{1,0:T(8,128)}, u32[]{:S(2)}) copy-start(s32[512,1]{1,0:T(8,128)} %constant.30.clone.key_ref) | copy-start | bytes 6148
  0.0 32.8 %copy-start.1 = (bf16[160,256]{1,0:T(8,128)(2,1)S(1)}, bf16[160,256]{1,0:T(8,128)(2,1)}, u32[]{:S(2)}) copy-start(bf16[160,256]{1,0:T(8,128)(2,1)} %constant.29.clone.xt_ref) | copy-start | bytes 245764
  0.0 32.8 %copy-start.2 = (s32[12288]{0:T(1024)S(1)}, s32[12288]{0:T(1024)}, u32[]{:S(2)}) copy-start(s32[12288]{0:T(1024)} %param.19) | copy-start | bytes 147460
  36.8 12.5 %copy-start.7 = (f32[2]{0:T(128)S(1)}, f32[2]{0:T(128)}, u32[]{:S(2)}) copy-start(f32[2]{0:T(128)} %param.18) | copy-start | bytes 28
  36.8 12.6 %copy-start.3 = (s32[1024]{0:T(1024)S(1)}, s32[1024]{0:T(1024)}, u32[]{:S(2)}) copy-start(s32[1024]{0:T(1024)} %vi_hbm.1) | copy-start | bytes 12292
  36.8 12.6 %copy-start.5 = (f32[48]{0:T(128)S(1)}, f32[48]{0:T(128)}, u32[]{:S(2)}) copy-start(f32[48]{0:T(128)} %param.16) | copy-start | bytes 580
  36.8 12.7 %copy-start.4 = (s32[1024]{0:T(1024)S(1)}, s32[1024]{0:T(1024)}, u32[]{:S(2)}) copy-start(s32[1024]{0:T(1024)} %ci_hbm.1) | copy-start | bytes 12292
  36.8 12.7 %copy-start.6 = (f32[64]{0:T(128)S(1)}, f32[64]{0:T(128)}, u32[]{:S(2)}) copy-start(f32[64]{0:T(128)} %param.17) | copy-start | bytes 772
  36.8 49.8 %all-to-all-start.1 = ((bf16[512,2,640]{2,1,0:T(2,128)(2,1)}), bf16[512,2,640]{2,1,0:T(2,128)(2,1)S(1)}, u32[]{:S(2)}, u32[]{:S(2)}) async-start(bf16[512,2,640]{2,1,0:T(2,128)(2,1)} %select.1), calls=%async_computation.1 | async-start | bytes 2621440 | tf_op jit(solution)/shard_map/all_to_all | solution.py:332
  87.1 12.7 %collective-permute-start.1 = (bf16[256,2,384]{2,1,0:T(2,128)(2,1)S(1)}, bf16[256,2,384]{2,1,0:T(2,128)(2,1)S(1)}, u32[]{:S(2)}, u32[]{:S(2)}) collective-permute-start(bf16[256,2,384]{2,1,0:T(2,128)(2,1)S(1)} %get-tuple-element.9), channel_id=1, source_target_pairs={{0,1},{1,2},{2,3},{3,4},{4,5},{5,6},{6,7},{7,0},{8,9},{9,10},{10,1... | collective-permute-start | bytes 1179656 | tf_op jit(solution)/shard_map/ppermute | solution.py:340
  91.0 12.6 %collective-permute-start = (bf16[256,2,384]{2,1,0:T(2,128)(2,1)S(1)}, bf16[256,2,384]{2,1,0:T(2,128)(2,1)S(1)}, u32[]{:S(2)}, u32[]{:S(2)}) collective-permute-start(bf16[256,2,384]{2,1,0:T(2,128)(2,1)S(1)} %get-tuple-element.10), channel_id=1, source_target_pairs={{1,0},{2,1},{3,2},{4,3},{5,4},{6,5},{7,6},{0,7},{9,8},{10,9},{11,1... | collective-permute-start | bytes 1179656 | tf_op jit(solution)/shard_map/ppermute | solution.py:339

commit v8 on v7

--- a/solution.py
+++ b/solution.py
@@ -218,8 +218,10 @@
         for which in range(2):
             col = 2 * r + which
             for other in range(rows):
-                start = other % 2 * TILE
-                out_ref[other * 2 * rows + col, :, half:] = halves[which][:, start : start + 2 * TILE]
+                third = other % 2 if other // 2 % 2 == 0 else 2
+                out_ref[other * 2 * rows + col, :, half:] = halves[which][
+                    :, third * TILE : (third + 1) * TILE
+                ]
 
 
 def select(block, gmap, rows):
@@ -227,7 +229,7 @@
     vmem = pl.BlockSpec(memory_space=pltpu.VMEM)
     return pl.pallas_call(
         select_kernel,
-        out_shape=jax.ShapeDtypeStruct((2 * rows * rows, 2, width // 2 + 2 * TILE), BF16),
+        out_shape=jax.ShapeDtypeStruct((2 * rows * rows, 2, width // 2 + TILE), BF16),
         in_specs=[vmem] * 4,
         out_specs=vmem,
         compiler_params=pltpu.CompilerParams(vmem_limit_bytes=32 * 2**20),
@@ -250,14 +252,11 @@
         move.wait()
 
 
-def own_kernel(mine_ref, thirds_ref, weight_ref, out_ref, right_ref, res_ref, sems):
+def own_kernel(mine_ref, zs_ref, cores_ref, weight_ref, out_ref, right_ref, res_ref, sems):
     pairs = right_ref.shape[0]
-    half = mine_ref.shape[2] - 2 * TILE
-    core = lax.axis_index("core")
-    here = pl.ds(pl.multiple_of(core * TILE, TILE), 2 * TILE)
-    there = pl.ds(pl.multiple_of((1 - core) * 2 * TILE, TILE), TILE)
-    right_ref[:, here] = mine_ref[:, :, half:].reshape(pairs, 2 * TILE)
-    right_ref[:, there] = thirds_ref[1 - core].reshape(pairs, TILE)
+    half = mine_ref.shape[2] - TILE
+    for third, value in enumerate((cores_ref[0], cores_ref[1], zs_ref[1])):
+        right_ref[:, third * TILE : (third + 1) * TILE] = value.reshape(pairs, TILE)
     left = mine_ref[:, :, :half].reshape(pairs, half)
     half_product(left, right_ref[...], weight_ref, out_ref, res_ref, sems, lax.axis_index("y") % 2)
 
@@ -285,15 +284,15 @@
     )
 
 
-def own_product(mine, thirds, weights, rows, width):
+def own_product(mine, by_z, by_core, weights, rows, width):
     vmem = pl.BlockSpec(memory_space=pltpu.VMEM)
     hbm = pl.BlockSpec(memory_space=pltpu.HBM)
     shapes = (
         jax.ShapeDtypeStruct((weights.shape[0], rows, width), F32),
         jax.ShapeDtypeStruct((PAIRS, width), BF16),
     )
-    call = half_call(own_kernel, "own_half", [vmem] * 3, shapes, (hbm, vmem), rows // 2, width, {})
-    return call(mine, thirds, weights)
+    call = half_call(own_kernel, "own_half", [vmem] * 4, shapes, (hbm, vmem), rows // 2, width, {})
+    return call(mine, by_z, by_core, weights)
 
 
 def rest_product(low, high, right, weights, begun):
@@ -338,12 +337,10 @@
     count = lax.axis_size("y")
     low = lax.ppermute(mine[:sources, :, :half], "y", [((i + 1) % count, i) for i in range(count)])
     high = lax.ppermute(mine[sources:, :, :half], "y", [(i, (i + 1) % count) for i in range(count)])
-    third = lax.dynamic_slice(
-        mine, (0, 0, half + lax.axis_index("core") * TILE), (2 * sources, 2, TILE)
-    )
-    thirds = lax.all_gather(third, "core")
+    by_z = lax.all_gather(mine[:, :, half:], "z_lo")
+    by_core = lax.all_gather(by_z[0], "core")
     weights = pair_weights(val_index, cond_index, val_energy, cond_energy, freqs)
-    begun, right = own_product(mine, thirds, weights, rows, width)
+    begun, right = own_product(mine, by_z, by_core, weights, rows, width)
     return rest_product(low, high, right, weights, begun)
 
 

time: 106 us -> 104 us (0.981)
  waiting for transfers between devices: 41 us -> 31.4 us
  blocking collectives: 32.5 us -> 40.6 us
    all_gather x1 -> x2, blocking collectives: 3.39 us -> 11.3 us  [the longest x1 6.67 us: shards(): by_z = lax.all_gather(mine[:, :, half:], 'z_lo')]
    all_to_all x1, waiting for transfers between devices: 37 us -> 31.4 us  [shards(): lax.all_to_all(select(block, gmap, row_count), ROW + COL, split_axis=0, c...]
    ppermute x1, waiting for transfers between devices: 3.76 us -> 0.01 us  [shards(): lax.ppermute(mine[:sources, :, :half], 'y', [((i + 1) % count, i) for i i...]
  transfers between devices with their start and end apart: 3 -> 3, of which waited for: 3 -> 1; matrix products, arithmetic and copies ran while one was open for 0% -> 1% of each run, Pallas kernels for 2% -> 2%
where the time goes in v8:
time: 104 us
  blocking collectives  40.6 us (39%)
  waiting for transfers between devices  31.4 us (30%)
  starting transfers between devices  19 us (18%)
  Pallas kernels  11.6 us (11%)
    all_to_all x1, waiting for transfers between devices, shards(): lax.all_to_all(select(block, gmap, row_count), ROW + COL, split_axis=0, c...  31.4 us
    all_to_all x1, blocking collectives, shards(): lax.all_to_all(partial.reshape(col_count, 8, COLS), COL, split_axis=0, co...  29.3 us
    all_to_all x1, starting transfers between devices, shards(): lax.all_to_all(select(block, gmap, row_count), ROW + COL, split_axis=0, c...  12.5 us
    all_gather x1, blocking collectives, shards(): by_z = lax.all_gather(mine[:, :, half:], 'z_lo')  6.67 us
    all_gather x1, blocking collectives, shards(): by_core = lax.all_gather(by_z[0], 'core')  4.62 us
    ppermute x1, starting transfers between devices, shards(): lax.ppermute(mine[sources:, :, :half], 'y', [(i, (i + 1) % count) for i i...  4.15 us
    pallas_call x1, Pallas kernels, select(): pl.pallas_call(select_kernel, out_shape=jax.ShapeDtypeStruct((2 * rows *...  3.83 us
    pallas_call x1, Pallas kernels, transform(): pl.pallas_call(transform_kernel, out_shape=jax.ShapeDtypeStruct((4 * pair...  3.62 us
  transfers between devices with their start and end apart: 3, of which 1 were waited for; matrix products, arithmetic and copies ran while one was open for 1% of the time, Pallas kernels for 2%

profile of v8, /device:TPU:1, one launch (start us, length us, event | category | flops | bytes accessed | tf_op | source)
XLA Modules:
  0.0 104.1 jit_solution(3801321568888864819)
XLA Ops:
  0.0 3.6 %transform.1 = bf16[256,512]{1,0:T(8,128)(2,1)} custom-call(bf16[48,2,4096]{2,1,0:T(2,128)(2,1)} %val_hbm.1, bf16[64,2,4096]{2,1,0:T(2,128)(2,1)} %cond_hbm.1, s32[1024]{0:T(1024)} %vi_hbm.1, s32[1024]{0:T(1024)} %ci_hbm.1, f32[2,128,128]{2,1,0:T(8,128)} %constant.18.yq_hbm, bf16[144,256]{1,0:T(8,128)(2,1)} %constant.13.clone.zt_hbm), custom_call_target="tpu_custom_call" | custom-call | tf_op jit(solution)/shard_map/transform/pallas_call | solution.py:173
  3.6 0.0 copy-start.7
  3.6 0.0 copy-start.3
  3.7 0.0 copy-start.5
  3.7 0.0 copy-start.4
  3.7 0.0 copy-start.6
  3.7 29.3 %all_to_all.10 = bf16[32,8,512]{2,1,0:T(8,128)(2,1)S(1)} all-to-all(bf16[32,8,512]{2,1,0:T(8,128)(2,1)} %bitcast.9), channel_id=1, replica_groups=mesh['x'=4,'z_lo'=2,'core'=2,'z_hi'=4,'y'=8] {'z_hi','y'}, dimensions={0} | all-to-all | bytes 524288 | tf_op jit(solution)/shard_map/all_to_all | solution.py:328
  33.0 3.8 %select.1 = bf16[512,2,512]{2,1,0:T(2,128)(2,1)} custom-call(bf16[256,512]{1,0:T(8,128)(2,1)S(1)} %bitcast.6, bf16[160,256]{1,0:T(8,128)(2,1)S(1)} %copy-done.1, s32[512,1]{1,0:T(8,128)S(1)} %copy-done, s32[16,1,768]{2,1,0:T(1,128)S(1)} %bitcast.8), custom_call_target="tpu_custom_call" | custom-call | tf_op jit(solution)/shard_map/select/pallas_call | solution.py:230
  36.8 12.5 %all-to-all-start.1 = ((bf16[512,2,512]{2,1,0:T(2,128)(2,1)}), bf16[512,2,512]{2,1,0:T(2,128)(2,1)S(1)}, u32[]{:S(2)}, u32[]{:S(2)}) async-start(bf16[512,2,512]{2,1,0:T(2,128)(2,1)} %select.1), calls=%async_computation.1 | async-start | bytes 2097152 | tf_op jit(solution)/shard_map/all_to_all | solution.py:331
  49.4 0.1 select_reduce_fusion.1
  49.5 0.1 select_reduce_fusion
  49.6 31.4 %all-to-all-done.1.mine_ref = bf16[512,2,512]{2,1,0:T(2,128)(2,1)S(1)} async-done(((bf16[512,2,512]{2,1,0:T(2,128)(2,1)}), bf16[512,2,512]{2,1,0:T(2,128)(2,1)S(1)}, u32[]{:S(2)}, u32[]{:S(2)}) %all-to-all-start.1) | async-done | bytes 1048608 | tf_op jit(solution)/shard_map/all_to_all | solution.py:331
  81.1 0.5 fusion
  81.6 4.1 %collective-permute-start.1 = (bf16[256,2,384]{2,1,0:T(2,128)(2,1)S(1)}, bf16[256,2,384]{2,1,0:T(2,128)(2,1)S(1)}, u32[]{:S(2)}, u32[]{:S(2)}) collective-permute-start(bf16[256,2,384]{2,1,0:T(2,128)(2,1)S(1)} %get-tuple-element.9), channel_id=1, source_target_pairs={{0,1},{1,2},{2,3},{3,4},{4,5},{5,6},{6,7},{7,0},{8,9},{9,10},{10,1... | collective-permute-start | bytes 1179656 | tf_op jit(solution)/shard_map/ppermute | solution.py:339
  85.8 2.3 %collective-permute-start = (bf16[256,2,384]{2,1,0:T(2,128)(2,1)S(1)}, bf16[256,2,384]{2,1,0:T(2,128)(2,1)S(1)}, u32[]{:S(2)}, u32[]{:S(2)}) collective-permute-start(bf16[256,2,384]{2,1,0:T(2,128)(2,1)S(1)} %get-tuple-element.10), channel_id=1, source_target_pairs={{1,0},{2,1},{3,2},{4,3},{5,4},{6,5},{7,6},{0,7},{9,8},{10,9},{11,1... | collective-permute-start | bytes 1179656 | tf_op jit(solution)/shard_map/ppermute | solution.py:338
  88.1 0.1 add_divide_fusion.weight_ref
  88.2 0.2 slice.19
  88.4 6.7 %all-gather = bf16[1024,2,128]{2,1,0:T(2,128)(2,1)S(1)} all-gather(bf16[512,2,128]{2,1,0:T(2,128)(2,1)S(1)} %slice.19), channel_id=2, replica_groups=mesh['x'=4,'z_lo'=2,'core'=2,'z_hi'=4,'y'=8] {'z_lo'}, dimensions={0}, use_global_device_ids=true | all-gather | bytes 786432 | tf_op jit(solution)/shard_map/all_gather | solution.py:340
  95.1 0.2 slice.20
  95.2 4.6 %all-gather.1 = bf16[1024,2,128]{2,1,0:T(2,128)(2,1)S(1)} all-gather(bf16[512,2,128]{2,1,0:T(2,128)(2,1)S(1)} %slice.20), channel_id=3, replica_groups=mesh['x'=4,'z_lo'=2,'core'=2,'z_hi'=4,'y'=8] {'core'}, dimensions={0}, use_global_device_ids=true | all-gather | bytes 786432 | tf_op jit(solution)/shard_map/all_gather | solution.py:341
  99.9 2.2 %own_half.1 = (f32[2,768,384]{2,1,0:T(8,128)}, bf16[1024,384]{1,0:T(8,128)(2,1)S(1)}) custom-call(bf16[512,2,512]{2,1,0:T(2,128)(2,1)S(1)} %all-to-all-done.1.mine_ref, bf16[2,512,2,128]{3,2,1,0:T(2,128)(2,1)S(1)} %bitcast.5, bf16[2,512,2,128]{3,2,1,0:T(2,128)(2,1)S(1)} %bitcast.7, f32[2,1024]{1,0:T(2,128)S(1)} %add_divide_fusion.weight_ref), custom_call_target="tpu_custom_call" | custom-call | flops 603979776 | bytes 5242880 | tf_op jit(solution)/shard_map/own_half/pallas_call | solution.py:295
  102.1 0.0 collective-permute-done.1.high_ref
  102.1 0.0 collective-permute-done.low_ref
  102.1 1.9 %other_half.1 = f32[2,768,384]{2,1,0:T(8,128)} custom-call(bf16[256,2,384]{2,1,0:T(2,128)(2,1)S(1)} %collective-permute-done.low_ref, bf16[256,2,384]{2,1,0:T(2,128)(2,1)S(1)} %collective-permute-done.1.high_ref, bf16[1024,384]{1,0:T(8,128)(2,1)S(1)} %get-tuple-element.7.right_ref, ...), custom_call_target="tpu_custom_call", output_to_operand_aliasing={{}: (4, {})} | custom-call | flops 603979776 | bytes 5242880 | tf_op jit(solution)/shard_map/other_half/pallas_call | solution.py:305
  (13 shorter events, 0.0 us)
Async XLA Ops:
  0.0 33.0 %copy-start = (s32[512,1]{1,0:T(8,128)S(1)}, s32[512,1]{1,0:T(8,128)}, u32[]{:S(2)}) copy-start(s32[512,1]{1,0:T(8,128)} %constant.15.clone.key_ref) | copy-start | bytes 6148
  0.0 33.0 %copy-start.1 = (bf16[160,256]{1,0:T(8,128)(2,1)S(1)}, bf16[160,256]{1,0:T(8,128)(2,1)}, u32[]{:S(2)}) copy-start(bf16[160,256]{1,0:T(8,128)(2,1)} %constant.14.clone.xt_ref) | copy-start | bytes 245764
  0.0 33.0 %copy-start.2 = (s32[12288]{0:T(1024)S(1)}, s32[12288]{0:T(1024)}, u32[]{:S(2)}) copy-start(s32[12288]{0:T(1024)} %param.19) | copy-start | bytes 147460
  3.6 45.7 %copy-start.7 = (f32[2]{0:T(128)S(1)}, f32[2]{0:T(128)}, u32[]{:S(2)}) copy-start(f32[2]{0:T(128)} %param.18) | copy-start | bytes 28
  3.6 45.7 %copy-start.3 = (s32[1024]{0:T(1024)S(1)}, s32[1024]{0:T(1024)}, u32[]{:S(2)}) copy-start(s32[1024]{0:T(1024)} %vi_hbm.1) | copy-start | bytes 12292
  3.7 45.7 %copy-start.5 = (f32[48]{0:T(128)S(1)}, f32[48]{0:T(128)}, u32[]{:S(2)}) copy-start(f32[48]{0:T(128)} %param.16) | copy-start | bytes 580
  3.7 45.8 %copy-start.4 = (s32[1024]{0:T(1024)S(1)}, s32[1024]{0:T(1024)}, u32[]{:S(2)}) copy-start(s32[1024]{0:T(1024)} %ci_hbm.1) | copy-start | bytes 12292
  3.7 45.8 %copy-start.6 = (f32[64]{0:T(128)S(1)}, f32[64]{0:T(128)}, u32[]{:S(2)}) copy-start(f32[64]{0:T(128)} %param.17) | copy-start | bytes 772
  36.8 44.2 %all-to-all-start.1 = ((bf16[512,2,512]{2,1,0:T(2,128)(2,1)}), bf16[512,2,512]{2,1,0:T(2,128)(2,1)S(1)}, u32[]{:S(2)}, u32[]{:S(2)}) async-start(bf16[512,2,512]{2,1,0:T(2,128)(2,1)} %select.1), calls=%async_computation.1 | async-start | bytes 2097152 | tf_op jit(solution)/shard_map/all_to_all | solution.py:331
  81.6 20.5 %collective-permute-start.1 = (bf16[256,2,384]{2,1,0:T(2,128)(2,1)S(1)}, bf16[256,2,384]{2,1,0:T(2,128)(2,1)S(1)}, u32[]{:S(2)}, u32[]{:S(2)}) collective-permute-start(bf16[256,2,384]{2,1,0:T(2,128)(2,1)S(1)} %get-tuple-element.9), channel_id=1, source_target_pairs={{0,1},{1,2},{2,3},{3,4},{4,5},{5,6},{6,7},{7,0},{8,9},{9,10},{10,1... | collective-permute-start | bytes 1179656 | tf_op jit(solution)/shard_map/ppermute | solution.py:339
  85.8 16.4 %collective-permute-start = (bf16[256,2,384]{2,1,0:T(2,128)(2,1)S(1)}, bf16[256,2,384]{2,1,0:T(2,128)(2,1)S(1)}, u32[]{:S(2)}, u32[]{:S(2)}) collective-permute-start(bf16[256,2,384]{2,1,0:T(2,128)(2,1)S(1)} %get-tuple-element.10), channel_id=1, source_target_pairs={{1,0},{2,1},{3,2},{4,3},{5,4},{6,5},{7,6},{0,7},{9,8},{10,9},{11,1... | collective-permute-start | bytes 1179656 | tf_op jit(solution)/shard_map/ppermute | solution.py:338

commit v9 on v8

--- a/solution.py
+++ b/solution.py
@@ -237,72 +237,55 @@
     )(block, jnp.asarray(x_constant(), BF16), jnp.asarray(column_keys()), gmap.reshape(rows, 1, width))
 
 
-def half_product(left, right, weight_ref, out_ref, res_ref, sems, half):
-    pairs, rows = left.shape
-    turned = left.T.astype(F32)
-    place = pl.ds(pl.multiple_of(half * rows, rows), rows)
+def product_kernel(
+    mine_ref, low_ref, high_ref, zs_ref, cores_ref, weight_ref, out_ref, right_ref, res_ref, sems
+):
+    pairs = right_ref.shape[0]
+    half = mine_ref.shape[2] - TILE
+    freqs = weight_ref.shape[0]
+    for third, value in enumerate((cores_ref[0], cores_ref[1], zs_ref[1])):
+        right_ref[:, third * TILE : (third + 1) * TILE] = value.reshape(pairs, TILE)
+    right = right_ref[...]
+    own = lax.axis_index("y") % 2
     moves = []
-    for f in range(weight_ref.shape[0]):
-        weighted = (turned * weight_ref[f : f + 1, :]).astype(BF16)
-        total = jnp.dot(weighted, right, preferred_element_type=F32)
-        res_ref[f] = total * (1.0 / math.sqrt(pairs))
-        moves.append(pltpu.make_async_copy(res_ref.at[f], out_ref.at[f, place], sems.at[f]))
-        moves[-1].start()
+    for step in range(2):
+        if step == 0:
+            left = mine_ref[:, :, :half].reshape(pairs, half)
+        else:
+            part = (pairs // 2, half)
+            left = jnp.concatenate([low_ref[...].reshape(part), high_ref[...].reshape(part)], 0)
+        place = own if step == 0 else 1 - own
+        place = pl.ds(pl.multiple_of(place * half, half), half)
+        turned = left.T.astype(F32)
+        for f in range(freqs):
+            weighted = (turned * weight_ref[f : f + 1, :]).astype(BF16)
+            total = jnp.dot(weighted, right, preferred_element_type=F32)
+            res_ref[step, f] = total * (1.0 / math.sqrt(pairs))
+            moves.append(
+                pltpu.make_async_copy(
+                    res_ref.at[step, f], out_ref.at[f, place], sems.at[step * freqs + f]
+                )
+            )
+            moves[-1].start()
     for move in moves:
         move.wait()
 
 
-def own_kernel(mine_ref, zs_ref, cores_ref, weight_ref, out_ref, right_ref, res_ref, sems):
-    pairs = right_ref.shape[0]
-    half = mine_ref.shape[2] - TILE
-    for third, value in enumerate((cores_ref[0], cores_ref[1], zs_ref[1])):
-        right_ref[:, third * TILE : (third + 1) * TILE] = value.reshape(pairs, TILE)
-    left = mine_ref[:, :, :half].reshape(pairs, half)
-    half_product(left, right_ref[...], weight_ref, out_ref, res_ref, sems, lax.axis_index("y") % 2)
-
-
-def rest_kernel(low_ref, high_ref, right_ref, weight_ref, begun_ref, out_ref, res_ref, sems):
-    part, _, half = low_ref.shape
-    left = jnp.concatenate(
-        [low_ref[...].reshape(2 * part, half), high_ref[...].reshape(2 * part, half)], 0
-    )
-    half_product(left, right_ref[...], weight_ref, out_ref, res_ref, sems, 1 - lax.axis_index("y") % 2)
-
-
-def half_call(kernel, name, in_specs, out_shape, out_specs, half, width, aliases):
-    work = 2 * 2 * PAIRS * half * width
+def product(mine, low, high, by_z, by_core, weights, rows, width):
+    freqs = weights.shape[0]
     return pl.pallas_call(
-        kernel,
-        out_shape=out_shape,
-        in_specs=in_specs,
-        out_specs=out_specs,
-        scratch_shapes=[pltpu.VMEM((2, half, width), F32), pltpu.SemaphoreType.DMA((2,))],
-        input_output_aliases=aliases,
-        cost_estimate=pl.CostEstimate(flops=work, bytes_accessed=5 * 2**20, transcendentals=0),
+        product_kernel,
+        out_shape=jax.ShapeDtypeStruct((freqs, rows, width), F32),
+        in_specs=[pl.BlockSpec(memory_space=pltpu.VMEM)] * 6,
+        out_specs=pl.BlockSpec(memory_space=pltpu.HBM),
+        scratch_shapes=[
+            pltpu.VMEM((PAIRS, width), BF16),
+            pltpu.VMEM((2, freqs, rows // 2, width), F32),
+            pltpu.SemaphoreType.DMA((2 * freqs,)),
+        ],
         compiler_params=pltpu.CompilerParams(vmem_limit_bytes=32 * 2**20),
-        name=name,
-    )
-
-
-def own_product(mine, by_z, by_core, weights, rows, width):
-    vmem = pl.BlockSpec(memory_space=pltpu.VMEM)
-    hbm = pl.BlockSpec(memory_space=pltpu.HBM)
-    shapes = (
-        jax.ShapeDtypeStruct((weights.shape[0], rows, width), F32),
-        jax.ShapeDtypeStruct((PAIRS, width), BF16),
-    )
-    call = half_call(own_kernel, "own_half", [vmem] * 4, shapes, (hbm, vmem), rows // 2, width, {})
-    return call(mine, by_z, by_core, weights)
-
-
-def rest_product(low, high, right, weights, begun):
-    vmem = pl.BlockSpec(memory_space=pltpu.VMEM)
-    hbm = pl.BlockSpec(memory_space=pltpu.HBM)
-    _, rows, width = begun.shape
-    shape = jax.ShapeDtypeStruct(begun.shape, F32)
-    specs = [vmem] * 4 + [hbm]
-    call = half_call(rest_kernel, "other_half", specs, shape, hbm, rows // 2, width, {4: 0})
-    return call(low, high, right, weights, begun)
+        name="product",
+    )(mine, low, high, by_z, by_core, weights)
 
 
 def pair_weights(val_index, cond_index, val_energy, cond_energy, freqs):
@@ -331,6 +314,8 @@
     mine = lax.all_to_all(
         select(block, gmap, row_count), ROW + COL, split_axis=0, concat_axis=0, tiled=True
     )
+    weights = pair_weights(val_index, cond_index, val_energy, cond_energy, freqs)
+    mine, weights = lax.optimization_barrier((mine, weights))
     sources = mine.shape[0] // 2
     rows, width = NG // row_count, NG // col_count
     half = rows // 2
@@ -339,9 +324,7 @@
     high = lax.ppermute(mine[sources:, :, :half], "y", [(i, (i + 1) % count) for i in range(count)])
     by_z = lax.all_gather(mine[:, :, half:], "z_lo")
     by_core = lax.all_gather(by_z[0], "core")
-    weights = pair_weights(val_index, cond_index, val_energy, cond_energy, freqs)
-    begun, right = own_product(mine, by_z, by_core, weights, rows, width)
-    return rest_product(low, high, right, weights, begun)
+    return product(mine, low, high, by_z, by_core, weights, rows, width)
 
 
 def solution(mesh):

time: 104 us -> 103 us (level)
  Pallas kernels: 11.6 us -> 10.5 us
    pallas_call x2 -> x1, Pallas kernels: 4.15 us -> 3.05 us  [product(): pl.pallas_call(product_kernel, out_shape=jax.ShapeDtypeStruct((freqs, row...]
  transfers between devices with their start and end apart: 3 -> 3, of which waited for: 1 -> 1; matrix products, arithmetic and copies ran while one was open for 1% -> 1% of each run, Pallas kernels for 2% -> 0%
where the time goes in v9:
time: 103 us
  blocking collectives  40.6 us (39%)
  waiting for transfers between devices  31.4 us (30%)
  starting transfers between devices  19 us (18%)
  Pallas kernels  10.5 us (10%)
    all_to_all x1, waiting for transfers between devices, shards(): lax.all_to_all(select(block, gmap, row_count), ROW + COL, split_axis=0, c...  31.4 us
    all_to_all x1, blocking collectives, shards(): lax.all_to_all(partial.reshape(col_count, 8, COLS), COL, split_axis=0, co...  29.3 us
    all_to_all x1, starting transfers between devices, shards(): lax.all_to_all(select(block, gmap, row_count), ROW + COL, split_axis=0, c...  12.5 us
    all_gather x1, blocking collectives, shards(): by_z = lax.all_gather(mine[:, :, half:], 'z_lo')  6.67 us
    all_gather x1, blocking collectives, shards(): by_core = lax.all_gather(by_z[0], 'core')  4.62 us
    ppermute x1, starting transfers between devices, shards(): lax.ppermute(mine[sources:, :, :half], 'y', [(i, (i + 1) % count) for i i...  4.15 us
    pallas_call x1, Pallas kernels, select(): pl.pallas_call(select_kernel, out_shape=jax.ShapeDtypeStruct((2 * rows *...  3.83 us
    pallas_call x1, Pallas kernels, transform(): pl.pallas_call(transform_kernel, out_shape=jax.ShapeDtypeStruct((4 * pair...  3.62 us
  transfers between devices with their start and end apart: 3, of which 1 were waited for; matrix products, arithmetic and copies ran while one was open for 1% of the time, Pallas kernels for 0%

profile of v9, /device:TPU:1, one launch (start us, length us, event | category | flops | bytes accessed | tf_op | source)
XLA Modules:
  0.0 102.8 jit_solution(4385390744619942518)
XLA Ops:
  0.0 3.6 %transform.1 = bf16[256,512]{1,0:T(8,128)(2,1)} custom-call(bf16[48,2,4096]{2,1,0:T(2,128)(2,1)} %val_hbm.1, bf16[64,2,4096]{2,1,0:T(2,128)(2,1)} %cond_hbm.1, s32[1024]{0:T(1024)} %vi_hbm.1, s32[1024]{0:T(1024)} %ci_hbm.1, f32[2,128,128]{2,1,0:T(8,128)} %constant.18.yq_hbm, bf16[144,256]{1,0:T(8,128)(2,1)} %constant.13.clone.zt_hbm), custom_call_target="tpu_custom_call" | custom-call | tf_op jit(solution)/shard_map/transform/pallas_call | solution.py:173
  3.6 0.0 copy-start.7
  3.6 0.0 copy-start.3
  3.7 0.0 copy-start.5
  3.7 0.0 copy-start.4
  3.7 0.0 copy-start.6
  3.7 29.3 %all_to_all.10 = bf16[32,8,512]{2,1,0:T(8,128)(2,1)S(1)} all-to-all(bf16[32,8,512]{2,1,0:T(8,128)(2,1)} %bitcast.9), channel_id=1, replica_groups=mesh['x'=4,'z_lo'=2,'core'=2,'z_hi'=4,'y'=8] {'z_hi','y'}, dimensions={0} | all-to-all | bytes 524288 | tf_op jit(solution)/shard_map/all_to_all | solution.py:311
  33.0 3.8 %select.1 = bf16[512,2,512]{2,1,0:T(2,128)(2,1)} custom-call(bf16[256,512]{1,0:T(8,128)(2,1)S(1)} %bitcast.7, bf16[160,256]{1,0:T(8,128)(2,1)S(1)} %copy-done.1, s32[512,1]{1,0:T(8,128)S(1)} %copy-done, s32[16,1,768]{2,1,0:T(1,128)S(1)} %bitcast.8), custom_call_target="tpu_custom_call" | custom-call | tf_op jit(solution)/shard_map/select/pallas_call | solution.py:230
  36.8 12.5 %all-to-all-start.1 = ((bf16[512,2,512]{2,1,0:T(2,128)(2,1)}), bf16[512,2,512]{2,1,0:T(2,128)(2,1)S(1)}, u32[]{:S(2)}, u32[]{:S(2)}) async-start(bf16[512,2,512]{2,1,0:T(2,128)(2,1)} %select.1), calls=%async_computation.1 | async-start | bytes 2097152 | tf_op jit(solution)/shard_map/all_to_all | solution.py:314
  49.3 0.0 copy-done.7
  49.4 0.1 select_reduce_fusion.1
  49.5 0.1 select_reduce_fusion
  49.6 0.1 add_divide_fusion.weight_ref
  49.7 31.4 %all-to-all-done.1.mine_ref = bf16[512,2,512]{2,1,0:T(2,128)(2,1)S(1)} async-done(((bf16[512,2,512]{2,1,0:T(2,128)(2,1)}), bf16[512,2,512]{2,1,0:T(2,128)(2,1)S(1)}, u32[]{:S(2)}, u32[]{:S(2)}) %all-to-all-start.1) | async-done | bytes 1048608 | tf_op jit(solution)/shard_map/all_to_all | solution.py:314
  81.1 0.5 fusion
  81.6 4.1 %collective-permute-start.1 = (bf16[256,2,384]{2,1,0:T(2,128)(2,1)S(1)}, bf16[256,2,384]{2,1,0:T(2,128)(2,1)S(1)}, u32[]{:S(2)}, u32[]{:S(2)}) collective-permute-start(bf16[256,2,384]{2,1,0:T(2,128)(2,1)S(1)} %get-tuple-element.9), channel_id=1, source_target_pairs={{0,1},{1,2},{2,3},{3,4},{4,5},{5,6},{6,7},{7,0},{8,9},{9,10},{10,1... | collective-permute-start | bytes 1179656 | tf_op jit(solution)/shard_map/ppermute | solution.py:324
  85.8 2.3 %collective-permute-start = (bf16[256,2,384]{2,1,0:T(2,128)(2,1)S(1)}, bf16[256,2,384]{2,1,0:T(2,128)(2,1)S(1)}, u32[]{:S(2)}, u32[]{:S(2)}) collective-permute-start(bf16[256,2,384]{2,1,0:T(2,128)(2,1)S(1)} %get-tuple-element.10), channel_id=1, source_target_pairs={{1,0},{2,1},{3,2},{4,3},{5,4},{6,5},{7,6},{0,7},{9,8},{10,9},{11,1... | collective-permute-start | bytes 1179656 | tf_op jit(solution)/shard_map/ppermute | solution.py:323
  88.1 0.2 slice.14
  88.3 6.7 %all-gather = bf16[1024,2,128]{2,1,0:T(2,128)(2,1)S(1)} all-gather(bf16[512,2,128]{2,1,0:T(2,128)(2,1)S(1)} %slice.14), channel_id=2, replica_groups=mesh['x'=4,'z_lo'=2,'core'=2,'z_hi'=4,'y'=8] {'z_lo'}, dimensions={0}, use_global_device_ids=true | all-gather | bytes 786432 | tf_op jit(solution)/shard_map/all_gather | solution.py:325
  95.0 0.2 slice.17
  95.2 4.6 %all-gather.1 = bf16[1024,2,128]{2,1,0:T(2,128)(2,1)S(1)} all-gather(bf16[512,2,128]{2,1,0:T(2,128)(2,1)S(1)} %slice.17), channel_id=3, replica_groups=mesh['x'=4,'z_lo'=2,'core'=2,'z_hi'=4,'y'=8] {'core'}, dimensions={0}, use_global_device_ids=true | all-gather | bytes 786432 | tf_op jit(solution)/shard_map/all_gather | solution.py:326
  99.8 0.0 collective-permute-done.1.high_ref
  99.8 0.0 collective-permute-done.low_ref
  99.8 3.1 %product.1 = f32[2,768,384]{2,1,0:T(8,128)} custom-call(bf16[512,2,512]{2,1,0:T(2,128)(2,1)S(1)} %all-to-all-done.1.mine_ref, bf16[256,2,384]{2,1,0:T(2,128)(2,1)S(1)} %collective-permute-done.low_ref, bf16[256,2,384]{2,1,0:T(2,128)(2,1)S(1)} %collective-permute-done.1.high_ref, bf16[2,512,2,128]{3,2,1,0:T(2,128)(2,1)S(1)} %bitcast.5, ...), custom_call_target="tpu_custom_call" | custom-call | tf_op jit(solution)/shard_map/product/pallas_call | solution.py:276
  (12 shorter events, 0.0 us)
Async XLA Ops:
  0.0 33.0 %copy-start = (s32[512,1]{1,0:T(8,128)S(1)}, s32[512,1]{1,0:T(8,128)}, u32[]{:S(2)}) copy-start(s32[512,1]{1,0:T(8,128)} %constant.15.clone.key_ref) | copy-start | bytes 6148
  0.0 33.0 %copy-start.1 = (bf16[160,256]{1,0:T(8,128)(2,1)S(1)}, bf16[160,256]{1,0:T(8,128)(2,1)}, u32[]{:S(2)}) copy-start(bf16[160,256]{1,0:T(8,128)(2,1)} %constant.14.clone.xt_ref) | copy-start | bytes 245764
  0.0 33.0 %copy-start.2 = (s32[12288]{0:T(1024)S(1)}, s32[12288]{0:T(1024)}, u32[]{:S(2)}) copy-start(s32[12288]{0:T(1024)} %param.19) | copy-start | bytes 147460
  3.6 45.7 %copy-start.7 = (f32[2]{0:T(128)S(1)}, f32[2]{0:T(128)}, u32[]{:S(2)}) copy-start(f32[2]{0:T(128)} %param.18) | copy-start | bytes 28
  3.6 45.7 %copy-start.3 = (s32[1024]{0:T(1024)S(1)}, s32[1024]{0:T(1024)}, u32[]{:S(2)}) copy-start(s32[1024]{0:T(1024)} %vi_hbm.1) | copy-start | bytes 12292
  3.7 45.7 %copy-start.5 = (f32[48]{0:T(128)S(1)}, f32[48]{0:T(128)}, u32[]{:S(2)}) copy-start(f32[48]{0:T(128)} %param.16) | copy-start | bytes 580
  3.7 45.8 %copy-start.4 = (s32[1024]{0:T(1024)S(1)}, s32[1024]{0:T(1024)}, u32[]{:S(2)}) copy-start(s32[1024]{0:T(1024)} %ci_hbm.1) | copy-start | bytes 12292
  3.7 45.8 %copy-start.6 = (f32[64]{0:T(128)S(1)}, f32[64]{0:T(128)}, u32[]{:S(2)}) copy-start(f32[64]{0:T(128)} %param.17) | copy-start | bytes 772
  36.8 44.2 %all-to-all-start.1 = ((bf16[512,2,512]{2,1,0:T(2,128)(2,1)}), bf16[512,2,512]{2,1,0:T(2,128)(2,1)S(1)}, u32[]{:S(2)}, u32[]{:S(2)}) async-start(bf16[512,2,512]{2,1,0:T(2,128)(2,1)} %select.1), calls=%async_computation.1 | async-start | bytes 2097152 | tf_op jit(solution)/shard_map/all_to_all | solution.py:314
  81.6 18.2 %collective-permute-start.1 = (bf16[256,2,384]{2,1,0:T(2,128)(2,1)S(1)}, bf16[256,2,384]{2,1,0:T(2,128)(2,1)S(1)}, u32[]{:S(2)}, u32[]{:S(2)}) collective-permute-start(bf16[256,2,384]{2,1,0:T(2,128)(2,1)S(1)} %get-tuple-element.9), channel_id=1, source_target_pairs={{0,1},{1,2},{2,3},{3,4},{4,5},{5,6},{6,7},{7,0},{8,9},{9,10},{10,1... | collective-permute-start | bytes 1179656 | tf_op jit(solution)/shard_map/ppermute | solution.py:324
  85.8 14.0 %collective-permute-start = (bf16[256,2,384]{2,1,0:T(2,128)(2,1)S(1)}, bf16[256,2,384]{2,1,0:T(2,128)(2,1)S(1)}, u32[]{:S(2)}, u32[]{:S(2)}) collective-permute-start(bf16[256,2,384]{2,1,0:T(2,128)(2,1)S(1)} %get-tuple-element.10), channel_id=1, source_target_pairs={{1,0},{2,1},{3,2},{4,3},{5,4},{6,5},{7,6},{0,7},{9,8},{10,9},{11,1... | collective-permute-start | bytes 1179656 | tf_op jit(solution)/shard_map/ppermute | solution.py:323

commit v10 on v9

--- a/solution.py
+++ b/solution.py
@@ -311,11 +311,11 @@
     block = lax.all_to_all(
         partial.reshape(col_count, 8, COLS), COL, split_axis=0, concat_axis=0, tiled=True
     ).reshape(4 * GRID, COLS)
+    weights = pair_weights(val_index, cond_index, val_energy, cond_energy, freqs)
+    block, weights = lax.optimization_barrier((block, weights))
     mine = lax.all_to_all(
         select(block, gmap, row_count), ROW + COL, split_axis=0, concat_axis=0, tiled=True
     )
-    weights = pair_weights(val_index, cond_index, val_energy, cond_energy, freqs)
-    mine, weights = lax.optimization_barrier((mine, weights))
     sources = mine.shape[0] // 2
     rows, width = NG // row_count, NG // col_count
     half = rows // 2

time: 103 us -> 102 us (level)
  waiting for transfers between devices: 31.4 us -> 12.3 us
  blocking collectives: 40.6 us -> 55.3 us
  starting transfers between devices: 19 us -> 23 us
    all_to_all x1, waiting for transfers between devices: 31.4 us -> 12.3 us  [shards(): lax.all_to_all(partial.reshape(col_count, 8, COLS), COL, split_axis=0, co...]
    all_to_all x1, blocking collectives: 29.3 us -> 44 us  [shards(): lax.all_to_all(select(block, gmap, row_count), ROW + COL, split_axis=0, c...]
    all_to_all x1, starting transfers between devices: 12.5 us -> 16.5 us  [shards(): lax.all_to_all(partial.reshape(col_count, 8, COLS), COL, split_axis=0, co...]
where the time goes in v10:
time: 102 us
  blocking collectives  55.3 us (54%)
  starting transfers between devices  23 us (23%)
  waiting for transfers between devices  12.3 us (12%)
  Pallas kernels  9.57 us (9%)
    all_to_all x1, blocking collectives, shards(): lax.all_to_all(select(block, gmap, row_count), ROW + COL, split_axis=0, c...  44 us
    all_to_all x1, starting transfers between devices, shards(): lax.all_to_all(partial.reshape(col_count, 8, COLS), COL, split_axis=0, co...  16.5 us
    all_to_all x1, waiting for transfers between devices, shards(): lax.all_to_all(partial.reshape(col_count, 8, COLS), COL, split_axis=0, co...  12.3 us
    all_gather x1, blocking collectives, shards(): by_z = lax.all_gather(mine[:, :, half:], 'z_lo')  6.66 us
    all_gather x1, blocking collectives, shards(): by_core = lax.all_gather(by_z[0], 'core')  4.63 us
    ppermute x1, starting transfers between devices, shards(): lax.ppermute(mine[sources:, :, :half], 'y', [(i, (i + 1) % count) for i i...  4.15 us
    pallas_call x1, Pallas kernels, transform(): pl.pallas_call(transform_kernel, out_shape=jax.ShapeDtypeStruct((4 * pair...  3.68 us
    pallas_call x1, Pallas kernels, product(): pl.pallas_call(product_kernel, out_shape=jax.ShapeDtypeStruct((freqs, row...  3.05 us
  transfers between devices with their start and end apart: 3, of which 1 were waited for; matrix products, arithmetic and copies ran while one was open for 1% of the time, Pallas kernels for 0%

profile of v10, /device:TPU:1, one launch (start us, length us, event | category | flops | bytes accessed | tf_op | source)
XLA Modules:
  0.0 101.6 jit_solution(16924563900506795878)
XLA Ops:
  0.0 0.0 copy-start.4
  0.0 0.0 copy-start.7
  0.0 0.0 copy-start.5
  0.0 0.0 copy-start.6
  0.0 0.0 copy-start.2
  0.1 3.7 %transform.1 = bf16[256,512]{1,0:T(8,128)(2,1)} custom-call(bf16[48,2,4096]{2,1,0:T(2,128)(2,1)} %val_hbm.1, bf16[64,2,4096]{2,1,0:T(2,128)(2,1)} %cond_hbm.1, s32[1024]{0:T(1024)} %vi_hbm.1, s32[1024]{0:T(1024)} %ci_hbm.1, f32[2,128,128]{2,1,0:T(8,128)} %constant.18.yq_hbm, bf16[144,256]{1,0:T(8,128)(2,1)} %constant.13.clone.zt_hbm), custom_call_target="tpu_custom_call" | custom-call | tf_op jit(solution)/shard_map/transform/pallas_call | solution.py:173
  3.7 16.5 %all-to-all-start = ((bf16[32,8,512]{2,1,0:T(8,128)(2,1)}), bf16[32,8,512]{2,1,0:T(8,128)(2,1)S(1)}, u32[]{:S(2)}, u32[]{:S(2)}) async-start(bf16[32,8,512]{2,1,0:T(8,128)(2,1)} %bitcast.9), calls=%async_computation | async-start | bytes 524288 | tf_op jit(solution)/shard_map/all_to_all | solution.py:311
  20.3 0.0 copy-done.7
  20.3 0.1 select_reduce_fusion
  20.4 0.1 select_reduce_fusion.1
  20.6 0.1 add_divide_fusion.weight_ref
  20.6 12.3 %all-to-all-done = bf16[32,8,512]{2,1,0:T(8,128)(2,1)S(1)} async-done(((bf16[32,8,512]{2,1,0:T(8,128)(2,1)}), bf16[32,8,512]{2,1,0:T(8,128)(2,1)S(1)}, u32[]{:S(2)}, u32[]{:S(2)}) %all-to-all-start) | async-done | bytes 262176 | tf_op jit(solution)/shard_map/all_to_all | solution.py:311
  32.9 2.8 %select.1 = bf16[512,2,512]{2,1,0:T(2,128)(2,1)S(1)} custom-call(bf16[256,512]{1,0:T(8,128)(2,1)S(1)} %bitcast.7, bf16[160,256]{1,0:T(8,128)(2,1)S(1)} %copy-done.1, s32[512,1]{1,0:T(8,128)S(1)} %copy-done, s32[16,1,768]{2,1,0:T(1,128)S(1)} %bitcast.8), custom_call_target="tpu_custom_call" | custom-call | tf_op jit(solution)/shard_map/select/pallas_call | solution.py:230
  35.8 44.0 %all_to_all.10.mine_ref = bf16[512,2,512]{2,1,0:T(2,128)(2,1)S(1)} all-to-all(bf16[512,2,512]{2,1,0:T(2,128)(2,1)S(1)} %select.1), channel_id=1, replica_groups=mesh['x'=4,'z_lo'=2,'core'=2,'z_hi'=4,'y'=8] {'x','z_lo','core','z_hi','y'}, dimensions={0} | all-to-all | bytes 2097152 | tf_op jit(solution)/shard_map/all_to_all | solution.py:316
  79.8 0.5 fusion
  80.4 4.1 %collective-permute-start.1 = (bf16[256,2,384]{2,1,0:T(2,128)(2,1)S(1)}, bf16[256,2,384]{2,1,0:T(2,128)(2,1)S(1)}, u32[]{:S(2)}, u32[]{:S(2)}) collective-permute-start(bf16[256,2,384]{2,1,0:T(2,128)(2,1)S(1)} %get-tuple-element.9), channel_id=1, source_target_pairs={{0,1},{1,2},{2,3},{3,4},{4,5},{5,6},{6,7},{7,0},{8,9},{9,10},{10,1... | collective-permute-start | bytes 1179656 | tf_op jit(solution)/shard_map/ppermute | solution.py:324
  84.5 2.3 %collective-permute-start = (bf16[256,2,384]{2,1,0:T(2,128)(2,1)S(1)}, bf16[256,2,384]{2,1,0:T(2,128)(2,1)S(1)}, u32[]{:S(2)}, u32[]{:S(2)}) collective-permute-start(bf16[256,2,384]{2,1,0:T(2,128)(2,1)S(1)} %get-tuple-element.10), channel_id=1, source_target_pairs={{1,0},{2,1},{3,2},{4,3},{5,4},{6,5},{7,6},{0,7},{9,8},{10,9},{11,1... | collective-permute-start | bytes 1179656 | tf_op jit(solution)/shard_map/ppermute | solution.py:323
  86.9 0.2 slice.19
  87.1 6.7 %all-gather = bf16[1024,2,128]{2,1,0:T(2,128)(2,1)S(1)} all-gather(bf16[512,2,128]{2,1,0:T(2,128)(2,1)S(1)} %slice.19), channel_id=2, replica_groups=mesh['x'=4,'z_lo'=2,'core'=2,'z_hi'=4,'y'=8] {'z_lo'}, dimensions={0}, use_global_device_ids=true | all-gather | bytes 786432 | tf_op jit(solution)/shard_map/all_gather | solution.py:325
  93.7 0.2 slice.20
  93.9 4.6 %all-gather.1 = bf16[1024,2,128]{2,1,0:T(2,128)(2,1)S(1)} all-gather(bf16[512,2,128]{2,1,0:T(2,128)(2,1)S(1)} %slice.20), channel_id=3, replica_groups=mesh['x'=4,'z_lo'=2,'core'=2,'z_hi'=4,'y'=8] {'core'}, dimensions={0}, use_global_device_ids=true | all-gather | bytes 786432 | tf_op jit(solution)/shard_map/all_gather | solution.py:326
  98.5 0.0 collective-permute-done.1.high_ref
  98.5 0.0 collective-permute-done.low_ref
  98.5 3.1 %product.1 = f32[2,768,384]{2,1,0:T(8,128)} custom-call(bf16[512,2,512]{2,1,0:T(2,128)(2,1)S(1)} %all_to_all.10.mine_ref, bf16[256,2,384]{2,1,0:T(2,128)(2,1)S(1)} %collective-permute-done.low_ref, bf16[256,2,384]{2,1,0:T(2,128)(2,1)S(1)} %collective-permute-done.1.high_ref, bf16[2,512,2,128]{3,2,1,0:T(2,128)(2,1)S(1)} %bitcast.5, ...), custom_call_target="tpu_custom_call" | custom-call | tf_op jit(solution)/shard_map/product/pallas_call | solution.py:276
  (12 shorter events, 0.0 us)
Async XLA Ops:
  0.0 32.9 %copy-start = (s32[512,1]{1,0:T(8,128)S(1)}, s32[512,1]{1,0:T(8,128)}, u32[]{:S(2)}) copy-start(s32[512,1]{1,0:T(8,128)} %constant.15.clone.key_ref) | copy-start | bytes 6148
  0.0 32.9 %copy-start.1 = (bf16[160,256]{1,0:T(8,128)(2,1)S(1)}, bf16[160,256]{1,0:T(8,128)(2,1)}, u32[]{:S(2)}) copy-start(bf16[160,256]{1,0:T(8,128)(2,1)} %constant.14.clone.xt_ref) | copy-start | bytes 245764
  0.0 20.3 %copy-start.3 = (s32[1024]{0:T(1024)S(1)}, s32[1024]{0:T(1024)}, u32[]{:S(2)}) copy-start(s32[1024]{0:T(1024)} %ci_hbm.1) | copy-start | bytes 12292
  0.0 20.4 %copy-start.4 = (s32[1024]{0:T(1024)S(1)}, s32[1024]{0:T(1024)}, u32[]{:S(2)}) copy-start(s32[1024]{0:T(1024)} %vi_hbm.1) | copy-start | bytes 12292
  0.0 20.3 %copy-start.7 = (f32[2]{0:T(128)S(1)}, f32[2]{0:T(128)}, u32[]{:S(2)}) copy-start(f32[2]{0:T(128)} %param.18) | copy-start | bytes 28
  0.0 20.3 %copy-start.5 = (f32[64]{0:T(128)S(1)}, f32[64]{0:T(128)}, u32[]{:S(2)}) copy-start(f32[64]{0:T(128)} %param.17) | copy-start | bytes 772
  0.0 20.4 %copy-start.6 = (f32[48]{0:T(128)S(1)}, f32[48]{0:T(128)}, u32[]{:S(2)}) copy-start(f32[48]{0:T(128)} %param.16) | copy-start | bytes 580
  0.0 32.9 %copy-start.2 = (s32[12288]{0:T(1024)S(1)}, s32[12288]{0:T(1024)}, u32[]{:S(2)}) copy-start(s32[12288]{0:T(1024)} %param.19) | copy-start | bytes 147460
  3.7 29.2 %all-to-all-start = ((bf16[32,8,512]{2,1,0:T(8,128)(2,1)}), bf16[32,8,512]{2,1,0:T(8,128)(2,1)S(1)}, u32[]{:S(2)}, u32[]{:S(2)}) async-start(bf16[32,8,512]{2,1,0:T(8,128)(2,1)} %bitcast.9), calls=%async_computation | async-start | bytes 524288 | tf_op jit(solution)/shard_map/all_to_all | solution.py:311
  80.4 18.2 %collective-permute-start.1 = (bf16[256,2,384]{2,1,0:T(2,128)(2,1)S(1)}, bf16[256,2,384]{2,1,0:T(2,128)(2,1)S(1)}, u32[]{:S(2)}, u32[]{:S(2)}) collective-permute-start(bf16[256,2,384]{2,1,0:T(2,128)(2,1)S(1)} %get-tuple-element.9), channel_id=1, source_target_pairs={{0,1},{1,2},{2,3},{3,4},{4,5},{5,6},{6,7},{7,0},{8,9},{9,10},{10,1... | collective-permute-start | bytes 1179656 | tf_op jit(solution)/shard_map/ppermute | solution.py:324
  84.5 14.0 %collective-permute-start = (bf16[256,2,384]{2,1,0:T(2,128)(2,1)S(1)}, bf16[256,2,384]{2,1,0:T(2,128)(2,1)S(1)}, u32[]{:S(2)}, u32[]{:S(2)}) collective-permute-start(bf16[256,2,384]{2,1,0:T(2,128)(2,1)S(1)} %get-tuple-element.10), channel_id=1, source_target_pairs={{1,0},{2,1},{3,2},{4,3},{5,4},{6,5},{7,6},{0,7},{9,8},{10,9},{11,1... | collective-permute-start | bytes 1179656 | tf_op jit(solution)/shard_map/ppermute | solution.py:323
